TPU v7x, 128 devices: a whole 4x4x4 slice. The times are simulated.
128 devices in a mesh: pole: 8 (over x, z_lo), col: 16 (over z_hi, y, core).
Axes of the slice: x: 4, y: 4, z: 4 (z_hi: 2, z_lo: 2; z = z_hi * 2 + z_lo), core: 2. Of those that a mesh axis runs over, the one named last changes fastest.
Arguments:
- panel: bfloat16 [256, 3072, 128], P('col', 'pole'), may hold values from -36 to 36
- pivot_inverse: bfloat16 [8, 256, 128, 128], P('pole', 'col'), may hold values from -0.5 to 0.5
- row_count: int32 [256], replicated, may hold values from 1 to 24, 3072 in all
- pole_weight: float32 [8], replicated, may hold values from 0.25 to 2
Outputs:
- density_panel: bfloat16 [256, 3072, 128], P('col', 'pole')
- density_diag: bfloat16 [256, 128, 128], P('col', 'pole')
All inputs are finite; a program needn't handle non-finite values.
Results may differ from a plain program's by a relative error of at most 0.017.
Values may be sent and summed in bfloat16 or wider, within the bound.
No kernel may reach another device: no remote copies, remote signals or barrier semaphores. Data moves between devices by JAX's collectives and lax.ppermute only.
A program may use at most 128 MiB of HBM per device.

v0:
```python
import jax
import jax.numpy as jnp
from jax import lax
from jax.sharding import PartitionSpec as P


def shards(panel, pivot_inverse, row_count, pole_weight):
    owned = panel.shape[0]
    block_size = panel.shape[2]
    rows_local = panel.shape[1] // block_size
    pole_count = lax.axis_size("pole")
    col_count = lax.axis_size("col")
    group_size = owned // col_count
    whole_rows = rows_local * pole_count
    pole_at = lax.axis_index("pole")
    col_at = lax.axis_index("col")
    counts = lax.dynamic_slice_in_dim(row_count, col_at * owned, owned, 0)
    row_total = (block_size * counts).astype(jnp.float32)
    stacked = lax.all_gather(
        panel.reshape(owned, rows_local, 1, block_size, block_size), "pole", axis=2, tiled=True
    )
    moved = lax.all_to_all(
        stacked.reshape(col_count, group_size, 1, whole_rows * block_size, block_size),
        "col",
        split_axis=0,
        concat_axis=2,
        tiled=True,
    )
    gathered = moved.reshape(owned, whole_rows, block_size, block_size)
    row_index = jnp.arange(whole_rows, dtype=jnp.int32)
    keep = (row_index[None, :] < counts[:, None]).astype(jnp.bfloat16)
    natural = (gathered * keep[:, :, None, None]).reshape(
        owned, whole_rows * block_size, block_size
    )
    inverse = pivot_inverse[0]
    weight = pole_weight[pole_at]
    product = jnp.einsum("srk,skj->srj", natural, inverse, preferred_element_type=jnp.float32)
    frontal = lax.optimization_barrier(product.astype(jnp.bfloat16))
    gram = jnp.einsum("srk,srj->skj", frontal, frontal, preferred_element_type=jnp.float32)
    panel_term = (-weight * frontal.astype(jnp.float32)).astype(jnp.bfloat16)
    diag_term = weight * (inverse.astype(jnp.float32) + gram / row_total[:, None, None])
    panel_sum = lax.psum_scatter(
        panel_term.reshape(owned, rows_local, pole_count, block_size, block_size),
        "pole",
        scatter_dimension=2,
        tiled=True,
    ).astype(jnp.float32)
    diag_sum = lax.psum_scatter(
        diag_term.astype(jnp.bfloat16), "pole", scatter_dimension=1, tiled=True
    )
    density_panel = panel_sum.reshape(owned, rows_local * block_size, block_size).astype(
        jnp.bfloat16
    )
    return (density_panel, diag_sum)


def solution(mesh):
    placed = (P("col", "pole", None), P("pole", "col", None, None), P(), P())
    return jax.shard_map(
        shards,
        mesh=mesh,
        in_specs=placed,
        out_specs=(P("col", "pole", None), P("col", "pole", None)),
        check_vma=False,
    )
```

profile of v0, /device:TPU:0, one launch (start us, length us, event | category | flops | bytes accessed | tf_op | source)
XLA Modules:
  0.0 1012.6 jit_solution(7860197841460956118)
XLA Ops:
  7.2 0.0 all-gather.2.cloned.1.call-start
  7.2 0.7 all-gather.2.cloned.1.call-update
  7.9 251.3 %all-gather.2.cloned.1.call-done = bf16[16,3,8,128,128]{4,3,1,0,2:T(8,128)(2,1)} async-done(((bf16[16,3,1,128,128]{4,3,1,0,2:T(8,128)(2,1)}), bf16[16,3,8,128,128]{4,3,1,0,2:T(8,128)(2,1)}) %all-gather.2.cloned.1.call-update) | async-done | bytes 12582928 | tf_op jit(solution)/shard_map/all_gather | solution.py:19
  259.2 11.9 %copy.9 = bf16[16,3,8,128,128]{4,3,2,1,0:T(8,128)(2,1)} copy(bf16[16,3,8,128,128]{4,3,1,0,2:T(8,128)(2,1)} %all-gather.2.cloned.1.call-done) | data formatting | bytes 25165824 | tf_op jit(solution)/shard_map/all_gather | solution.py:19
  271.1 0.0 copy-start.1
  271.1 0.0 copy-start.3
  271.1 0.0 copy-start.2
  271.1 6.9 all-to-all-start
  278.0 0.0 all-reduce.3.cloned.1.call-start
  278.0 0.0 copy-done.1
  278.0 0.1 multiply_convert_fusion.2
  278.1 0.1 fusion.4
  278.2 0.1 mul.33
  278.3 0.0 copy-done.3
  278.4 0.6 dynamic_slice.6
  279.6 167.4 %all-to-all-done = bf16[16,1,1,3072,128]{4,3,2,1,0:T(8,128)(2,1)} async-done(((bf16[16,1,1,3072,128]{4,3,2,1,0:T(8,128)(2,1)}), bf16[16,1,1,3072,128]{4,3,2,1,0:T(8,128)(2,1)}, u32[]{:S(2)}, u32[]{:S(2)}) %all-to-all-start) | async-done | bytes 12582944 | tf_op jit(solution)/shard_map/all_to_all | solution.py:22
  447.0 0.0 copy-done.2
  447.0 11.0 %fusion.1 = bf16[16,3072,128]{2,1,0:T(8,128)(2,1)S(1)} fusion(bf16[16,1,1,3072,128]{4,3,2,1,0:T(8,128)(2,1)} %all-to-all-done, bf16[16,3072]{1,0:T(8,128)(2,1)S(1)} %bitcast.34, bf16[1,16,128,128]{3,2,1,0:T(8,128)(2,1)S(1)} %copy-done.2), kind=kOutput, calls=%fused_computation.3 | convolution fusion | flops 1623195648 | bytes 25788416 | tf_op jit(solution)/shard_map/srk,skj->srj/dot_general | solution.py:37
  457.9 0.0 copy-start
  458.0 7.9 multiply_convert_fusion
  465.9 0.5 copy-done
  466.4 0.0 all-reduce.3.cloned.1.call-update
  466.4 0.0 reduce-scatter.5.cloned.1.call-start
  466.5 0.0 copy-start.4
  466.5 11.8 %multiply_convert_fusion.1 = bf16[16,128,128]{2,1,0:T(8,128)(2,1)} fusion(bf16[16,3072,128]{2,1,0:T(8,128)(2,1)} %copy-done, bf16[1,16,128,128]{3,2,1,0:T(8,128)(2,1)S(1)} %copy-done.2, f32[16]{0:T(128)S(1)} %get-tuple-element.2, f32[]{:T(128)} %bitcast), kind=kOutput, calls=%fused_computation.5 | convolution fusion | flops 1611923456 | bytes 13631556 | tf_op jit(solution)/shard_map/srk,srj->skj/dot_general | solution.py:39
  478.3 0.0 reduce-scatter.5.cloned.1.call-update
  478.3 0.0 copy-done.4
  478.4 0.7 dynamic-slice
  479.0 485.5 %all-reduce.3.cloned.1.call-done = bf16[16,3,8,128,128]{4,3,2,1,0:T(8,128)(2,1)} async-done(((bf16[16,3,8,128,128]{4,3,2,1,0:T(8,128)(2,1)}), bf16[16,3,8,128,128]{4,3,2,1,0:T(8,128)(2,1)}) %all-reduce.3.cloned.1.call-update) | async-done | bytes 12582928
  964.5 3.4 constant_dynamic-slice_fusion
  968.0 38.1 %reduce-scatter.5.cloned.1.call-done = bf16[16,16,128]{2,1,0:T(8,128)(2,1)} async-done(((bf16[16,128,128]{2,1,0:T(8,128)(2,1)}), bf16[16,16,128]{2,1,0:T(8,128)(2,1)}) %reduce-scatter.5.cloned.1.call-update) | async-done | bytes 65552 | tf_op jit(solution)/shard_map/reduce_scatter | solution.py:48
  (1 shorter events, 0.0 us)
Async XLA Ops:
  7.2 252.0 %all-gather.2.cloned.1.call-start = ((), (), s32[]{:S(2)}) async-start(), calls=%async_computation.2 | async-start | bytes 14155776 | tf_op jit(solution)/shard_map/all_gather | solution.py:19
  271.1 7.0 copy-start.1
  271.1 7.3 copy-start.3
  271.1 175.9 %copy-start.2 = (bf16[1,16,128,128]{3,2,1,0:T(8,128)(2,1)S(1)}, bf16[1,16,128,128]{3,2,1,0:T(8,128)(2,1)}, u32[]{:S(2)}) copy-start(bf16[1,16,128,128]{3,2,1,0:T(8,128)(2,1)} %param.5) | copy-start | bytes 1572868
  271.1 175.9 %all-to-all-start = ((bf16[16,1,1,3072,128]{4,3,2,1,0:T(8,128)(2,1)}), bf16[16,1,1,3072,128]{4,3,2,1,0:T(8,128)(2,1)}, u32[]{:S(2)}, u32[]{:S(2)}) async-start(bf16[16,1,1,3072,128]{4,3,2,1,0:T(8,128)(2,1)} %bitcast.29), calls=%async_computation | async-start | bytes 25165824 | tf_op jit(solution)/shard_map/all_to_all | solution.py:22
  278.0 686.6 %all-reduce.3.cloned.1.call-start = ((), (), s32[]{:S(2)}) async-start(), calls=%async_computation.4 | async-start | bytes 25165824
  457.9 8.4 copy-start
  466.4 539.6 %reduce-scatter.5.cloned.1.call-start = ((), (), s32[]{:S(2)}) async-start(), calls=%async_computation.3 | async-start | bytes 589824 | tf_op jit(solution)/shard_map/reduce_scatter | solution.py:48
  466.5 11.9 %copy-start.4 = (u32[128]{0:T(128)S(1)}, u32[128]{0:T(128)}, u32[]{:S(2)}) copy-start(u32[128]{0:T(128)} %constant.22) | copy-start | bytes 1540
Sparse Core Ops, SparseCore 0:
  9.6 249.4 all-gather.1
  466.5 497.9 all-reduce.2
  967.5 38.5 reduce-scatter.4
where the time goes:
time: 1010 us
  waiting for transfers between devices  943 us (93%)
  matrix products  22.8 us (2%)
  local copies, waits for them, and re-layouts  17.2 us (2%)
  between operations  14.5 us (1%)
    unnamed x4, waiting for transfers between devices  486 us
    all_gather x1, waiting for transfers between devices, shards(): lax.all_gather(panel.reshape(owned, rows_local, 1, block_size, block_size...  251 us
    all_to_all x1, waiting for transfers between devices, shards(): lax.all_to_all(stacked.reshape(col_count, group_size, 1, whole_rows * blo...  167 us
    reduce_scatter x1, waiting for transfers between devices, shards(): lax.psum_scatter(diag_term.astype(jnp.bfloat16), 'pole', scatter_dimensio...  38.1 us
  transfers between devices with their start and end apart: 4, of which 4 were waited for; matrix products, arithmetic and copies ran while one was open for 2% of the time, Pallas kernels for 0%

commit v1 on v0

v1 whole, which is shorter than its diff:
```python
import jax
import jax.numpy as jnp
from jax import lax
from jax.sharding import PartitionSpec as P


def shards(panel, pivot_inverse, row_count, pole_weight):
    owned, rows, block = panel.shape
    rows_local = rows // block
    poles = lax.axis_size("pole")
    cols = lax.axis_size("col")
    pole_at = lax.axis_index("pole")
    col_at = lax.axis_index("col")
    share = owned // poles
    moved = lax.all_to_all(panel, "col", 0, 0, tiled=True)
    natural_row = jnp.arange(rows_local, dtype=jnp.int32) * poles + pole_at
    stored_counts = lax.dynamic_index_in_dim(row_count.reshape(owned, cols), col_at, 1, keepdims=False)
    keep = (natural_row[None, :] < stored_counts[:, None]).astype(jnp.bfloat16)
    masked = (panel.reshape(owned, rows_local, block, block) * keep[:, :, None, None]).reshape(owned, rows, block)
    part = jnp.einsum("sra,srb->sab", masked, masked, preferred_element_type=jnp.float32).astype(jnp.bfloat16)
    sent = jnp.stack([pivot_inverse[0], part], axis=1)
    got = lax.all_to_all(sent, "pole", 0, 0, tiled=True).reshape(poles, share, 2, block, block)
    inv = got[:, :, 0]
    gram = jnp.sum(got[:, :, 1].astype(jnp.float32), axis=0)
    w = pole_weight
    msum = jnp.einsum("p,psab->sab", w, inv.astype(jnp.float32), precision="highest")
    mneg = (-msum).astype(jnp.bfloat16)
    mall = lax.all_gather(mneg, "pole", axis=0, tiled=True)
    half = lax.rem(col_at, 2)
    a = lax.dynamic_index_in_dim(gram, half, 0, keepdims=False)
    b = lax.dynamic_index_in_dim(gram, 1 - half, 0, keepdims=False)
    n = poles * cols
    sw = lambda p, c, f: (c // 2) * cols + 2 * p + ((c % 2) ^ f)
    pa = [(p * cols + c, sw(p, c, 0)) for p in range(poles) for c in range(cols)]
    pb = [(p * cols + c, sw(p, c, 1)) for p in range(poles) for c in range(cols)]
    a = lax.ppermute(a, ("pole", "col"), pa)
    b = lax.ppermute(b, ("pole", "col"), pb)
    lo = jnp.where(half == 0, a, b)
    hi = jnp.where(half == 0, b, a)
    full = jnp.stack([lo, hi])
    mine = lax.dynamic_slice_in_dim(row_count, col_at * owned + pole_at * share, share, 0)
    scale = 1.0 / (block * mine).astype(jnp.float32)
    inv32 = inv.astype(jnp.float32)
    right = jnp.einsum("sab,psbc->psac", full, inv32, precision="highest")
    quad = jnp.einsum("psab,psac->sbc", inv32 * w[:, None, None, None], right, precision="highest")
    diag = (msum + quad * scale[:, None, None]).astype(jnp.bfloat16)
    diag = lax.all_to_all(diag, "pole", 1, 0, tiled=True)
    counts = lax.dynamic_slice_in_dim(row_count, col_at * owned, owned, 0)
    keep2 = (natural_row[None, :] < counts[:, None]).astype(jnp.bfloat16)
    masked2 = (moved.reshape(owned, rows_local, block, block) * keep2[:, :, None, None]).reshape(owned, rows, block)
    density = jnp.einsum("srk,skj->srj", masked2, mall, preferred_element_type=jnp.float32).astype(jnp.bfloat16)
    return density, diag


def solution(mesh):
    placed = (P("col", "pole", None), P("pole", "col", None, None), P(), P())
    return jax.shard_map(
        shards,
        mesh=mesh,
        in_specs=placed,
        out_specs=(P("col", "pole", None), P("col", "pole", None)),
        check_vma=False,
    )
```

time: 1010 us -> 111 us (0.11)
  waiting for transfers between devices: 943 us -> 16 us
  blocking collectives: 0 us -> 67.3 us
  matrix products: 22.8 us -> 8.82 us
  between operations: 14.5 us -> 0.84 us
  local copies, waits for them, and re-layouts: 17.2 us -> 4.19 us
    unnamed x4 -> x0, waiting for transfers between devices: 486 us -> none
    all_gather x1 -> x0, waiting for transfers between devices: 251 us -> none  [shards(): lax.all_gather(panel.reshape(owned, rows_local, 1, block_size, block_size...]
    all_to_all x1 -> x2, waiting for transfers between devices: 167 us -> 15.7 us  [the longest x1 15.7 us: shards(): lax.all_to_all(sent, 'pole', 0, 0, tiled=True)]
    all_gather x0 -> x1, blocking collectives: none -> 41.2 us  [shards(): mall = lax.all_gather(mneg, 'pole', axis=0, tiled=True)]
    reduce_scatter x1 -> x0, waiting for transfers between devices: 38.1 us -> none  [shards(): lax.psum_scatter(diag_term.astype(jnp.bfloat16), 'pole', scatter_dimensio...]
    all_to_all x0 -> x1, blocking collectives: none -> 26.2 us  [shards(): diag = lax.all_to_all(diag, 'pole', 1, 0, tiled=True)]
    dot_general x2 -> x5, matrix products: 22.8 us -> 8.82 us  [the longest x1 4.26 us: shards(): jnp.einsum('sra,srb->sab', masked, masked, preferred_element_type=jnp.flo...]
    all_gather x1 -> x0, local copies, waits for them, and re-layouts: 11.9 us -> none  [shards(): lax.all_gather(panel.reshape(owned, rows_local, 1, block_size, block_size...]
  transfers between devices with their start and end apart: 4 -> 4, of which waited for: 4 -> 2; matrix products, arithmetic and copies ran while one was open for 2% -> 2% of each run, Pallas kernels for 0% -> 0%
where the time goes in v1:
time: 111 us; the launch traced here: 109 us
  blocking collectives  67.3 us (61%)
  waiting for transfers between devices  16 us (14%)
  starting transfers between devices  11.6 us (10%)
  matrix products  8.82 us (8%)
  local copies, waits for them, and re-layouts  4.19 us (4%)
    all_gather x1, blocking collectives, shards(): mall = lax.all_gather(mneg, 'pole', axis=0, tiled=True)  41.2 us
    all_to_all x1, blocking collectives, shards(): diag = lax.all_to_all(diag, 'pole', 1, 0, tiled=True)  26.2 us
    all_to_all x1, waiting for transfers between devices, shards(): lax.all_to_all(sent, 'pole', 0, 0, tiled=True)  15.7 us
    all_to_all x1, starting transfers between devices, shards(): lax.all_to_all(sent, 'pole', 0, 0, tiled=True)  5.87 us
    all_to_all x1, starting transfers between devices, shards(): moved = lax.all_to_all(panel, 'col', 0, 0, tiled=True)  5.01 us
    dot_general x1, matrix products, shards(): jnp.einsum('sra,srb->sab', masked, masked, preferred_element_type=jnp.flo...  4.26 us
  transfers between devices with their start and end apart: 4, of which 2 were waited for; matrix products, arithmetic and copies ran while one was open for 2% of the time, Pallas kernels for 0%

profile of v1, /device:TPU:0, one launch (start us, length us, event | category | flops | bytes accessed | tf_op | source)
XLA Modules:
  0.0 109.1 jit_solution(11657720161349791457)
XLA Ops:
  0.6 0.8 reshape.83
  1.4 0.8 dynamic_slice.19
  2.2 0.2 dynamic-slice_reduce_fusion
  2.3 0.1 compare_convert_fusion.1
  2.4 0.1 mul.65
  2.5 0.0 copy-start
  2.5 4.3 %fusion.6 = bf16[16,1,128,128]{3,2,0,1:T(8,128)(2,1)S(1)} fusion(bf16[16,384,128]{2,1,0:T(8,128)(2,1)} %param.4, bf16[16,384]{1,0:T(8,128)(2,1)S(1)} %bitcast.68), kind=kOutput, calls=%fused_computation.6 | convolution fusion | flops 202375168 | bytes 2109440 | tf_op jit(solution)/shard_map/sra,srb->sab/dot_general | solution.py:20
  6.8 0.0 copy-done
  6.8 0.1 pad_maximum_fusion
  6.9 1.0 copy.22
  8.0 5.9 %all-to-all-start.1 = ((bf16[16,2,128,128]{3,2,1,0:T(8,128)(2,1)}), bf16[16,2,128,128]{3,2,1,0:T(8,128)(2,1)S(1)}, u32[]{:S(2)}, u32[]{:S(2)}) async-start(bf16[16,2,128,128]{3,2,1,0:T(8,128)(2,1)} %copy.22), calls=%async_computation.1 | async-start | bytes 2097152 | tf_op jit(solution)/shard_map/all_to_all | solution.py:22
  13.8 0.0 copy-done.2
  13.9 0.1 convert_divide_fusion
  13.9 15.7 %all-to-all-done.1 = bf16[16,2,128,128]{3,2,1,0:T(8,128)(2,1)S(1)} async-done(((bf16[16,2,128,128]{3,2,1,0:T(8,128)(2,1)}), bf16[16,2,128,128]{3,2,1,0:T(8,128)(2,1)S(1)}, u32[]{:S(2)}, u32[]{:S(2)}) %all-to-all-start.1) | async-done | bytes 1048608 | tf_op jit(solution)/shard_map/all_to_all | solution.py:22
  29.7 0.1 convert_reduce_fusion
  29.7 0.3 fusion.25
  30.0 0.7 collective-permute-start
  30.7 0.1 collective-permute-start.1
  30.8 0.7 fusion.16
  31.5 0.3 copy.34
  31.8 0.0 collective-permute-done
  31.8 0.2 collective-permute-done.1
  32.1 0.6 convolution_bitcast_fusion
  32.6 1.2 %fusion.11 = bf16[2,128,128]{2,1,0:T(8,128)(2,1)S(1)} fusion(f32[2,128,128]{2,1,0:T(8,128)S(1)} %bitcast.60, f32[8,2,128,128]{2,3,0,1:T(8,128)S(1)} %convolution_bitcast_fusion, bf16[8,2,1,128,128]{3,4,0,1,2:T(8,128)(2,1)S(1)} %copy.34, f32[8]{0:T(128)S(1)} %copy-done.1, f32[2]{0:T(128)S(1)} %convert_divide_fusion), kind=kOutput, calls=%fused_computation.10 | convolution fusion | flops 403275776 | bytes 1769512 | tf_op jit(solution)/shard_map/psab,psac->sbc/dot_general | solution.py:45
  33.9 0.1 copy.25
  33.9 26.2 %all_to_all.28 = bf16[2,128,128]{2,0,1:T(2,128)(2,1)S(1)} all-to-all(bf16[2,128,128]{2,0,1:T(2,128)(2,1)S(1)} %copy.25), channel_id=1, replica_groups=mesh['pole'=8,'col'=16] {'pole'}, dimensions={1} | all-to-all | bytes 131072 | tf_op jit(solution)/shard_map/all_to_all | solution.py:47
  60.1 5.0 %all-to-all-start = ((bf16[16,384,128]{2,1,0:T(8,128)(2,1)}), bf16[16,384,128]{2,1,0:T(8,128)(2,1)S(1)}, u32[]{:S(2)}, u32[]{:S(2)}) async-start(bf16[16,384,128]{2,1,0:T(8,128)(2,1)} %param.4), calls=%async_computation | async-start | bytes 3145728 | tf_op jit(solution)/shard_map/all_to_all | solution.py:15
  65.1 0.1 mul.61
  65.3 41.2 %all_gather.3 = bf16[16,128,128]{2,1,0:T(8,128)(2,1)S(1)} all-gather(bf16[2,128,128]{2,1,0:T(8,128)(2,1)S(1)} %negate_convert_fusion), channel_id=1, replica_groups=mesh['pole'=8,'col'=16] {'pole'}, dimensions={0}, use_global_device_ids=true | all-gather | bytes 589824 | tf_op jit(solution)/shard_map/all_gather | solution.py:28
  106.4 0.6 copy.26
  107.0 0.0 all-to-all-done
  107.1 2.1 %convolution_convert_fusion = bf16[16,384,128]{2,1,0:T(8,128)(2,1)} fusion(bf16[16,128,128]{2,1,0:T(8,128)(2,1)S(1)} %all_gather.3, bf16[16,384,128]{2,1,0:T(8,128)(2,1)S(1)} %all-to-all-done, bf16[16,384]{1,0:T(8,128)(2,1)S(1)} %bitcast.67), kind=kOutput, calls=%fused_computation | convolution fusion | flops 202899456 | bytes 3682304 | tf_op jit(solution)/shard_map/srk,skj->srj/dot_general | solution.py:51
  (9 shorter events, 0.1 us)
Async XLA Ops:
  2.5 4.3 %copy-start = (bf16[1,16,128,128]{3,2,1,0:T(8,128)(2,1)S(1)}, bf16[1,16,128,128]{3,2,1,0:T(8,128)(2,1)}, u32[]{:S(2)}) copy-start(bf16[1,16,128,128]{3,2,1,0:T(8,128)(2,1)} %param.5) | copy-start | bytes 1572868
  8.0 5.9 %copy-start.2 = (s32[256]{0:T(256)S(1)}, s32[256]{0:T(256)}, u32[]{:S(2)}) copy-start(s32[256]{0:T(256)} %param.6) | copy-start | bytes 3076
  8.0 21.7 %all-to-all-start.1 = ((bf16[16,2,128,128]{3,2,1,0:T(8,128)(2,1)}), bf16[16,2,128,128]{3,2,1,0:T(8,128)(2,1)S(1)}, u32[]{:S(2)}, u32[]{:S(2)}) async-start(bf16[16,2,128,128]{3,2,1,0:T(8,128)(2,1)} %copy.22), calls=%async_computation.1 | async-start | bytes 2097152 | tf_op jit(solution)/shard_map/all_to_all | solution.py:22
  13.8 17.0 %copy-start.1 = (f32[8]{0:T(128)S(1)}, f32[8]{0:T(128)}, u32[]{:S(2)}) copy-start(f32[8]{0:T(128)} %param.7) | copy-start | bytes 100
  30.0 1.8 %collective-permute-start = (f32[128,128]{1,0:T(8,128)S(1)}, f32[128,128]{1,0:T(8,128)S(1)}, u32[]{:S(2)}, u32[]{:S(2)}) collective-permute-start(f32[128,128]{1,0:T(8,128)S(1)} %get-tuple-element.6), channel_id=1, source_target_pairs={{0,0},{1,1},{2,16},{3,17},{4,32},{5,33},{6,48},{7,49},{8,64},{9,65... | collective-permute-start | bytes 196616 | tf_op jit(solution)/shard_map/ppermute | solution.py:36
  30.7 1.3 %collective-permute-start.1 = (f32[128,128]{1,0:T(8,128)S(1)}, f32[128,128]{1,0:T(8,128)S(1)}, u32[]{:S(2)}, u32[]{:S(2)}) collective-permute-start(f32[128,128]{1,0:T(8,128)S(1)} %get-tuple-element.7), channel_id=1, source_target_pairs={{0,1},{1,0},{2,17},{3,16},{4,33},{5,32},{6,49},{7,48},{8,65},{9,64... | collective-permute-start | bytes 196616 | tf_op jit(solution)/shard_map/ppermute | solution.py:37
  60.1 46.9 %all-to-all-start = ((bf16[16,384,128]{2,1,0:T(8,128)(2,1)}), bf16[16,384,128]{2,1,0:T(8,128)(2,1)S(1)}, u32[]{:S(2)}, u32[]{:S(2)}) async-start(bf16[16,384,128]{2,1,0:T(8,128)(2,1)} %param.4), calls=%async_computation | async-start | bytes 3145728 | tf_op jit(solution)/shard_map/all_to_all | solution.py:15

commit v2 on v1

v2 whole, which is shorter than its diff:
```python
import functools

import jax
import jax.numpy as jnp
from jax import lax
from jax.experimental import pallas as pl
from jax.experimental.pallas import tpu as pltpu
from jax.sharding import PartitionSpec as P

F32 = jnp.float32
BF16 = jnp.bfloat16


def dot(a, b):
    return lax.dot_general(a, b, (((1,), (0,)), ((), ())), preferred_element_type=F32)


def dot_t(a, b):
    return lax.dot_general(a, b, (((0,), (0,)), ((), ())), preferred_element_type=F32)


def kept_rows(source, count, pole, poles, block):
    zero = jnp.zeros((block, block), BF16)
    rows_local = source.shape[0] // block
    return jnp.concatenate(
        [
            lax.select(k * poles + pole < count, source[pl.ds(k * block, block), :], zero)
            for k in range(rows_local)
        ],
        axis=0,
    )


def gram_kernel(poles, share, at_ref, count_ref, panel_ref, inv_ref, *out_refs):
    pole, col = at_ref[0], at_ref[1]
    owned, block = inv_ref.shape[0], inv_ref.shape[1]
    for k, out_ref in enumerate(out_refs):
        for t in range(share):
            i = col ^ (share * ((pole // 2) ^ k) + t)
            x = kept_rows(panel_ref.at[i], count_ref[i * owned + col], pole, poles, block)
            out_ref[t, 0] = inv_ref[i]
            out_ref[t, 1] = dot_t(x, x).astype(BF16)


def sums_kernel(share, at_ref, w_ref, *refs):
    *got_refs, m_ref, g_ref = refs
    pole = at_ref[0]
    for t in range(share):
        m = g = None
        for k, got_ref in enumerate(got_refs):
            mk = -w_ref[pole ^ (2 * k)] * got_ref[t, 0].astype(F32)
            gk = got_ref[t, 1].astype(F32)
            m, g = (mk, gk) if m is None else (m + mk, g + gk)
        m_ref[t] = m.astype(BF16)
        g_ref[t] = g.astype(BF16)


def both_kernel(a_ref, b_ref, *out_refs):
    for t, out_ref in enumerate(out_refs):
        out_ref[...] = (a_ref[t].astype(F32) + b_ref[t].astype(F32)).astype(BF16)


def add_kernel(a_ref, b_ref, out_ref):
    out_ref[...] = (a_ref[...].astype(F32) + b_ref[...].astype(F32)).astype(BF16)


def diag_kernel(share, at_ref, count_ref, w_ref, *refs):
    half = (len(refs) - 1 - share)
    g_refs, got_refs, out_ref = refs[:share], refs[share:share + half], refs[-1]
    pole, col = at_ref[0], at_ref[1]
    owned = share * half
    block = g_refs[0].shape[0]
    chunk = out_ref.shape[2]
    for t in range(share):
        count = count_ref[col * owned + (col ^ (share * (pole // 2) + t))]
        scale = 1.0 / (jnp.full((block, block), block, F32) * count.astype(F32))
        g = g_refs[t][...]
        acc = jnp.zeros((block, block), F32)
        base = jnp.zeros((block, block), F32)
        for k in range(half):
            inv = got_refs[k][t, 0]
            w = w_ref[pole ^ (2 * k)]
            v = w * dot(g, inv)
            hi = v.astype(BF16)
            lo = (v - hi.astype(F32)).astype(BF16)
            acc = acc + dot_t(inv, hi) + dot_t(inv, lo)
            base = base + w * inv.astype(F32)
        d = (base + acc * scale).astype(BF16)
        for p in range(out_ref.shape[0]):
            out_ref[p, t] = d[p * chunk:(p + 1) * chunk]


def finish_kernel(share, at_ref, got_ref, out_ref):
    col = at_ref[1]
    for x in range(got_ref.shape[0] // 2):
        for t in range(share):
            d = got_ref[2 * x, t].astype(F32) + got_ref[2 * x + 1, t].astype(F32)
            out_ref[col ^ (share * x + t)] = d.astype(BF16)


def density_kernel(poles, share, at_ref, count_ref, moved_ref, *refs):
    *m_refs, out_ref = refs
    pole, col = at_ref[0], at_ref[1]
    owned, block = moved_ref.shape[0], moved_ref.shape[2]
    for k, m_ref in enumerate(m_refs):
        for t in range(share):
            i = col ^ (share * ((pole // 2) ^ k) + t)
            x = kept_rows(moved_ref.at[i], count_ref[col * owned + i], pole, poles, block)
            out_ref[i] = dot(x, m_ref[t]).astype(BF16)


def shards(panel, pivot_inverse, row_count, pole_weight):
    owned, rows, block = panel.shape
    poles = lax.axis_size("pole")
    cols = lax.axis_size("col")
    pole_at = lax.axis_index("pole")
    col_at = lax.axis_index("col")
    half = poles // 2
    share = owned // half
    chunk = block // poles
    at = jnp.stack([pole_at, col_at]).astype(jnp.int32)
    smem = pl.BlockSpec(memory_space=pltpu.SMEM)
    vmem = pl.BlockSpec(memory_space=pltpu.VMEM)
    shape = lambda *s: jax.ShapeDtypeStruct(s, BF16)

    def call(body, name, ins, outs, flops=0):
        moved_bytes = 2 * sum(o.size for o in outs) * 2
        return pl.pallas_call(
            body,
            in_specs=ins,
            out_specs=[vmem] * len(outs),
            out_shape=outs,
            compiler_params=pltpu.CompilerParams(vmem_limit_bytes=32 * 1024 * 1024),
            cost_estimate=pl.CostEstimate(flops=flops, bytes_accessed=moved_bytes, transcendentals=0),
            name=name,
        )

    def swap(x, k):
        return lax.ppermute(x, "pole", [(i, i ^ k) for i in range(poles)])

    moved = lax.all_to_all(panel, "col", 0, 0, tiled=True)

    sent = call(
        functools.partial(gram_kernel, poles, share), "gram",
        [smem, smem, vmem, vmem], [shape(share, 2, block, block)] * half,
        2 * owned * rows * block * block,
    )(at, row_count, panel, pivot_inverse[0])
    got = [sent[0]] + [swap(sent[k], 2 * k) for k in range(1, half)]
    mhalf, ghalf = call(
        functools.partial(sums_kernel, share), "sums",
        [smem, smem] + [vmem] * half, [shape(share, block, block)] * 2,
    )(at, pole_weight, *got)

    grams = call(both_kernel, "grams", [vmem] * 2, [shape(block, block)] * share)(ghalf, swap(ghalf, 1))

    def to_owner(g, t):
        return lax.ppermute(
            g, ("pole", "col"),
            [(p * cols + c, p * cols + (c ^ (share * (p // 2) + t))) for p in range(poles) for c in range(cols)],
        )

    grams = [to_owner(g, t) for t, g in enumerate(grams)]
    mfull = call(add_kernel, "weights", [vmem] * 2, [shape(share, block, block)])(mhalf, swap(mhalf, 1))[0]
    mparts = [mfull] + [swap(mfull, 2 * k) for k in range(1, half)]

    part = call(
        functools.partial(diag_kernel, share), "diag",
        [smem, smem, smem] + [vmem] * (share + half), [shape(poles, share, chunk, block)],
        6 * owned * block * block * block,
    )(at, row_count, pole_weight, *grams, *got)[0]
    part, moved = lax.optimization_barrier((part, moved))
    part = lax.all_to_all(part, "pole", 0, 0, tiled=True)
    diag = call(functools.partial(finish_kernel, share), "finish", [smem, vmem], [shape(owned, chunk, block)])(at, part)[0]

    density = call(
        functools.partial(density_kernel, poles, share), "density",
        [smem, smem, vmem] + [vmem] * half, [shape(owned, rows, block)],
        2 * owned * rows * block * block,
    )(at, row_count, moved, *mparts)[0]
    return density, diag


def solution(mesh):
    placed = (P("col", "pole", None), P("pole", "col", None, None), P(), P())
    return jax.shard_map(
        shards,
        mesh=mesh,
        in_specs=placed,
        out_specs=(P("col", "pole", None), P("col", "pole", None)),
        check_vma=False,
    )
```

time: 111 us -> 68.6 us (0.62)
  the two profiles are of different devices: /device:TPU:0 before, /device:TPU:1 now
where the time goes in v2:
time: 68.6 us; the launch traced here: 68.3 us
  starting transfers between devices  39.5 us (58%)
  waiting for transfers between devices  19.2 us (28%)
  Pallas kernels  7.84 us (11%)
  local copies, waits for them, and re-layouts  1.05 us (2%)
  between operations  0.72 us (1%)
    ppermute x8, starting transfers between devices, swap(): return lax.ppermute(x, 'pole', [(i, i ^ k) for i in range(poles)])  16.6 us
    ppermute x8, waiting for transfers between devices, swap(): return lax.ppermute(x, 'pole', [(i, i ^ k) for i in range(poles)])  16.2 us
    all_to_all x1, starting transfers between devices, shards(): moved = lax.all_to_all(panel, 'col', 0, 0, tiled=True)  9.44 us
    all_to_all x1, starting transfers between devices, shards(): part = lax.all_to_all(part, 'pole', 0, 0, tiled=True)  7.5 us
    ppermute x4, starting transfers between devices, to_owner(): lax.ppermute(g, ('pole', 'col'), [(p * cols + c, p * cols + (c ^ share *...  5.96 us
    all_to_all x1, waiting for transfers between devices, shards(): part = lax.all_to_all(part, 'pole', 0, 0, tiled=True)  2.96 us
    pallas_call x1, Pallas kernels, shards(): call(functools.partial(diag_kernel, share), 'diag', [smem, smem, smem] +...  2.42 us
    pallas_call x1, Pallas kernels, shards(): call(functools.partial(density_kernel, poles, share), 'density', [smem, s...  2.27 us
  transfers between devices with their start and end apart: 14, of which 5 were waited for; matrix products, arithmetic and copies ran while one was open for 0% of the time, Pallas kernels for 10%

profile of v2, /device:TPU:1, one launch (start us, length us, event | category | flops | bytes accessed | tf_op | source)
XLA Modules:
  0.0 68.3 jit_solution(6036186555825646028)
XLA Ops:
  0.6 9.4 %all-to-all-start = ((bf16[16,384,128]{2,1,0:T(8,128)(2,1)}), bf16[16,384,128]{2,1,0:T(8,128)(2,1)S(1)}, u32[]{:S(2)}, u32[]{:S(2)}) async-start(bf16[16,384,128]{2,1,0:T(8,128)(2,1)} %panel_ref.1), calls=%async_computation | async-start | bytes 3145728 | tf_op jit(solution)/shard_map/all_to_all | solution.py:141
  10.1 0.1 pad_add_fusion.at_ref
  10.2 1.0 %copy-done.1 = bf16[1,16,128,128]{3,2,1,0:T(8,128)(2,1)S(1)} copy-done((bf16[1,16,128,128]{3,2,1,0:T(8,128)(2,1)S(1)}, bf16[1,16,128,128]{3,2,1,0:T(8,128)(2,1)}, u32[]{:S(2)}) %copy-start.1) | copy-done | bytes 524312
  11.2 1.2 %gram.1 = (bf16[4,2,128,128]{3,2,1,0:T(8,128)(2,1)S(1)}, bf16[4,2,128,128]{3,2,1,0:T(8,128)(2,1)S(1)}, bf16[4,2,128,128]{3,2,1,0:T(8,128)(2,1)S(1)}, bf16[4,2,128,128]{3,2,1,0:T(8,128)(2,1)S(1)}) custom-call(s32[2]{0:T(128)S(1)} %pad_add_fusion.at_ref, s32[256]{0:T(256)S(1)} %copy-done.2, bf16[16,384,128]{2,1,0:T(8,128)(2,1)S(1)} %copy-done, ...), custom_call_target="tpu_custom_call" | custom-call | flops 201326592 | bytes 2097152 | tf_op jit(solution)/shard_map/gram/pallas_call | solution.py:143
  12.4 1.3 %collective-permute-start = (bf16[4,2,128,128]{3,2,1,0:T(8,128)(2,1)S(1)}, bf16[4,2,128,128]{3,2,1,0:T(8,128)(2,1)S(1)}, u32[]{:S(2)}, u32[]{:S(2)}) collective-permute-start(bf16[4,2,128,128]{3,2,1,0:T(8,128)(2,1)S(1)} %get-tuple-element.15), channel_id=1, source_target_pairs={{0,32},{16,48},{32,0},{48,16},{64,96},{80,112},{96,64},{112,80},{1... | collective-permute-start | bytes 786440 | tf_op jit(solution)/shard_map/ppermute | solution.py:139
  13.7 2.4 %collective-permute-start.1 = (bf16[4,2,128,128]{3,2,1,0:T(8,128)(2,1)S(1)}, bf16[4,2,128,128]{3,2,1,0:T(8,128)(2,1)S(1)}, u32[]{:S(2)}, u32[]{:S(2)}) collective-permute-start(bf16[4,2,128,128]{3,2,1,0:T(8,128)(2,1)S(1)} %get-tuple-element.16), channel_id=1, source_target_pairs={{0,64},{16,80},{32,96},{48,112},{64,0},{80,16},{96,32},{112,48},{1... | collective-permute-start | bytes 786440 | tf_op jit(solution)/shard_map/ppermute | solution.py:139
  16.2 0.2 collective-permute-start.2
  16.4 4.0 %collective-permute-done.refs_1_.refs_5_ = bf16[4,2,128,128]{3,2,1,0:T(8,128)(2,1)S(1)} collective-permute-done((bf16[4,2,128,128]{3,2,1,0:T(8,128)(2,1)S(1)}, bf16[4,2,128,128]{3,2,1,0:T(8,128)(2,1)S(1)}, u32[]{:S(2)}, u32[]{:S(2)}) %collective-permute-start) | collective-permute-done | bytes 262176 | tf_op jit(solution)/shard_map/ppermute | solution.py:139
  20.4 7.8 %collective-permute-done.1.refs_2_.refs_6_ = bf16[4,2,128,128]{3,2,1,0:T(8,128)(2,1)S(1)} collective-permute-done((bf16[4,2,128,128]{3,2,1,0:T(8,128)(2,1)S(1)}, bf16[4,2,128,128]{3,2,1,0:T(8,128)(2,1)S(1)}, u32[]{:S(2)}, u32[]{:S(2)}) %collective-permute-start.1) | collective-permute-done | bytes 262176 | tf_op jit(solution)/shard_map/ppermute | solution.py:139
  28.2 2.0 %collective-permute-done.2.refs_3_.refs_7_ = bf16[4,2,128,128]{3,2,1,0:T(8,128)(2,1)S(1)} collective-permute-done((bf16[4,2,128,128]{3,2,1,0:T(8,128)(2,1)S(1)}, bf16[4,2,128,128]{3,2,1,0:T(8,128)(2,1)S(1)}, u32[]{:S(2)}, u32[]{:S(2)}) %collective-permute-start.2) | collective-permute-done | bytes 262176 | tf_op jit(solution)/shard_map/ppermute | solution.py:139
  30.2 0.7 %sums.1 = (bf16[4,128,128]{2,1,0:T(8,128)(2,1)S(1)}, bf16[4,128,128]{2,1,0:T(8,128)(2,1)S(1)}) custom-call(s32[2]{0:T(128)S(1)} %pad_add_fusion.at_ref, f32[8]{0:T(128)S(1)} %copy-done.3, bf16[4,2,128,128]{3,2,1,0:T(8,128)(2,1)S(1)} %get-tuple-element.14.refs_0_.refs_4_, bf16[4,2,128,128]{3,2,1,0:T(8,128)(2,1)S(1)} %collective-permute-done.refs_1_.refs_5_, ...), custom_call_target="tpu_custom_call" | custom-call | bytes 524288 | tf_op jit(solution)/shard_map/sums/pallas_call | solution.py:149
  30.9 0.8 %collective-permute-start.3 = (bf16[4,128,128]{2,1,0:T(8,128)(2,1)S(1)}, bf16[4,128,128]{2,1,0:T(8,128)(2,1)S(1)}, u32[]{:S(2)}, u32[]{:S(2)}) collective-permute-start(bf16[4,128,128]{2,1,0:T(8,128)(2,1)S(1)} %get-tuple-element.18.a_ref), channel_id=1, source_target_pairs={{0,16},{16,0},{32,48},{48,32},{64,80},{80,64},{96,112},{112,96},{1... | collective-permute-start | bytes 393224 | tf_op jit(solution)/shard_map/ppermute | solution.py:139
  31.8 0.7 %collective-permute-start.8 = (bf16[4,128,128]{2,1,0:T(8,128)(2,1)S(1)}, bf16[4,128,128]{2,1,0:T(8,128)(2,1)S(1)}, u32[]{:S(2)}, u32[]{:S(2)}) collective-permute-start(bf16[4,128,128]{2,1,0:T(8,128)(2,1)S(1)} %get-tuple-element.24.a_ref), channel_id=1, source_target_pairs={{0,16},{16,0},{32,48},{48,32},{64,80},{80,64},{96,112},{112,96},{1... | collective-permute-start | bytes 393224 | tf_op jit(solution)/shard_map/ppermute | solution.py:139
  32.5 2.4 %collective-permute-done.3.b_ref = bf16[4,128,128]{2,1,0:T(8,128)(2,1)S(1)} collective-permute-done((bf16[4,128,128]{2,1,0:T(8,128)(2,1)S(1)}, bf16[4,128,128]{2,1,0:T(8,128)(2,1)S(1)}, u32[]{:S(2)}, u32[]{:S(2)}) %collective-permute-start.3) | collective-permute-done | bytes 131104 | tf_op jit(solution)/shard_map/ppermute | solution.py:139
  34.9 0.7 collective-permute-start.4
  35.6 3.6 %collective-permute-start.5 = (bf16[128,128]{1,0:T(8,128)(2,1)S(1)}, bf16[128,128]{1,0:T(8,128)(2,1)S(1)}, u32[]{:S(2)}, u32[]{:S(2)}) collective-permute-start(bf16[128,128]{1,0:T(8,128)(2,1)S(1)} %get-tuple-element.20), channel_id=1, source_target_pairs={{0,1},{1,0},{2,3},{3,2},{4,5},{5,4},{6,7},{7,6},{8,9},{9,8},{10,11... | collective-permute-start | bytes 98312 | tf_op jit(solution)/shard_map/ppermute | solution.py:157
  39.1 1.1 %collective-permute-start.6 = (bf16[128,128]{1,0:T(8,128)(2,1)S(1)}, bf16[128,128]{1,0:T(8,128)(2,1)S(1)}, u32[]{:S(2)}, u32[]{:S(2)}) collective-permute-start(bf16[128,128]{1,0:T(8,128)(2,1)S(1)} %get-tuple-element.21), channel_id=1, source_target_pairs={{0,2},{1,3},{2,0},{3,1},{4,6},{5,7},{6,4},{7,5},{8,10},{9,11},{10,... | collective-permute-start | bytes 98312 | tf_op jit(solution)/shard_map/ppermute | solution.py:157
  40.2 0.7 collective-permute-start.7
  40.9 0.0 collective-permute-done.8.b_ref
  40.9 10.4 %collective-permute-start.11 = (bf16[4,128,128]{2,1,0:T(8,128)(2,1)S(1)}, bf16[4,128,128]{2,1,0:T(8,128)(2,1)S(1)}, u32[]{:S(2)}, u32[]{:S(2)}) collective-permute-start(bf16[4,128,128]{2,1,0:T(8,128)(2,1)S(1)} %weights.1.refs_0_), channel_id=1, source_target_pairs={{0,96},{16,112},{32,64},{48,80},{64,32},{80,48},{96,0},{112,16},{1... | collective-permute-start | bytes 393224 | tf_op jit(solution)/shard_map/ppermute | solution.py:139
  51.3 0.0 collective-permute-done.4.refs_0_
  51.3 0.0 collective-permute-start.10
  51.3 0.0 collective-permute-done.5.refs_1_
  51.3 0.7 collective-permute-start.9
  52.0 2.4 %diag.1 = bf16[8,4,16,128]{3,2,1,0:T(8,128)(2,1)} custom-call(s32[2]{0:T(128)S(1)} %pad_add_fusion.at_ref, s32[256]{0:T(256)S(1)} %copy-done.2, f32[8]{0:T(128)S(1)} %copy-done.3, bf16[128,128]{1,0:T(8,128)(2,1)S(1)} %collective-permute-done.4.refs_0_, bf16[128,128]{1,0:T(8,128)(2,1)S(1)} %collective-permute-done.5.refs_1_, ...), custom_call_target="tpu_custom_call" | custom-call | flops 201326592 | bytes 262144 | tf_op jit(solution)/shard_map/diag/pallas_call | solution.py:166
  54.4 0.0 all-to-all-done.moved_ref
  54.4 7.5 %all-to-all-start.1 = ((bf16[8,4,16,128]{3,2,1,0:T(8,128)(2,1)}), bf16[8,4,16,128]{3,2,1,0:T(8,128)(2,1)S(1)}, u32[]{:S(2)}, u32[]{:S(2)}) async-start(bf16[8,4,16,128]{3,2,1,0:T(8,128)(2,1)} %diag.1), calls=%async_computation.1 | async-start | bytes 262144 | tf_op jit(solution)/shard_map/all_to_all | solution.py:172
  61.9 0.0 collective-permute-done.11.refs_3_
  61.9 0.0 collective-permute-done.10.refs_2_
  61.9 2.3 %density.1 = bf16[16,384,128]{2,1,0:T(8,128)(2,1)} custom-call(s32[2]{0:T(128)S(1)} %pad_add_fusion.at_ref, s32[256]{0:T(256)S(1)} %copy-done.2, bf16[16,384,128]{2,1,0:T(8,128)(2,1)S(1)} %all-to-all-done.moved_ref, bf16[4,128,128]{2,1,0:T(8,128)(2,1)S(1)} %weights.1.refs_0_, bf16[4,128,128]{2,1,0:T(8,128)(2,1)S(1)} %collective-permute-done.9.refs_1_, ...), custom_call_target="tpu_custom_call" | custom-call | flops 201326592 | bytes 3145728 | tf_op jit(solution)/shard_map/density/pallas_call | solution.py:175
  64.2 3.0 %all-to-all-done.1.got_ref = bf16[8,4,16,128]{3,2,1,0:T(8,128)(2,1)S(1)} async-done(((bf16[8,4,16,128]{3,2,1,0:T(8,128)(2,1)}), bf16[8,4,16,128]{3,2,1,0:T(8,128)(2,1)S(1)}, u32[]{:S(2)}, u32[]{:S(2)}) %all-to-all-start.1) | async-done | bytes 131104 | tf_op jit(solution)/shard_map/all_to_all | solution.py:172
  67.1 1.2 %finish.1 = bf16[16,16,128]{2,1,0:T(8,128)(2,1)} custom-call(s32[2]{0:T(128)S(1)} %pad_add_fusion.at_ref, bf16[8,4,16,128]{3,2,1,0:T(8,128)(2,1)S(1)} %all-to-all-done.1.got_ref), custom_call_target="tpu_custom_call" | custom-call | bytes 131072 | tf_op jit(solution)/shard_map/finish/pallas_call | solution.py:173
  (12 shorter events, 0.1 us)
Async XLA Ops:
  0.6 9.6 %copy-start = (bf16[16,384,128]{2,1,0:T(8,128)(2,1)S(1)}, bf16[16,384,128]{2,1,0:T(8,128)(2,1)}, u32[]{:S(2)}) copy-start(bf16[16,384,128]{2,1,0:T(8,128)(2,1)} %panel_ref.1) | copy-start | bytes 4718596
  0.6 9.5 %copy-start.2 = (s32[256]{0:T(256)S(1)}, s32[256]{0:T(256)}, u32[]{:S(2)}) copy-start(s32[256]{0:T(256)} %count_ref.5) | copy-start | bytes 3076
  0.6 53.7 %all-to-all-start = ((bf16[16,384,128]{2,1,0:T(8,128)(2,1)}), bf16[16,384,128]{2,1,0:T(8,128)(2,1)S(1)}, u32[]{:S(2)}, u32[]{:S(2)}) async-start(bf16[16,384,128]{2,1,0:T(8,128)(2,1)} %panel_ref.1), calls=%async_computation | async-start | bytes 3145728 | tf_op jit(solution)/shard_map/all_to_all | solution.py:141
  10.1 20.1 %copy-start.3 = (f32[8]{0:T(128)S(1)}, f32[8]{0:T(128)}, u32[]{:S(2)}) copy-start(f32[8]{0:T(128)} %w_ref.3) | copy-start | bytes 100
  10.2 1.0 %copy-start.1 = (bf16[1,16,128,128]{3,2,1,0:T(8,128)(2,1)S(1)}, bf16[1,16,128,128]{3,2,1,0:T(8,128)(2,1)}, u32[]{:S(2)}) copy-start(bf16[1,16,128,128]{3,2,1,0:T(8,128)(2,1)} %param.5) | copy-start | bytes 1572868
  12.4 8.0 %collective-permute-start = (bf16[4,2,128,128]{3,2,1,0:T(8,128)(2,1)S(1)}, bf16[4,2,128,128]{3,2,1,0:T(8,128)(2,1)S(1)}, u32[]{:S(2)}, u32[]{:S(2)}) collective-permute-start(bf16[4,2,128,128]{3,2,1,0:T(8,128)(2,1)S(1)} %get-tuple-element.15), channel_id=1, source_target_pairs={{0,32},{16,48},{32,0},{48,16},{64,96},{80,112},{96,64},{112,80},{1... | collective-permute-start | bytes 786440 | tf_op jit(solution)/shard_map/ppermute | solution.py:139
  13.7 14.5 %collective-permute-start.1 = (bf16[4,2,128,128]{3,2,1,0:T(8,128)(2,1)S(1)}, bf16[4,2,128,128]{3,2,1,0:T(8,128)(2,1)S(1)}, u32[]{:S(2)}, u32[]{:S(2)}) collective-permute-start(bf16[4,2,128,128]{3,2,1,0:T(8,128)(2,1)S(1)} %get-tuple-element.16), channel_id=1, source_target_pairs={{0,64},{16,80},{32,96},{48,112},{64,0},{80,16},{96,32},{112,48},{1... | collective-permute-start | bytes 786440 | tf_op jit(solution)/shard_map/ppermute | solution.py:139
  16.2 14.0 %collective-permute-start.2 = (bf16[4,2,128,128]{3,2,1,0:T(8,128)(2,1)S(1)}, bf16[4,2,128,128]{3,2,1,0:T(8,128)(2,1)S(1)}, u32[]{:S(2)}, u32[]{:S(2)}) collective-permute-start(bf16[4,2,128,128]{3,2,1,0:T(8,128)(2,1)S(1)} %get-tuple-element.17), channel_id=1, source_target_pairs={{0,96},{16,112},{32,64},{48,80},{64,32},{80,48},{96,0},{112,16},{1... | collective-permute-start | bytes 786440 | tf_op jit(solution)/shard_map/ppermute | solution.py:139
  30.9 3.9 %collective-permute-start.3 = (bf16[4,128,128]{2,1,0:T(8,128)(2,1)S(1)}, bf16[4,128,128]{2,1,0:T(8,128)(2,1)S(1)}, u32[]{:S(2)}, u32[]{:S(2)}) collective-permute-start(bf16[4,128,128]{2,1,0:T(8,128)(2,1)S(1)} %get-tuple-element.18.a_ref), channel_id=1, source_target_pairs={{0,16},{16,0},{32,48},{48,32},{64,80},{80,64},{96,112},{112,96},{1... | collective-permute-start | bytes 393224 | tf_op jit(solution)/shard_map/ppermute | solution.py:139
  31.8 9.1 %collective-permute-start.8 = (bf16[4,128,128]{2,1,0:T(8,128)(2,1)S(1)}, bf16[4,128,128]{2,1,0:T(8,128)(2,1)S(1)}, u32[]{:S(2)}, u32[]{:S(2)}) collective-permute-start(bf16[4,128,128]{2,1,0:T(8,128)(2,1)S(1)} %get-tuple-element.24.a_ref), channel_id=1, source_target_pairs={{0,16},{16,0},{32,48},{48,32},{64,80},{80,64},{96,112},{112,96},{1... | collective-permute-start | bytes 393224 | tf_op jit(solution)/shard_map/ppermute | solution.py:139
  34.9 16.4 %collective-permute-start.4 = (bf16[128,128]{1,0:T(8,128)(2,1)S(1)}, bf16[128,128]{1,0:T(8,128)(2,1)S(1)}, u32[]{:S(2)}, u32[]{:S(2)}) collective-permute-start(bf16[128,128]{1,0:T(8,128)(2,1)S(1)} %get-tuple-element.19), channel_id=1, source_target_pairs={{0,0},{1,1},{2,2},{3,3},{4,4},{5,5},{6,6},{7,7},{8,8},{9,9},{10,10... | collective-permute-start | bytes 98312 | tf_op jit(solution)/shard_map/ppermute | solution.py:157
  35.6 15.7 %collective-permute-start.5 = (bf16[128,128]{1,0:T(8,128)(2,1)S(1)}, bf16[128,128]{1,0:T(8,128)(2,1)S(1)}, u32[]{:S(2)}, u32[]{:S(2)}) collective-permute-start(bf16[128,128]{1,0:T(8,128)(2,1)S(1)} %get-tuple-element.20), channel_id=1, source_target_pairs={{0,1},{1,0},{2,3},{3,2},{4,5},{5,4},{6,7},{7,6},{8,9},{9,8},{10,11... | collective-permute-start | bytes 98312 | tf_op jit(solution)/shard_map/ppermute | solution.py:157
  39.1 12.8 %collective-permute-start.6 = (bf16[128,128]{1,0:T(8,128)(2,1)S(1)}, bf16[128,128]{1,0:T(8,128)(2,1)S(1)}, u32[]{:S(2)}, u32[]{:S(2)}) collective-permute-start(bf16[128,128]{1,0:T(8,128)(2,1)S(1)} %get-tuple-element.21), channel_id=1, source_target_pairs={{0,2},{1,3},{2,0},{3,1},{4,6},{5,7},{6,4},{7,5},{8,10},{9,11},{10,... | collective-permute-start | bytes 98312 | tf_op jit(solution)/shard_map/ppermute | solution.py:157
  40.2 11.8 %collective-permute-start.7 = (bf16[128,128]{1,0:T(8,128)(2,1)S(1)}, bf16[128,128]{1,0:T(8,128)(2,1)S(1)}, u32[]{:S(2)}, u32[]{:S(2)}) collective-permute-start(bf16[128,128]{1,0:T(8,128)(2,1)S(1)} %get-tuple-element.22), channel_id=1, source_target_pairs={{0,3},{1,2},{2,1},{3,0},{4,7},{5,6},{6,5},{7,4},{8,11},{9,10},{10,... | collective-permute-start | bytes 98312 | tf_op jit(solution)/shard_map/ppermute | solution.py:157
  40.9 21.0 %collective-permute-start.11 = (bf16[4,128,128]{2,1,0:T(8,128)(2,1)S(1)}, bf16[4,128,128]{2,1,0:T(8,128)(2,1)S(1)}, u32[]{:S(2)}, u32[]{:S(2)}) collective-permute-start(bf16[4,128,128]{2,1,0:T(8,128)(2,1)S(1)} %weights.1.refs_0_), channel_id=1, source_target_pairs={{0,96},{16,112},{32,64},{48,80},{64,32},{80,48},{96,0},{112,16},{1... | collective-permute-start | bytes 393224 | tf_op jit(solution)/shard_map/ppermute | solution.py:139
  51.3 10.6 %collective-permute-start.10 = (bf16[4,128,128]{2,1,0:T(8,128)(2,1)S(1)}, bf16[4,128,128]{2,1,0:T(8,128)(2,1)S(1)}, u32[]{:S(2)}, u32[]{:S(2)}) collective-permute-start(bf16[4,128,128]{2,1,0:T(8,128)(2,1)S(1)} %weights.1.refs_0_), channel_id=1, source_target_pairs={{0,64},{16,80},{32,96},{48,112},{64,0},{80,16},{96,32},{112,48},{1... | collective-permute-start | bytes 393224 | tf_op jit(solution)/shard_map/ppermute | solution.py:139
  51.3 10.6 %collective-permute-start.9 = (bf16[4,128,128]{2,1,0:T(8,128)(2,1)S(1)}, bf16[4,128,128]{2,1,0:T(8,128)(2,1)S(1)}, u32[]{:S(2)}, u32[]{:S(2)}) collective-permute-start(bf16[4,128,128]{2,1,0:T(8,128)(2,1)S(1)} %weights.1.refs_0_), channel_id=1, source_target_pairs={{0,32},{16,48},{32,0},{48,16},{64,96},{80,112},{96,64},{112,80},{1... | collective-permute-start | bytes 393224 | tf_op jit(solution)/shard_map/ppermute | solution.py:139
  54.4 12.8 %all-to-all-start.1 = ((bf16[8,4,16,128]{3,2,1,0:T(8,128)(2,1)}), bf16[8,4,16,128]{3,2,1,0:T(8,128)(2,1)S(1)}, u32[]{:S(2)}, u32[]{:S(2)}) async-start(bf16[8,4,16,128]{3,2,1,0:T(8,128)(2,1)} %diag.1), calls=%async_computation.1 | async-start | bytes 262144 | tf_op jit(solution)/shard_map/all_to_all | solution.py:172

commit v3 on v2

--- a/solution.py
+++ b/solution.py
@@ -34,25 +34,25 @@
 def gram_kernel(poles, share, at_ref, count_ref, panel_ref, inv_ref, *out_refs):
     pole, col = at_ref[0], at_ref[1]
     owned, block = inv_ref.shape[0], inv_ref.shape[1]
-    for k, out_ref in enumerate(out_refs):
+    half = len(out_refs) // 2
+    for k in range(half):
         for t in range(share):
             i = col ^ (share * ((pole // 2) ^ k) + t)
             x = kept_rows(panel_ref.at[i], count_ref[i * owned + col], pole, poles, block)
-            out_ref[t, 0] = inv_ref[i]
-            out_ref[t, 1] = dot_t(x, x).astype(BF16)
-
-
-def sums_kernel(share, at_ref, w_ref, *refs):
-    *got_refs, m_ref, g_ref = refs
-    pole = at_ref[0]
+            out_refs[k][t] = dot_t(x, x).astype(BF16)
+            out_refs[half + k][t] = inv_ref[i]
+
+
+def gsum_kernel(share, *refs):
+    *got_refs, keep_ref, give_ref = refs
     for t in range(share):
-        m = g = None
-        for k, got_ref in enumerate(got_refs):
-            mk = -w_ref[pole ^ (2 * k)] * got_ref[t, 0].astype(F32)
-            gk = got_ref[t, 1].astype(F32)
-            m, g = (mk, gk) if m is None else (m + mk, g + gk)
-        m_ref[t] = m.astype(BF16)
-        g_ref[t] = g.astype(BF16)
+        g = sum(got_ref[t].astype(F32) for got_ref in got_refs).astype(BF16)
+        (give_ref if t % 2 else keep_ref)[t // 2] = g
+
+
+def pair_kernel(a_ref, b_ref, out_ref):
+    out_ref[:, 0] = a_ref[...]
+    out_ref[:, 1] = b_ref[...]
 
 
 def both_kernel(a_ref, b_ref, *out_refs):
@@ -64,28 +64,39 @@
     out_ref[...] = (a_ref[...].astype(F32) + b_ref[...].astype(F32)).astype(BF16)
 
 
-def diag_kernel(share, at_ref, count_ref, w_ref, *refs):
-    half = (len(refs) - 1 - share)
-    g_refs, got_refs, out_ref = refs[:share], refs[share:share + half], refs[-1]
+def prep_kernel(share, at_ref, w_ref, *refs):
+    *got_refs, m_ref, base_ref, wide_ref, flip_ref = refs
+    pole = at_ref[0]
+    block = m_ref.shape[1]
+    for t in range(share):
+        base = jnp.zeros((block, block), F32)
+        for k, got_ref in enumerate(got_refs):
+            inv = got_ref[t]
+            base = base + w_ref[pole ^ (2 * k)] * inv.astype(F32)
+            wide_ref[t, :, k * block:(k + 1) * block] = inv
+            flip_ref[t, :, k * block:(k + 1) * block] = inv.T
+        base_ref[t] = base
+        m_ref[t] = (-base).astype(BF16)
+
+
+def diag_kernel(share, at_ref, count_ref, w_ref, base_ref, wide_ref, flip_ref, *refs):
+    *g_refs, out_ref = refs
     pole, col = at_ref[0], at_ref[1]
+    block = base_ref.shape[1]
+    half = wide_ref.shape[2] // block
     owned = share * half
-    block = g_refs[0].shape[0]
     chunk = out_ref.shape[2]
     for t in range(share):
         count = count_ref[col * owned + (col ^ (share * (pole // 2) + t))]
         scale = 1.0 / (jnp.full((block, block), block, F32) * count.astype(F32))
-        g = g_refs[t][...]
-        acc = jnp.zeros((block, block), F32)
-        base = jnp.zeros((block, block), F32)
-        for k in range(half):
-            inv = got_refs[k][t, 0]
-            w = w_ref[pole ^ (2 * k)]
-            v = w * dot(g, inv)
-            hi = v.astype(BF16)
-            lo = (v - hi.astype(F32)).astype(BF16)
-            acc = acc + dot_t(inv, hi) + dot_t(inv, lo)
-            base = base + w * inv.astype(F32)
-        d = (base + acc * scale).astype(BF16)
+        v = dot(g_refs[t // 2][t % 2], wide_ref[t])
+        v = jnp.concatenate(
+            [w_ref[pole ^ (2 * k)] * v[:, k * block:(k + 1) * block] for k in range(half)], axis=0
+        )
+        hi = v.astype(BF16)
+        lo = (v - hi.astype(F32)).astype(BF16)
+        flip = flip_ref[t]
+        d = (base_ref[t] + (dot(flip, hi) + dot(flip, lo)) * scale).astype(BF16)
         for p in range(out_ref.shape[0]):
             out_ref[p, t] = d[p * chunk:(p + 1) * chunk]
 
@@ -142,32 +153,40 @@
 
     sent = call(
         functools.partial(gram_kernel, poles, share), "gram",
-        [smem, smem, vmem, vmem], [shape(share, 2, block, block)] * half,
+        [smem, smem, vmem, vmem], [shape(share, block, block)] * poles,
         2 * owned * rows * block * block,
     )(at, row_count, panel, pivot_inverse[0])
-    got = [sent[0]] + [swap(sent[k], 2 * k) for k in range(1, half)]
-    mhalf, ghalf = call(
-        functools.partial(sums_kernel, share), "sums",
-        [smem, smem] + [vmem] * half, [shape(share, block, block)] * 2,
-    )(at, pole_weight, *got)
-
-    grams = call(both_kernel, "grams", [vmem] * 2, [shape(block, block)] * share)(ghalf, swap(ghalf, 1))
-
-    def to_owner(g, t):
+    grams = [sent[0]] + [swap(sent[k], 2 * k) for k in range(1, half)]
+    inverses = [sent[half]] + [swap(sent[half + k], 2 * k) for k in range(1, half)]
+
+    keep, give = call(
+        functools.partial(gsum_kernel, share), "gsum", [vmem] * half, [shape(share // 2, block, block)] * 2
+    )(*grams)
+    near = lax.ppermute(give, "col", [(c, c ^ 1) for c in range(cols)])
+    ghalf = call(pair_kernel, "pair", [vmem] * 2, [shape(share // 2, 2, block, block)])(keep, near)[0]
+    gfull = call(both_kernel, "gboth", [vmem] * 2, [shape(2, block, block)] * (share // 2))(ghalf, swap(ghalf, 1))
+
+    def to_owner(g, f):
         return lax.ppermute(
             g, ("pole", "col"),
-            [(p * cols + c, p * cols + (c ^ (share * (p // 2) + t))) for p in range(poles) for c in range(cols)],
+            [(p * cols + c, p * cols + (c ^ (share * (p // 2) + 2 * f))) for p in range(poles) for c in range(cols)],
         )
 
-    grams = [to_owner(g, t) for t, g in enumerate(grams)]
+    gfull = [to_owner(g, f) for f, g in enumerate(gfull)]
+
+    wide = shape(share, block, half * block)
+    mhalf, base, wide, flip = call(
+        functools.partial(prep_kernel, share), "prep", [smem, smem] + [vmem] * half,
+        [shape(share, block, block), jax.ShapeDtypeStruct((share, block, block), F32), wide, wide],
+    )(at, pole_weight, *inverses)
     mfull = call(add_kernel, "weights", [vmem] * 2, [shape(share, block, block)])(mhalf, swap(mhalf, 1))[0]
     mparts = [mfull] + [swap(mfull, 2 * k) for k in range(1, half)]
 
     part = call(
         functools.partial(diag_kernel, share), "diag",
-        [smem, smem, smem] + [vmem] * (share + half), [shape(poles, share, chunk, block)],
+        [smem, smem, smem, vmem, vmem, vmem] + [vmem] * (share // 2), [shape(poles, share, chunk, block)],
         6 * owned * block * block * block,
-    )(at, row_count, pole_weight, *grams, *got)[0]
+    )(at, row_count, pole_weight, base, wide, flip, *gfull)[0]
     part, moved = lax.optimization_barrier((part, moved))
     part = lax.all_to_all(part, "pole", 0, 0, tiled=True)
     diag = call(functools.partial(finish_kernel, share), "finish", [smem, vmem], [shape(owned, chunk, block)])(at, part)[0]

time: 68.6 us -> 61.3 us (0.89)
  the two profiles are of different devices: /device:TPU:1 before, /device:TPU:0 now
where the time goes in v3:
time: 61.3 us; the launch traced here: 61 us
  starting transfers between devices  36.8 us (60%)
  waiting for transfers between devices  14.5 us (24%)
  Pallas kernels  7.89 us (13%)
  local copies, waits for them, and re-layouts  1.06 us (2%)
  between operations  0.74 us (1%)
    ppermute x11, starting transfers between devices, swap(): return lax.ppermute(x, 'pole', [(i, i ^ k) for i in range(poles)])  19 us
    ppermute x11, waiting for transfers between devices, swap(): return lax.ppermute(x, 'pole', [(i, i ^ k) for i in range(poles)])  9.09 us
    all_to_all x1, starting transfers between devices, shards(): moved = lax.all_to_all(panel, 'col', 0, 0, tiled=True)  8.11 us
    all_to_all x1, starting transfers between devices, shards(): part = lax.all_to_all(part, 'pole', 0, 0, tiled=True)  7.58 us
    all_to_all x1, waiting for transfers between devices, shards(): part = lax.all_to_all(part, 'pole', 0, 0, tiled=True)  4.11 us
    pallas_call x1, Pallas kernels, shards(): call(functools.partial(diag_kernel, share), 'diag', [smem, smem, smem, vm...  2.3 us
    pallas_call x1, Pallas kernels, shards(): call(functools.partial(density_kernel, poles, share), 'density', [smem, s...  2.27 us
    ppermute x2, starting transfers between devices, to_owner(): lax.ppermute(g, ('pole', 'col'), [(p * cols + c, p * cols + (c ^ share *...  1.98 us
  transfers between devices with their start and end apart: 16, of which 7 were waited for; matrix products, arithmetic and copies ran while one was open for 0% of the time, Pallas kernels for 11%

profile of v3, /device:TPU:0, one launch (start us, length us, event | category | flops | bytes accessed | tf_op | source)
XLA Modules:
  0.0 61.0 jit_solution(12810731553615074571)
XLA Ops:
  0.6 8.1 %all-to-all-start = ((bf16[16,384,128]{2,1,0:T(8,128)(2,1)}), bf16[16,384,128]{2,1,0:T(8,128)(2,1)S(1)}, u32[]{:S(2)}, u32[]{:S(2)}) async-start(bf16[16,384,128]{2,1,0:T(8,128)(2,1)} %panel_ref.1), calls=%async_computation | async-start | bytes 3145728 | tf_op jit(solution)/shard_map/all_to_all | solution.py:152
  8.8 0.0 copy-start.3
  8.8 0.1 pad_add_fusion.at_ref
  8.9 1.0 %copy-done.1 = bf16[1,16,128,128]{3,2,1,0:T(8,128)(2,1)S(1)} copy-done((bf16[1,16,128,128]{3,2,1,0:T(8,128)(2,1)S(1)}, bf16[1,16,128,128]{3,2,1,0:T(8,128)(2,1)}, u32[]{:S(2)}) %copy-start.1) | copy-done | bytes 524312
  9.9 1.2 %gram.1 = (bf16[4,128,128]{2,1,0:T(8,128)(2,1)S(1)}, bf16[4,128,128]{2,1,0:T(8,128)(2,1)S(1)}, bf16[4,128,128]{2,1,0:T(8,128)(2,1)S(1)}, bf16[4,128,128]{2,1,0:T...) custom-call(s32[2]{0:T(128)S(1)} %pad_add_fusion.at_ref, ...), custom_call_target="tpu_custom_call" | custom-call | flops 201326592 | bytes 2097152 | tf_op jit(solution)/shard_map/gram/pallas_call | solution.py:154
  11.1 1.6 %collective-permute-start.3 = (bf16[4,128,128]{2,1,0:T(8,128)(2,1)S(1)}, bf16[4,128,128]{2,1,0:T(8,128)(2,1)S(1)}, u32[]{:S(2)}, u32[]{:S(2)}) collective-permute-start(bf16[4,128,128]{2,1,0:T(8,128)(2,1)S(1)} %get-tuple-element.28), channel_id=1, source_target_pairs={{0,32},{16,48},{32,0},{48,16},{64,96},{80,112},{96,64},{112,80},{1... | collective-permute-start | bytes 393224 | tf_op jit(solution)/shard_map/ppermute | solution.py:150
  12.7 2.7 %collective-permute-start.4 = (bf16[4,128,128]{2,1,0:T(8,128)(2,1)S(1)}, bf16[4,128,128]{2,1,0:T(8,128)(2,1)S(1)}, u32[]{:S(2)}, u32[]{:S(2)}) collective-permute-start(bf16[4,128,128]{2,1,0:T(8,128)(2,1)S(1)} %get-tuple-element.29), channel_id=1, source_target_pairs={{0,64},{16,80},{32,96},{48,112},{64,0},{80,16},{96,32},{112,48},{1... | collective-permute-start | bytes 393224 | tf_op jit(solution)/shard_map/ppermute | solution.py:150
  15.4 0.5 collective-permute-start.5
  15.9 0.3 collective-permute-start
  16.2 3.9 %collective-permute-start.1 = (bf16[4,128,128]{2,1,0:T(8,128)(2,1)S(1)}, bf16[4,128,128]{2,1,0:T(8,128)(2,1)S(1)}, u32[]{:S(2)}, u32[]{:S(2)}) collective-permute-start(bf16[4,128,128]{2,1,0:T(8,128)(2,1)S(1)} %get-tuple-element.22), channel_id=1, source_target_pairs={{0,64},{16,80},{32,96},{48,112},{64,0},{80,16},{96,32},{112,48},{1... | collective-permute-start | bytes 393224 | tf_op jit(solution)/shard_map/ppermute | solution.py:150
  20.1 0.0 collective-permute-done.3.refs_1_
  20.1 0.5 collective-permute-start.2
  20.6 1.9 %collective-permute-done.4.refs_2_ = bf16[4,128,128]{2,1,0:T(8,128)(2,1)S(1)} collective-permute-done((bf16[4,128,128]{2,1,0:T(8,128)(2,1)S(1)}, bf16[4,128,128]{2,1,0:T(8,128)(2,1)S(1)}, u32[]{:S(2)}, u32[]{:S(2)}) %collective-permute-start.4) | collective-permute-done | bytes 131104 | tf_op jit(solution)/shard_map/ppermute | solution.py:150
  22.5 2.9 %collective-permute-done.5.refs_3_ = bf16[4,128,128]{2,1,0:T(8,128)(2,1)S(1)} collective-permute-done((bf16[4,128,128]{2,1,0:T(8,128)(2,1)S(1)}, bf16[4,128,128]{2,1,0:T(8,128)(2,1)S(1)}, u32[]{:S(2)}, u32[]{:S(2)}) %collective-permute-start.5) | collective-permute-done | bytes 131104 | tf_op jit(solution)/shard_map/ppermute | solution.py:150
  25.4 0.1 gsum.1
  25.5 0.1 collective-permute-start.6
  25.6 1.2 %collective-permute-done.6.b_ref = bf16[2,128,128]{2,1,0:T(8,128)(2,1)S(1)} collective-permute-done((bf16[2,128,128]{2,1,0:T(8,128)(2,1)S(1)}, bf16[2,128,128]{2,1,0:T(8,128)(2,1)S(1)}, u32[]{:S(2)}, u32[]{:S(2)}) %collective-permute-start.6) | collective-permute-done | bytes 65568 | tf_op jit(solution)/shard_map/ppermute | solution.py:165
  26.8 1.1 %collective-permute-start.7 = (bf16[2,2,128,128]{3,2,1,0:T(8,128)(2,1)S(1)}, bf16[2,2,128,128]{3,2,1,0:T(8,128)(2,1)S(1)}, u32[]{:S(2)}, u32[]{:S(2)}) collective-permute-start(bf16[2,2,128,128]{3,2,1,0:T(8,128)(2,1)S(1)} %pair.1.a_ref), channel_id=1, source_target_pairs={{0,16},{16,0},{32,48},{48,32},{64,80},{80,64},{96,112},{112,96},{1... | collective-permute-start | bytes 393224 | tf_op jit(solution)/shard_map/ppermute | solution.py:150
  27.9 2.2 %collective-permute-done.2.refs_3_ = bf16[4,128,128]{2,1,0:T(8,128)(2,1)S(1)} collective-permute-done((bf16[4,128,128]{2,1,0:T(8,128)(2,1)S(1)}, bf16[4,128,128]{2,1,0:T(8,128)(2,1)S(1)}, u32[]{:S(2)}, u32[]{:S(2)}) %collective-permute-start.2) | collective-permute-done | bytes 131104 | tf_op jit(solution)/shard_map/ppermute | solution.py:150
  30.1 0.8 %prep.1 = (bf16[4,128,128]{2,1,0:T(8,128)(2,1)S(1)}, f32[4,128,128]{2,1,0:T(8,128)S(1)}, bf16[4,128,512]{2,1,0:T(8,128)(2,1)S(1)}, bf16[4,128,512]{2,1,0:T(8,128)(2,1)S(1)}) custom-call(s32[2]{0:T(128)S(1)} %pad_add_fusion.at_ref, f32[8]{0:T(128)S(1)} %copy-done.3, bf16[4,128,128]{2,1,0:T(8,128)(2,1)S(1)} %get-tuple-element.20.refs_0_, ...), custom_call_target="tpu_custom_call" | custom-call | bytes 2621440 | tf_op jit(solution)/shard_map/prep/pallas_call | solution.py:178
  31.0 1.1 %collective-permute-start.10 = (bf16[4,128,128]{2,1,0:T(8,128)(2,1)S(1)}, bf16[4,128,128]{2,1,0:T(8,128)(2,1)S(1)}, u32[]{:S(2)}, u32[]{:S(2)}) collective-permute-start(bf16[4,128,128]{2,1,0:T(8,128)(2,1)S(1)} %get-tuple-element.36.a_ref), channel_id=1, source_target_pairs={{0,16},{16,0},{32,48},{48,32},{64,80},{80,64},{96,112},{112,96},{1... | collective-permute-start | bytes 393224 | tf_op jit(solution)/shard_map/ppermute | solution.py:150
  32.1 1.2 %collective-permute-done.7.b_ref = bf16[2,2,128,128]{3,2,1,0:T(8,128)(2,1)S(1)} collective-permute-done((bf16[2,2,128,128]{3,2,1,0:T(8,128)(2,1)S(1)}, bf16[2,2,128,128]{3,2,1,0:T(8,128)(2,1)S(1)}, u32[]{:S(2)}, u32[]{:S(2)}) %collective-permute-start.7) | collective-permute-done | bytes 131104 | tf_op jit(solution)/shard_map/ppermute | solution.py:150
  33.3 0.7 %collective-permute-start.8 = (bf16[2,128,128]{2,1,0:T(8,128)(2,1)S(1)}, bf16[2,128,128]{2,1,0:T(8,128)(2,1)S(1)}, u32[]{:S(2)}, u32[]{:S(2)}) collective-permute-start(bf16[2,128,128]{2,1,0:T(8,128)(2,1)S(1)} %get-tuple-element.33), channel_id=1, source_target_pairs={{0,0},{1,1},{2,2},{3,3},{4,4},{5,5},{6,6},{7,7},{8,8},{9,9},{10,10... | collective-permute-start | bytes 196616 | tf_op jit(solution)/shard_map/ppermute | solution.py:170
  33.9 1.3 %collective-permute-start.9 = (bf16[2,128,128]{2,1,0:T(8,128)(2,1)S(1)}, bf16[2,128,128]{2,1,0:T(8,128)(2,1)S(1)}, u32[]{:S(2)}, u32[]{:S(2)}) collective-permute-start(bf16[2,128,128]{2,1,0:T(8,128)(2,1)S(1)} %get-tuple-element.34), channel_id=1, source_target_pairs={{0,2},{1,3},{2,0},{3,1},{4,6},{5,7},{6,4},{7,5},{8,10},{9,11},{10,... | collective-permute-start | bytes 196616 | tf_op jit(solution)/shard_map/ppermute | solution.py:170
  35.3 0.9 %collective-permute-done.10.b_ref = bf16[4,128,128]{2,1,0:T(8,128)(2,1)S(1)} collective-permute-done((bf16[4,128,128]{2,1,0:T(8,128)(2,1)S(1)}, bf16[4,128,128]{2,1,0:T(8,128)(2,1)S(1)}, u32[]{:S(2)}, u32[]{:S(2)}) %collective-permute-start.10) | collective-permute-done | bytes 131104 | tf_op jit(solution)/shard_map/ppermute | solution.py:150
  36.2 6.4 %collective-permute-start.13 = (bf16[4,128,128]{2,1,0:T(8,128)(2,1)S(1)}, bf16[4,128,128]{2,1,0:T(8,128)(2,1)S(1)}, u32[]{:S(2)}, u32[]{:S(2)}) collective-permute-start(bf16[4,128,128]{2,1,0:T(8,128)(2,1)S(1)} %weights.1.refs_0_), channel_id=1, source_target_pairs={{0,96},{16,112},{32,64},{48,80},{64,32},{80,48},{96,0},{112,16},{1... | collective-permute-start | bytes 393224 | tf_op jit(solution)/shard_map/ppermute | solution.py:150
  42.6 0.9 %collective-permute-start.11 = (bf16[4,128,128]{2,1,0:T(8,128)(2,1)S(1)}, bf16[4,128,128]{2,1,0:T(8,128)(2,1)S(1)}, u32[]{:S(2)}, u32[]{:S(2)}) collective-permute-start(bf16[4,128,128]{2,1,0:T(8,128)(2,1)S(1)} %weights.1.refs_0_), channel_id=1, source_target_pairs={{0,32},{16,48},{32,0},{48,16},{64,96},{80,112},{96,64},{112,80},{1... | collective-permute-start | bytes 393224 | tf_op jit(solution)/shard_map/ppermute | solution.py:150
  43.5 2.3 %diag.1 = bf16[8,4,16,128]{3,2,1,0:T(8,128)(2,1)} custom-call(s32[2]{0:T(128)S(1)} %pad_add_fusion.at_ref, s32[256]{0:T(256)S(1)} %copy-done.2, f32[8]{0:T(128)S(1)} %copy-done.3, f32[4,128,128]{2,1,0:T(8,128)S(1)} %get-tuple-element.24.base_ref, bf16[4,128,512]{2,1,0:T(8,128)(2,1)S(1)} %get-tuple-element.25.wide_ref, ...), custom_call_target="tpu_custom_call" | custom-call | flops 201326592 | bytes 262144 | tf_op jit(solution)/shard_map/diag/pallas_call | solution.py:185
  45.8 7.6 %all-to-all-start.1 = ((bf16[8,4,16,128]{3,2,1,0:T(8,128)(2,1)}), bf16[8,4,16,128]{3,2,1,0:T(8,128)(2,1)S(1)}, u32[]{:S(2)}, u32[]{:S(2)}) async-start(bf16[8,4,16,128]{3,2,1,0:T(8,128)(2,1)} %diag.1), calls=%async_computation.1 | async-start | bytes 262144 | tf_op jit(solution)/shard_map/all_to_all | solution.py:191
  53.4 2.3 %density.1 = bf16[16,384,128]{2,1,0:T(8,128)(2,1)} custom-call(s32[2]{0:T(128)S(1)} %pad_add_fusion.at_ref, s32[256]{0:T(256)S(1)} %copy-done.2, bf16[16,384,128]{2,1,0:T(8,128)(2,1)S(1)} %all-to-all-done.moved_ref, bf16[4,128,128]{2,1,0:T(8,128)(2,1)S(1)} %weights.1.refs_0_, bf16[4,128,128]{2,1,0:T(8,128)(2,1)S(1)} %collective-permute-done.11.refs_1_, ...), custom_call_target="tpu_custom_call" | custom-call | flops 201326592 | bytes 3145728 | tf_op jit(solution)/shard_map/density/pallas_call | solution.py:194
  55.7 4.1 %all-to-all-done.1.got_ref = bf16[8,4,16,128]{3,2,1,0:T(8,128)(2,1)S(1)} async-done(((bf16[8,4,16,128]{3,2,1,0:T(8,128)(2,1)}), bf16[8,4,16,128]{3,2,1,0:T(8,128)(2,1)S(1)}, u32[]{:S(2)}, u32[]{:S(2)}) %all-to-all-start.1) | async-done | bytes 131104 | tf_op jit(solution)/shard_map/all_to_all | solution.py:191
  59.8 1.2 %finish.1 = bf16[16,16,128]{2,1,0:T(8,128)(2,1)} custom-call(s32[2]{0:T(128)S(1)} %pad_add_fusion.at_ref, bf16[8,4,16,128]{3,2,1,0:T(8,128)(2,1)S(1)} %all-to-all-done.1.got_ref), custom_call_target="tpu_custom_call" | custom-call | bytes 131072 | tf_op jit(solution)/shard_map/finish/pallas_call | solution.py:192
  (18 shorter events, 0.1 us)
Async XLA Ops:
  0.6 8.2 %copy-start = (bf16[16,384,128]{2,1,0:T(8,128)(2,1)S(1)}, bf16[16,384,128]{2,1,0:T(8,128)(2,1)}, u32[]{:S(2)}) copy-start(bf16[16,384,128]{2,1,0:T(8,128)(2,1)} %panel_ref.1) | copy-start | bytes 4718596
  0.6 8.2 %copy-start.2 = (s32[256]{0:T(256)S(1)}, s32[256]{0:T(256)}, u32[]{:S(2)}) copy-start(s32[256]{0:T(256)} %count_ref.5) | copy-start | bytes 3076
  0.6 45.2 %all-to-all-start = ((bf16[16,384,128]{2,1,0:T(8,128)(2,1)}), bf16[16,384,128]{2,1,0:T(8,128)(2,1)S(1)}, u32[]{:S(2)}, u32[]{:S(2)}) async-start(bf16[16,384,128]{2,1,0:T(8,128)(2,1)} %panel_ref.1), calls=%async_computation | async-start | bytes 3145728 | tf_op jit(solution)/shard_map/all_to_all | solution.py:152
  8.8 21.4 %copy-start.3 = (f32[8]{0:T(128)S(1)}, f32[8]{0:T(128)}, u32[]{:S(2)}) copy-start(f32[8]{0:T(128)} %w_ref.3) | copy-start | bytes 100
  8.9 1.0 %copy-start.1 = (bf16[1,16,128,128]{3,2,1,0:T(8,128)(2,1)S(1)}, bf16[1,16,128,128]{3,2,1,0:T(8,128)(2,1)}, u32[]{:S(2)}) copy-start(bf16[1,16,128,128]{3,2,1,0:T(8,128)(2,1)} %param.5) | copy-start | bytes 1572868
  11.1 9.0 %collective-permute-start.3 = (bf16[4,128,128]{2,1,0:T(8,128)(2,1)S(1)}, bf16[4,128,128]{2,1,0:T(8,128)(2,1)S(1)}, u32[]{:S(2)}, u32[]{:S(2)}) collective-permute-start(bf16[4,128,128]{2,1,0:T(8,128)(2,1)S(1)} %get-tuple-element.28), channel_id=1, source_target_pairs={{0,32},{16,48},{32,0},{48,16},{64,96},{80,112},{96,64},{112,80},{1... | collective-permute-start | bytes 393224 | tf_op jit(solution)/shard_map/ppermute | solution.py:150
  12.7 9.9 %collective-permute-start.4 = (bf16[4,128,128]{2,1,0:T(8,128)(2,1)S(1)}, bf16[4,128,128]{2,1,0:T(8,128)(2,1)S(1)}, u32[]{:S(2)}, u32[]{:S(2)}) collective-permute-start(bf16[4,128,128]{2,1,0:T(8,128)(2,1)S(1)} %get-tuple-element.29), channel_id=1, source_target_pairs={{0,64},{16,80},{32,96},{48,112},{64,0},{80,16},{96,32},{112,48},{1... | collective-permute-start | bytes 393224 | tf_op jit(solution)/shard_map/ppermute | solution.py:150
  15.4 10.0 %collective-permute-start.5 = (bf16[4,128,128]{2,1,0:T(8,128)(2,1)S(1)}, bf16[4,128,128]{2,1,0:T(8,128)(2,1)S(1)}, u32[]{:S(2)}, u32[]{:S(2)}) collective-permute-start(bf16[4,128,128]{2,1,0:T(8,128)(2,1)S(1)} %get-tuple-element.30), channel_id=1, source_target_pairs={{0,96},{16,112},{32,64},{48,80},{64,32},{80,48},{96,0},{112,16},{1... | collective-permute-start | bytes 393224 | tf_op jit(solution)/shard_map/ppermute | solution.py:150
  15.9 12.0 %collective-permute-start = (bf16[4,128,128]{2,1,0:T(8,128)(2,1)S(1)}, bf16[4,128,128]{2,1,0:T(8,128)(2,1)S(1)}, u32[]{:S(2)}, u32[]{:S(2)}) collective-permute-start(bf16[4,128,128]{2,1,0:T(8,128)(2,1)S(1)} %get-tuple-element.21), channel_id=1, source_target_pairs={{0,32},{16,48},{32,0},{48,16},{64,96},{80,112},{96,64},{112,80},{1... | collective-permute-start | bytes 393224 | tf_op jit(solution)/shard_map/ppermute | solution.py:150
  16.2 11.8 %collective-permute-start.1 = (bf16[4,128,128]{2,1,0:T(8,128)(2,1)S(1)}, bf16[4,128,128]{2,1,0:T(8,128)(2,1)S(1)}, u32[]{:S(2)}, u32[]{:S(2)}) collective-permute-start(bf16[4,128,128]{2,1,0:T(8,128)(2,1)S(1)} %get-tuple-element.22), channel_id=1, source_target_pairs={{0,64},{16,80},{32,96},{48,112},{64,0},{80,16},{96,32},{112,48},{1... | collective-permute-start | bytes 393224 | tf_op jit(solution)/shard_map/ppermute | solution.py:150
  20.1 10.0 %collective-permute-start.2 = (bf16[4,128,128]{2,1,0:T(8,128)(2,1)S(1)}, bf16[4,128,128]{2,1,0:T(8,128)(2,1)S(1)}, u32[]{:S(2)}, u32[]{:S(2)}) collective-permute-start(bf16[4,128,128]{2,1,0:T(8,128)(2,1)S(1)} %get-tuple-element.23), channel_id=1, source_target_pairs={{0,96},{16,112},{32,64},{48,80},{64,32},{80,48},{96,0},{112,16},{1... | collective-permute-start | bytes 393224 | tf_op jit(solution)/shard_map/ppermute | solution.py:150
  25.5 1.3 %collective-permute-start.6 = (bf16[2,128,128]{2,1,0:T(8,128)(2,1)S(1)}, bf16[2,128,128]{2,1,0:T(8,128)(2,1)S(1)}, u32[]{:S(2)}, u32[]{:S(2)}) collective-permute-start(bf16[2,128,128]{2,1,0:T(8,128)(2,1)S(1)} %get-tuple-element.32), channel_id=1, source_target_pairs={{0,1},{1,0},{2,3},{3,2},{4,5},{5,4},{6,7},{7,6},{8,9},{9,8},{10,11... | collective-permute-start | bytes 196616 | tf_op jit(solution)/shard_map/ppermute | solution.py:165
  26.8 6.4 %collective-permute-start.7 = (bf16[2,2,128,128]{3,2,1,0:T(8,128)(2,1)S(1)}, bf16[2,2,128,128]{3,2,1,0:T(8,128)(2,1)S(1)}, u32[]{:S(2)}, u32[]{:S(2)}) collective-permute-start(bf16[2,2,128,128]{3,2,1,0:T(8,128)(2,1)S(1)} %pair.1.a_ref), channel_id=1, source_target_pairs={{0,16},{16,0},{32,48},{48,32},{64,80},{80,64},{96,112},{112,96},{1... | collective-permute-start | bytes 393224 | tf_op jit(solution)/shard_map/ppermute | solution.py:150
  31.0 5.2 %collective-permute-start.10 = (bf16[4,128,128]{2,1,0:T(8,128)(2,1)S(1)}, bf16[4,128,128]{2,1,0:T(8,128)(2,1)S(1)}, u32[]{:S(2)}, u32[]{:S(2)}) collective-permute-start(bf16[4,128,128]{2,1,0:T(8,128)(2,1)S(1)} %get-tuple-element.36.a_ref), channel_id=1, source_target_pairs={{0,16},{16,0},{32,48},{48,32},{64,80},{80,64},{96,112},{112,96},{1... | collective-permute-start | bytes 393224 | tf_op jit(solution)/shard_map/ppermute | solution.py:150
  33.3 10.3 %collective-permute-start.8 = (bf16[2,128,128]{2,1,0:T(8,128)(2,1)S(1)}, bf16[2,128,128]{2,1,0:T(8,128)(2,1)S(1)}, u32[]{:S(2)}, u32[]{:S(2)}) collective-permute-start(bf16[2,128,128]{2,1,0:T(8,128)(2,1)S(1)} %get-tuple-element.33), channel_id=1, source_target_pairs={{0,0},{1,1},{2,2},{3,3},{4,4},{5,5},{6,6},{7,7},{8,8},{9,9},{10,10... | collective-permute-start | bytes 196616 | tf_op jit(solution)/shard_map/ppermute | solution.py:170
  33.9 9.6 %collective-permute-start.9 = (bf16[2,128,128]{2,1,0:T(8,128)(2,1)S(1)}, bf16[2,128,128]{2,1,0:T(8,128)(2,1)S(1)}, u32[]{:S(2)}, u32[]{:S(2)}) collective-permute-start(bf16[2,128,128]{2,1,0:T(8,128)(2,1)S(1)} %get-tuple-element.34), channel_id=1, source_target_pairs={{0,2},{1,3},{2,0},{3,1},{4,6},{5,7},{6,4},{7,5},{8,10},{9,11},{10,... | collective-permute-start | bytes 196616 | tf_op jit(solution)/shard_map/ppermute | solution.py:170
  36.2 17.2 %collective-permute-start.13 = (bf16[4,128,128]{2,1,0:T(8,128)(2,1)S(1)}, bf16[4,128,128]{2,1,0:T(8,128)(2,1)S(1)}, u32[]{:S(2)}, u32[]{:S(2)}) collective-permute-start(bf16[4,128,128]{2,1,0:T(8,128)(2,1)S(1)} %weights.1.refs_0_), channel_id=1, source_target_pairs={{0,96},{16,112},{32,64},{48,80},{64,32},{80,48},{96,0},{112,16},{1... | collective-permute-start | bytes 393224 | tf_op jit(solution)/shard_map/ppermute | solution.py:150
  42.6 10.9 %collective-permute-start.12 = (bf16[4,128,128]{2,1,0:T(8,128)(2,1)S(1)}, bf16[4,128,128]{2,1,0:T(8,128)(2,1)S(1)}, u32[]{:S(2)}, u32[]{:S(2)}) collective-permute-start(bf16[4,128,128]{2,1,0:T(8,128)(2,1)S(1)} %weights.1.refs_0_), channel_id=1, source_target_pairs={{0,64},{16,80},{32,96},{48,112},{64,0},{80,16},{96,32},{112,48},{1... | collective-permute-start | bytes 393224 | tf_op jit(solution)/shard_map/ppermute | solution.py:150
  42.6 10.9 %collective-permute-start.11 = (bf16[4,128,128]{2,1,0:T(8,128)(2,1)S(1)}, bf16[4,128,128]{2,1,0:T(8,128)(2,1)S(1)}, u32[]{:S(2)}, u32[]{:S(2)}) collective-permute-start(bf16[4,128,128]{2,1,0:T(8,128)(2,1)S(1)} %weights.1.refs_0_), channel_id=1, source_target_pairs={{0,32},{16,48},{32,0},{48,16},{64,96},{80,112},{96,64},{112,80},{1... | collective-permute-start | bytes 393224 | tf_op jit(solution)/shard_map/ppermute | solution.py:150
  45.8 14.0 %all-to-all-start.1 = ((bf16[8,4,16,128]{3,2,1,0:T(8,128)(2,1)}), bf16[8,4,16,128]{3,2,1,0:T(8,128)(2,1)S(1)}, u32[]{:S(2)}, u32[]{:S(2)}) async-start(bf16[8,4,16,128]{3,2,1,0:T(8,128)(2,1)} %diag.1), calls=%async_computation.1 | async-start | bytes 262144 | tf_op jit(solution)/shard_map/all_to_all | solution.py:191

commit v4 on v3

--- a/solution.py
+++ b/solution.py
@@ -64,45 +64,45 @@
     out_ref[...] = (a_ref[...].astype(F32) + b_ref[...].astype(F32)).astype(BF16)
 
 
-def prep_kernel(share, at_ref, w_ref, *refs):
-    *got_refs, m_ref, base_ref, wide_ref, flip_ref = refs
-    pole = at_ref[0]
+def prep_kernel(share, at_ref, w_ref, count_ref, *refs):
+    *got_refs, m_ref, base_ref, gain_ref, wide_ref, flip_ref = refs
+    pole, col = at_ref[0], at_ref[1]
     block = m_ref.shape[1]
+    owned = share * len(got_refs)
     for t in range(share):
+        count = count_ref[col * owned + (col ^ (share * (pole // 2) + t))]
+        scale = 1.0 / (jnp.full((1, block), block, F32) * count.astype(F32))
         base = jnp.zeros((block, block), F32)
         for k, got_ref in enumerate(got_refs):
             inv = got_ref[t]
-            base = base + w_ref[pole ^ (2 * k)] * inv.astype(F32)
+            w = w_ref[pole ^ (2 * k)]
+            base = base + w * inv.astype(F32)
+            gain_ref[t, :, k * block:(k + 1) * block] = w * scale
             wide_ref[t, :, k * block:(k + 1) * block] = inv
             flip_ref[t, :, k * block:(k + 1) * block] = inv.T
         base_ref[t] = base
         m_ref[t] = (-base).astype(BF16)
 
 
-def diag_kernel(share, at_ref, count_ref, w_ref, base_ref, wide_ref, flip_ref, *refs):
+def diag_kernel(share, base_ref, gain_ref, wide_ref, flip_ref, *refs):
     *g_refs, out_ref = refs
-    pole, col = at_ref[0], at_ref[1]
     block = base_ref.shape[1]
     half = wide_ref.shape[2] // block
-    owned = share * half
     chunk = out_ref.shape[2]
     for t in range(share):
-        count = count_ref[col * owned + (col ^ (share * (pole // 2) + t))]
-        scale = 1.0 / (jnp.full((block, block), block, F32) * count.astype(F32))
-        v = dot(g_refs[t // 2][t % 2], wide_ref[t])
-        v = jnp.concatenate(
-            [w_ref[pole ^ (2 * k)] * v[:, k * block:(k + 1) * block] for k in range(half)], axis=0
-        )
+        g = g_refs[t // 2][t % 2]
+        v = dot(g, wide_ref[t]) * gain_ref[t]
+        v = jnp.concatenate([v[:, k * block:(k + 1) * block] for k in range(half)], axis=0)
         hi = v.astype(BF16)
         lo = (v - hi.astype(F32)).astype(BF16)
         flip = flip_ref[t]
-        d = (base_ref[t] + (dot(flip, hi) + dot(flip, lo)) * scale).astype(BF16)
+        d = (base_ref[t] + dot(flip, hi) + dot(flip, lo)).astype(BF16)
         for p in range(out_ref.shape[0]):
             out_ref[p, t] = d[p * chunk:(p + 1) * chunk]
 
 
-def finish_kernel(share, at_ref, got_ref, out_ref):
-    col = at_ref[1]
+def finish_kernel(share, got_ref, out_ref):
+    col = lax.axis_index("col")
     for x in range(got_ref.shape[0] // 2):
         for t in range(share):
             d = got_ref[2 * x, t].astype(F32) + got_ref[2 * x + 1, t].astype(F32)
@@ -164,7 +164,10 @@
     )(*grams)
     near = lax.ppermute(give, "col", [(c, c ^ 1) for c in range(cols)])
     ghalf = call(pair_kernel, "pair", [vmem] * 2, [shape(share // 2, 2, block, block)])(keep, near)[0]
-    gfull = call(both_kernel, "gboth", [vmem] * 2, [shape(2, block, block)] * (share // 2))(ghalf, swap(ghalf, 1))
+
+    gfull = call(
+        both_kernel, "gboth", [vmem] * 2, [shape(2, block, block)] * (share // 2)
+    )(ghalf, swap(ghalf, 1))
 
     def to_owner(g, f):
         return lax.ppermute(
@@ -172,24 +175,24 @@
             [(p * cols + c, p * cols + (c ^ (share * (p // 2) + 2 * f))) for p in range(poles) for c in range(cols)],
         )
 
-    gfull = [to_owner(g, f) for f, g in enumerate(gfull)]
+    gparts = [to_owner(g, f) for f, g in enumerate(gfull)]
 
     wide = shape(share, block, half * block)
-    mhalf, base, wide, flip = call(
-        functools.partial(prep_kernel, share), "prep", [smem, smem] + [vmem] * half,
-        [shape(share, block, block), jax.ShapeDtypeStruct((share, block, block), F32), wide, wide],
-    )(at, pole_weight, *inverses)
+    mhalf, base, gain, wide, flip = call(
+        functools.partial(prep_kernel, share), "prep", [smem] * 3 + [vmem] * half,
+        [shape(share, block, block), jax.ShapeDtypeStruct((share, block, block), F32), jax.ShapeDtypeStruct((share, 1, half * block), F32), wide, wide],
+    )(at, pole_weight, row_count, *inverses)
     mfull = call(add_kernel, "weights", [vmem] * 2, [shape(share, block, block)])(mhalf, swap(mhalf, 1))[0]
     mparts = [mfull] + [swap(mfull, 2 * k) for k in range(1, half)]
 
     part = call(
         functools.partial(diag_kernel, share), "diag",
-        [smem, smem, smem, vmem, vmem, vmem] + [vmem] * (share // 2), [shape(poles, share, chunk, block)],
+        [vmem] * (4 + share // 2), [shape(poles, share, chunk, block)],
         6 * owned * block * block * block,
-    )(at, row_count, pole_weight, base, wide, flip, *gfull)[0]
+    )(base, gain, wide, flip, *gparts)[0]
     part, moved = lax.optimization_barrier((part, moved))
     part = lax.all_to_all(part, "pole", 0, 0, tiled=True)
-    diag = call(functools.partial(finish_kernel, share), "finish", [smem, vmem], [shape(owned, chunk, block)])(at, part)[0]
+    diag = call(functools.partial(finish_kernel, share), "finish", [vmem], [shape(owned, chunk, block)])(part)[0]
 
     density = call(
         functools.partial(density_kernel, poles, share), "density",

time: 61.3 us -> 60.2 us (0.982)
  Pallas kernels: 7.89 us -> 6.81 us
    pallas_call x3, Pallas kernels: 4.3 us -> 3.21 us  [the longest x1 1.74 us: shards(): call(functools.partial(diag_kernel, share), 'diag', [vmem] * (4 + share /...]
  transfers between devices with their start and end apart: 16 -> 16, of which waited for: 7 -> 7; matrix products, arithmetic and copies ran while one was open for 0% -> 0% of each run, Pallas kernels for 11% -> 10%
where the time goes in v4:
time: 60.2 us; the launch traced here: 59.9 us
  starting transfers between devices  36.8 us (61%)
  waiting for transfers between devices  14.5 us (24%)
  Pallas kernels  6.81 us (11%)
  local copies, waits for them, and re-layouts  1.06 us (2%)
  between operations  0.74 us (1%)
    ppermute x11, starting transfers between devices, swap(): return lax.ppermute(x, 'pole', [(i, i ^ k) for i in range(poles)])  19 us
    ppermute x11, waiting for transfers between devices, swap(): return lax.ppermute(x, 'pole', [(i, i ^ k) for i in range(poles)])  9.09 us
    all_to_all x1, starting transfers between devices, shards(): moved = lax.all_to_all(panel, 'col', 0, 0, tiled=True)  8.11 us
    all_to_all x1, starting transfers between devices, shards(): part = lax.all_to_all(part, 'pole', 0, 0, tiled=True)  7.58 us
    all_to_all x1, waiting for transfers between devices, shards(): part = lax.all_to_all(part, 'pole', 0, 0, tiled=True)  4.11 us
    pallas_call x1, Pallas kernels, shards(): call(functools.partial(density_kernel, poles, share), 'density', [smem, s...  2.27 us
    ppermute x2, starting transfers between devices, to_owner(): lax.ppermute(g, ('pole', 'col'), [(p * cols + c, p * cols + (c ^ share *...  1.98 us
    pallas_call x1, Pallas kernels, shards(): call(functools.partial(diag_kernel, share), 'diag', [vmem] * (4 + share /...  1.74 us
  transfers between devices with their start and end apart: 16, of which 7 were waited for; matrix products, arithmetic and copies ran while one was open for 0% of the time, Pallas kernels for 10%

profile of v4, /device:TPU:0, one launch (start us, length us, event | category | flops | bytes accessed | tf_op | source)
XLA Modules:
  0.0 59.9 jit_solution(2086550010584245571)
XLA Ops:
  0.6 8.1 %all-to-all-start = ((bf16[16,384,128]{2,1,0:T(8,128)(2,1)}), bf16[16,384,128]{2,1,0:T(8,128)(2,1)S(1)}, u32[]{:S(2)}, u32[]{:S(2)}) async-start(bf16[16,384,128]{2,1,0:T(8,128)(2,1)} %panel_ref.1), calls=%async_computation | async-start | bytes 3145728 | tf_op jit(solution)/shard_map/all_to_all | solution.py:152
  8.8 0.0 copy-start.3
  8.8 0.1 pad_add_fusion.at_ref
  8.9 1.0 %copy-done.1 = bf16[1,16,128,128]{3,2,1,0:T(8,128)(2,1)S(1)} copy-done((bf16[1,16,128,128]{3,2,1,0:T(8,128)(2,1)S(1)}, bf16[1,16,128,128]{3,2,1,0:T(8,128)(2,1)}, u32[]{:S(2)}) %copy-start.1) | copy-done | bytes 524312
  9.9 1.2 %gram.1 = (bf16[4,128,128]{2,1,0:T(8,128)(2,1)S(1)}, bf16[4,128,128]{2,1,0:T(8,128)(2,1)S(1)}, bf16[4,128,128]{2,1,0:T(8,128)(2,1)S(1)}, bf16[4,128,128]{2,1,0:T...) custom-call(s32[2]{0:T(128)S(1)} %pad_add_fusion.at_ref, ...), custom_call_target="tpu_custom_call" | custom-call | flops 201326592 | bytes 2097152 | tf_op jit(solution)/shard_map/gram/pallas_call | solution.py:154
  11.1 1.6 %collective-permute-start.3 = (bf16[4,128,128]{2,1,0:T(8,128)(2,1)S(1)}, bf16[4,128,128]{2,1,0:T(8,128)(2,1)S(1)}, u32[]{:S(2)}, u32[]{:S(2)}) collective-permute-start(bf16[4,128,128]{2,1,0:T(8,128)(2,1)S(1)} %get-tuple-element.30), channel_id=1, source_target_pairs={{0,32},{16,48},{32,0},{48,16},{64,96},{80,112},{96,64},{112,80},{1... | collective-permute-start | bytes 393224 | tf_op jit(solution)/shard_map/ppermute | solution.py:150
  12.7 2.7 %collective-permute-start.4 = (bf16[4,128,128]{2,1,0:T(8,128)(2,1)S(1)}, bf16[4,128,128]{2,1,0:T(8,128)(2,1)S(1)}, u32[]{:S(2)}, u32[]{:S(2)}) collective-permute-start(bf16[4,128,128]{2,1,0:T(8,128)(2,1)S(1)} %get-tuple-element.31), channel_id=1, source_target_pairs={{0,64},{16,80},{32,96},{48,112},{64,0},{80,16},{96,32},{112,48},{1... | collective-permute-start | bytes 393224 | tf_op jit(solution)/shard_map/ppermute | solution.py:150
  15.4 0.5 collective-permute-start.5
  15.9 0.3 collective-permute-start
  16.2 3.9 %collective-permute-start.1 = (bf16[4,128,128]{2,1,0:T(8,128)(2,1)S(1)}, bf16[4,128,128]{2,1,0:T(8,128)(2,1)S(1)}, u32[]{:S(2)}, u32[]{:S(2)}) collective-permute-start(bf16[4,128,128]{2,1,0:T(8,128)(2,1)S(1)} %get-tuple-element.23), channel_id=1, source_target_pairs={{0,64},{16,80},{32,96},{48,112},{64,0},{80,16},{96,32},{112,48},{1... | collective-permute-start | bytes 393224 | tf_op jit(solution)/shard_map/ppermute | solution.py:150
  20.1 0.0 collective-permute-done.3.refs_1_
  20.1 0.5 collective-permute-start.2
  20.6 1.9 %collective-permute-done.4.refs_2_ = bf16[4,128,128]{2,1,0:T(8,128)(2,1)S(1)} collective-permute-done((bf16[4,128,128]{2,1,0:T(8,128)(2,1)S(1)}, bf16[4,128,128]{2,1,0:T(8,128)(2,1)S(1)}, u32[]{:S(2)}, u32[]{:S(2)}) %collective-permute-start.4) | collective-permute-done | bytes 131104 | tf_op jit(solution)/shard_map/ppermute | solution.py:150
  22.5 2.9 %collective-permute-done.5.refs_3_ = bf16[4,128,128]{2,1,0:T(8,128)(2,1)S(1)} collective-permute-done((bf16[4,128,128]{2,1,0:T(8,128)(2,1)S(1)}, bf16[4,128,128]{2,1,0:T(8,128)(2,1)S(1)}, u32[]{:S(2)}, u32[]{:S(2)}) %collective-permute-start.5) | collective-permute-done | bytes 131104 | tf_op jit(solution)/shard_map/ppermute | solution.py:150
  25.4 0.1 gsum.1
  25.5 0.1 collective-permute-start.6
  25.6 1.2 %collective-permute-done.6.b_ref = bf16[2,128,128]{2,1,0:T(8,128)(2,1)S(1)} collective-permute-done((bf16[2,128,128]{2,1,0:T(8,128)(2,1)S(1)}, bf16[2,128,128]{2,1,0:T(8,128)(2,1)S(1)}, u32[]{:S(2)}, u32[]{:S(2)}) %collective-permute-start.6) | collective-permute-done | bytes 65568 | tf_op jit(solution)/shard_map/ppermute | solution.py:165
  26.8 1.1 %collective-permute-start.7 = (bf16[2,2,128,128]{3,2,1,0:T(8,128)(2,1)S(1)}, bf16[2,2,128,128]{3,2,1,0:T(8,128)(2,1)S(1)}, u32[]{:S(2)}, u32[]{:S(2)}) collective-permute-start(bf16[2,2,128,128]{3,2,1,0:T(8,128)(2,1)S(1)} %pair.1.a_ref), channel_id=1, source_target_pairs={{0,16},{16,0},{32,48},{48,32},{64,80},{80,64},{96,112},{112,96},{1... | collective-permute-start | bytes 393224 | tf_op jit(solution)/shard_map/ppermute | solution.py:150
  27.9 2.2 %collective-permute-done.2.refs_3_ = bf16[4,128,128]{2,1,0:T(8,128)(2,1)S(1)} collective-permute-done((bf16[4,128,128]{2,1,0:T(8,128)(2,1)S(1)}, bf16[4,128,128]{2,1,0:T(8,128)(2,1)S(1)}, u32[]{:S(2)}, u32[]{:S(2)}) %collective-permute-start.2) | collective-permute-done | bytes 131104 | tf_op jit(solution)/shard_map/ppermute | solution.py:150
  30.1 0.8 %prep.1 = (bf16[4,128,128]{2,1,0:T(8,128)(2,1)S(1)}, f32[4,128,128]{2,1,0:T(8,128)S(1)}, f32[4,1,512]{2,1,0:T(1,128)S(1)}, bf16[4,128,512]{2,1,0:T(8,128)(2,1)S(1)}, bf16[4,128,512]{2,1,0:T(8,128)(2,1)S(1)}) custom-call(s32[2]{0:T(128)S(1)} %pad_add_fusion.at_ref, f32[8]{0:T(128)S(1)} %copy-done.3, s32[256]{0:T(256)S(1)} %copy-done.2, ...), custom_call_target="tpu_custom_call" | custom-call | bytes 2629632 | tf_op jit(solution)/shard_map/prep/pallas_call | solution.py:181
  31.0 1.1 %collective-permute-start.10 = (bf16[4,128,128]{2,1,0:T(8,128)(2,1)S(1)}, bf16[4,128,128]{2,1,0:T(8,128)(2,1)S(1)}, u32[]{:S(2)}, u32[]{:S(2)}) collective-permute-start(bf16[4,128,128]{2,1,0:T(8,128)(2,1)S(1)} %get-tuple-element.38.a_ref), channel_id=1, source_target_pairs={{0,16},{16,0},{32,48},{48,32},{64,80},{80,64},{96,112},{112,96},{1... | collective-permute-start | bytes 393224 | tf_op jit(solution)/shard_map/ppermute | solution.py:150
  32.1 1.2 %collective-permute-done.7.b_ref = bf16[2,2,128,128]{3,2,1,0:T(8,128)(2,1)S(1)} collective-permute-done((bf16[2,2,128,128]{3,2,1,0:T(8,128)(2,1)S(1)}, bf16[2,2,128,128]{3,2,1,0:T(8,128)(2,1)S(1)}, u32[]{:S(2)}, u32[]{:S(2)}) %collective-permute-start.7) | collective-permute-done | bytes 131104 | tf_op jit(solution)/shard_map/ppermute | solution.py:150
  33.3 0.7 %collective-permute-start.8 = (bf16[2,128,128]{2,1,0:T(8,128)(2,1)S(1)}, bf16[2,128,128]{2,1,0:T(8,128)(2,1)S(1)}, u32[]{:S(2)}, u32[]{:S(2)}) collective-permute-start(bf16[2,128,128]{2,1,0:T(8,128)(2,1)S(1)} %get-tuple-element.35), channel_id=1, source_target_pairs={{0,0},{1,1},{2,2},{3,3},{4,4},{5,5},{6,6},{7,7},{8,8},{9,9},{10,10... | collective-permute-start | bytes 196616 | tf_op jit(solution)/shard_map/ppermute | solution.py:173
  33.9 1.3 %collective-permute-start.9 = (bf16[2,128,128]{2,1,0:T(8,128)(2,1)S(1)}, bf16[2,128,128]{2,1,0:T(8,128)(2,1)S(1)}, u32[]{:S(2)}, u32[]{:S(2)}) collective-permute-start(bf16[2,128,128]{2,1,0:T(8,128)(2,1)S(1)} %get-tuple-element.36), channel_id=1, source_target_pairs={{0,2},{1,3},{2,0},{3,1},{4,6},{5,7},{6,4},{7,5},{8,10},{9,11},{10,... | collective-permute-start | bytes 196616 | tf_op jit(solution)/shard_map/ppermute | solution.py:173
  35.3 0.9 %collective-permute-done.10.b_ref = bf16[4,128,128]{2,1,0:T(8,128)(2,1)S(1)} collective-permute-done((bf16[4,128,128]{2,1,0:T(8,128)(2,1)S(1)}, bf16[4,128,128]{2,1,0:T(8,128)(2,1)S(1)}, u32[]{:S(2)}, u32[]{:S(2)}) %collective-permute-start.10) | collective-permute-done | bytes 131104 | tf_op jit(solution)/shard_map/ppermute | solution.py:150
  36.2 6.4 %collective-permute-start.13 = (bf16[4,128,128]{2,1,0:T(8,128)(2,1)S(1)}, bf16[4,128,128]{2,1,0:T(8,128)(2,1)S(1)}, u32[]{:S(2)}, u32[]{:S(2)}) collective-permute-start(bf16[4,128,128]{2,1,0:T(8,128)(2,1)S(1)} %weights.1.refs_0_), channel_id=1, source_target_pairs={{0,96},{16,112},{32,64},{48,80},{64,32},{80,48},{96,0},{112,16},{1... | collective-permute-start | bytes 393224 | tf_op jit(solution)/shard_map/ppermute | solution.py:150
  42.6 0.9 %collective-permute-start.11 = (bf16[4,128,128]{2,1,0:T(8,128)(2,1)S(1)}, bf16[4,128,128]{2,1,0:T(8,128)(2,1)S(1)}, u32[]{:S(2)}, u32[]{:S(2)}) collective-permute-start(bf16[4,128,128]{2,1,0:T(8,128)(2,1)S(1)} %weights.1.refs_0_), channel_id=1, source_target_pairs={{0,32},{16,48},{32,0},{48,16},{64,96},{80,112},{96,64},{112,80},{1... | collective-permute-start | bytes 393224 | tf_op jit(solution)/shard_map/ppermute | solution.py:150
  43.5 1.7 %diag.1 = bf16[8,4,16,128]{3,2,1,0:T(8,128)(2,1)} custom-call(f32[4,128,128]{2,1,0:T(8,128)S(1)} %get-tuple-element.25.base_ref, f32[4,1,512]{2,1,0:T(1,128)S(1)} %get-tuple-element.26.gain_ref, bf16[4,128,512]{2,1,0:T(8,128)(2,1)S(1)} %get-tuple-element.27.wide_ref, bf16[4,128,512]{2,1,0:T(8,128)(2,1)S(1)} %get-tuple-element.28.flip_ref, ...), custom_call_target="tpu_custom_call" | custom-call | flops 201326592 | bytes 262144 | tf_op jit(solution)/shard_map/diag/pallas_call | solution.py:188
  45.3 7.6 %all-to-all-start.1 = ((bf16[8,4,16,128]{3,2,1,0:T(8,128)(2,1)}), bf16[8,4,16,128]{3,2,1,0:T(8,128)(2,1)S(1)}, u32[]{:S(2)}, u32[]{:S(2)}) async-start(bf16[8,4,16,128]{3,2,1,0:T(8,128)(2,1)} %diag.1), calls=%async_computation.1 | async-start | bytes 262144 | tf_op jit(solution)/shard_map/all_to_all | solution.py:194
  52.9 2.3 %density.1 = bf16[16,384,128]{2,1,0:T(8,128)(2,1)} custom-call(s32[2]{0:T(128)S(1)} %pad_add_fusion.at_ref, s32[256]{0:T(256)S(1)} %copy-done.2, bf16[16,384,128]{2,1,0:T(8,128)(2,1)S(1)} %all-to-all-done.moved_ref, bf16[4,128,128]{2,1,0:T(8,128)(2,1)S(1)} %weights.1.refs_0_, bf16[4,128,128]{2,1,0:T(8,128)(2,1)S(1)} %collective-permute-done.11.refs_1_, ...), custom_call_target="tpu_custom_call" | custom-call | flops 201326592 | bytes 3145728 | tf_op jit(solution)/shard_map/density/pallas_call | solution.py:197
  55.1 4.1 %all-to-all-done.1.got_ref = bf16[8,4,16,128]{3,2,1,0:T(8,128)(2,1)S(1)} async-done(((bf16[8,4,16,128]{3,2,1,0:T(8,128)(2,1)}), bf16[8,4,16,128]{3,2,1,0:T(8,128)(2,1)S(1)}, u32[]{:S(2)}, u32[]{:S(2)}) %all-to-all-start.1) | async-done | bytes 131104 | tf_op jit(solution)/shard_map/all_to_all | solution.py:194
  59.3 0.6 %finish.1 = bf16[16,16,128]{2,1,0:T(8,128)(2,1)} custom-call(bf16[8,4,16,128]{3,2,1,0:T(8,128)(2,1)S(1)} %all-to-all-done.1.got_ref), custom_call_target="tpu_custom_call" | custom-call | bytes 131072 | tf_op jit(solution)/shard_map/finish/pallas_call | solution.py:195
  (18 shorter events, 0.1 us)
Async XLA Ops:
  0.6 8.2 %copy-start = (bf16[16,384,128]{2,1,0:T(8,128)(2,1)S(1)}, bf16[16,384,128]{2,1,0:T(8,128)(2,1)}, u32[]{:S(2)}) copy-start(bf16[16,384,128]{2,1,0:T(8,128)(2,1)} %panel_ref.1) | copy-start | bytes 4718596
  0.6 8.2 %copy-start.2 = (s32[256]{0:T(256)S(1)}, s32[256]{0:T(256)}, u32[]{:S(2)}) copy-start(s32[256]{0:T(256)} %count_ref.5) | copy-start | bytes 3076
  0.6 44.6 %all-to-all-start = ((bf16[16,384,128]{2,1,0:T(8,128)(2,1)}), bf16[16,384,128]{2,1,0:T(8,128)(2,1)S(1)}, u32[]{:S(2)}, u32[]{:S(2)}) async-start(bf16[16,384,128]{2,1,0:T(8,128)(2,1)} %panel_ref.1), calls=%async_computation | async-start | bytes 3145728 | tf_op jit(solution)/shard_map/all_to_all | solution.py:152
  8.8 21.4 %copy-start.3 = (f32[8]{0:T(128)S(1)}, f32[8]{0:T(128)}, u32[]{:S(2)}) copy-start(f32[8]{0:T(128)} %w_ref.1) | copy-start | bytes 100
  8.9 1.0 %copy-start.1 = (bf16[1,16,128,128]{3,2,1,0:T(8,128)(2,1)S(1)}, bf16[1,16,128,128]{3,2,1,0:T(8,128)(2,1)}, u32[]{:S(2)}) copy-start(bf16[1,16,128,128]{3,2,1,0:T(8,128)(2,1)} %param.5) | copy-start | bytes 1572868
  11.1 9.0 %collective-permute-start.3 = (bf16[4,128,128]{2,1,0:T(8,128)(2,1)S(1)}, bf16[4,128,128]{2,1,0:T(8,128)(2,1)S(1)}, u32[]{:S(2)}, u32[]{:S(2)}) collective-permute-start(bf16[4,128,128]{2,1,0:T(8,128)(2,1)S(1)} %get-tuple-element.30), channel_id=1, source_target_pairs={{0,32},{16,48},{32,0},{48,16},{64,96},{80,112},{96,64},{112,80},{1... | collective-permute-start | bytes 393224 | tf_op jit(solution)/shard_map/ppermute | solution.py:150
  12.7 9.9 %collective-permute-start.4 = (bf16[4,128,128]{2,1,0:T(8,128)(2,1)S(1)}, bf16[4,128,128]{2,1,0:T(8,128)(2,1)S(1)}, u32[]{:S(2)}, u32[]{:S(2)}) collective-permute-start(bf16[4,128,128]{2,1,0:T(8,128)(2,1)S(1)} %get-tuple-element.31), channel_id=1, source_target_pairs={{0,64},{16,80},{32,96},{48,112},{64,0},{80,16},{96,32},{112,48},{1... | collective-permute-start | bytes 393224 | tf_op jit(solution)/shard_map/ppermute | solution.py:150
  15.4 10.0 %collective-permute-start.5 = (bf16[4,128,128]{2,1,0:T(8,128)(2,1)S(1)}, bf16[4,128,128]{2,1,0:T(8,128)(2,1)S(1)}, u32[]{:S(2)}, u32[]{:S(2)}) collective-permute-start(bf16[4,128,128]{2,1,0:T(8,128)(2,1)S(1)} %get-tuple-element.32), channel_id=1, source_target_pairs={{0,96},{16,112},{32,64},{48,80},{64,32},{80,48},{96,0},{112,16},{1... | collective-permute-start | bytes 393224 | tf_op jit(solution)/shard_map/ppermute | solution.py:150
  15.9 12.0 %collective-permute-start = (bf16[4,128,128]{2,1,0:T(8,128)(2,1)S(1)}, bf16[4,128,128]{2,1,0:T(8,128)(2,1)S(1)}, u32[]{:S(2)}, u32[]{:S(2)}) collective-permute-start(bf16[4,128,128]{2,1,0:T(8,128)(2,1)S(1)} %get-tuple-element.22), channel_id=1, source_target_pairs={{0,32},{16,48},{32,0},{48,16},{64,96},{80,112},{96,64},{112,80},{1... | collective-permute-start | bytes 393224 | tf_op jit(solution)/shard_map/ppermute | solution.py:150
  16.2 11.8 %collective-permute-start.1 = (bf16[4,128,128]{2,1,0:T(8,128)(2,1)S(1)}, bf16[4,128,128]{2,1,0:T(8,128)(2,1)S(1)}, u32[]{:S(2)}, u32[]{:S(2)}) collective-permute-start(bf16[4,128,128]{2,1,0:T(8,128)(2,1)S(1)} %get-tuple-element.23), channel_id=1, source_target_pairs={{0,64},{16,80},{32,96},{48,112},{64,0},{80,16},{96,32},{112,48},{1... | collective-permute-start | bytes 393224 | tf_op jit(solution)/shard_map/ppermute | solution.py:150
  20.1 10.0 %collective-permute-start.2 = (bf16[4,128,128]{2,1,0:T(8,128)(2,1)S(1)}, bf16[4,128,128]{2,1,0:T(8,128)(2,1)S(1)}, u32[]{:S(2)}, u32[]{:S(2)}) collective-permute-start(bf16[4,128,128]{2,1,0:T(8,128)(2,1)S(1)} %get-tuple-element.24), channel_id=1, source_target_pairs={{0,96},{16,112},{32,64},{48,80},{64,32},{80,48},{96,0},{112,16},{1... | collective-permute-start | bytes 393224 | tf_op jit(solution)/shard_map/ppermute | solution.py:150
  25.5 1.3 %collective-permute-start.6 = (bf16[2,128,128]{2,1,0:T(8,128)(2,1)S(1)}, bf16[2,128,128]{2,1,0:T(8,128)(2,1)S(1)}, u32[]{:S(2)}, u32[]{:S(2)}) collective-permute-start(bf16[2,128,128]{2,1,0:T(8,128)(2,1)S(1)} %get-tuple-element.34), channel_id=1, source_target_pairs={{0,1},{1,0},{2,3},{3,2},{4,5},{5,4},{6,7},{7,6},{8,9},{9,8},{10,11... | collective-permute-start | bytes 196616 | tf_op jit(solution)/shard_map/ppermute | solution.py:165
  26.8 6.4 %collective-permute-start.7 = (bf16[2,2,128,128]{3,2,1,0:T(8,128)(2,1)S(1)}, bf16[2,2,128,128]{3,2,1,0:T(8,128)(2,1)S(1)}, u32[]{:S(2)}, u32[]{:S(2)}) collective-permute-start(bf16[2,2,128,128]{3,2,1,0:T(8,128)(2,1)S(1)} %pair.1.a_ref), channel_id=1, source_target_pairs={{0,16},{16,0},{32,48},{48,32},{64,80},{80,64},{96,112},{112,96},{1... | collective-permute-start | bytes 393224 | tf_op jit(solution)/shard_map/ppermute | solution.py:150
  31.0 5.2 %collective-permute-start.10 = (bf16[4,128,128]{2,1,0:T(8,128)(2,1)S(1)}, bf16[4,128,128]{2,1,0:T(8,128)(2,1)S(1)}, u32[]{:S(2)}, u32[]{:S(2)}) collective-permute-start(bf16[4,128,128]{2,1,0:T(8,128)(2,1)S(1)} %get-tuple-element.38.a_ref), channel_id=1, source_target_pairs={{0,16},{16,0},{32,48},{48,32},{64,80},{80,64},{96,112},{112,96},{1... | collective-permute-start | bytes 393224 | tf_op jit(solution)/shard_map/ppermute | solution.py:150
  33.3 10.3 %collective-permute-start.8 = (bf16[2,128,128]{2,1,0:T(8,128)(2,1)S(1)}, bf16[2,128,128]{2,1,0:T(8,128)(2,1)S(1)}, u32[]{:S(2)}, u32[]{:S(2)}) collective-permute-start(bf16[2,128,128]{2,1,0:T(8,128)(2,1)S(1)} %get-tuple-element.35), channel_id=1, source_target_pairs={{0,0},{1,1},{2,2},{3,3},{4,4},{5,5},{6,6},{7,7},{8,8},{9,9},{10,10... | collective-permute-start | bytes 196616 | tf_op jit(solution)/shard_map/ppermute | solution.py:173
  33.9 9.6 %collective-permute-start.9 = (bf16[2,128,128]{2,1,0:T(8,128)(2,1)S(1)}, bf16[2,128,128]{2,1,0:T(8,128)(2,1)S(1)}, u32[]{:S(2)}, u32[]{:S(2)}) collective-permute-start(bf16[2,128,128]{2,1,0:T(8,128)(2,1)S(1)} %get-tuple-element.36), channel_id=1, source_target_pairs={{0,2},{1,3},{2,0},{3,1},{4,6},{5,7},{6,4},{7,5},{8,10},{9,11},{10,... | collective-permute-start | bytes 196616 | tf_op jit(solution)/shard_map/ppermute | solution.py:173
  36.2 16.7 %collective-permute-start.13 = (bf16[4,128,128]{2,1,0:T(8,128)(2,1)S(1)}, bf16[4,128,128]{2,1,0:T(8,128)(2,1)S(1)}, u32[]{:S(2)}, u32[]{:S(2)}) collective-permute-start(bf16[4,128,128]{2,1,0:T(8,128)(2,1)S(1)} %weights.1.refs_0_), channel_id=1, source_target_pairs={{0,96},{16,112},{32,64},{48,80},{64,32},{80,48},{96,0},{112,16},{1... | collective-permute-start | bytes 393224 | tf_op jit(solution)/shard_map/ppermute | solution.py:150
  42.6 10.3 %collective-permute-start.12 = (bf16[4,128,128]{2,1,0:T(8,128)(2,1)S(1)}, bf16[4,128,128]{2,1,0:T(8,128)(2,1)S(1)}, u32[]{:S(2)}, u32[]{:S(2)}) collective-permute-start(bf16[4,128,128]{2,1,0:T(8,128)(2,1)S(1)} %weights.1.refs_0_), channel_id=1, source_target_pairs={{0,64},{16,80},{32,96},{48,112},{64,0},{80,16},{96,32},{112,48},{1... | collective-permute-start | bytes 393224 | tf_op jit(solution)/shard_map/ppermute | solution.py:150
  42.6 10.3 %collective-permute-start.11 = (bf16[4,128,128]{2,1,0:T(8,128)(2,1)S(1)}, bf16[4,128,128]{2,1,0:T(8,128)(2,1)S(1)}, u32[]{:S(2)}, u32[]{:S(2)}) collective-permute-start(bf16[4,128,128]{2,1,0:T(8,128)(2,1)S(1)} %weights.1.refs_0_), channel_id=1, source_target_pairs={{0,32},{16,48},{32,0},{48,16},{64,96},{80,112},{96,64},{112,80},{1... | collective-permute-start | bytes 393224 | tf_op jit(solution)/shard_map/ppermute | solution.py:150
  45.3 14.0 %all-to-all-start.1 = ((bf16[8,4,16,128]{3,2,1,0:T(8,128)(2,1)}), bf16[8,4,16,128]{3,2,1,0:T(8,128)(2,1)S(1)}, u32[]{:S(2)}, u32[]{:S(2)}) async-start(bf16[8,4,16,128]{3,2,1,0:T(8,128)(2,1)} %diag.1), calls=%async_computation.1 | async-start | bytes 262144 | tf_op jit(solution)/shard_map/all_to_all | solution.py:194

commit v5 on v4

--- a/solution.py
+++ b/solution.py
@@ -50,14 +50,15 @@
         (give_ref if t % 2 else keep_ref)[t // 2] = g
 
 
-def pair_kernel(a_ref, b_ref, out_ref):
-    out_ref[:, 0] = a_ref[...]
-    out_ref[:, 1] = b_ref[...]
-
-
-def both_kernel(a_ref, b_ref, *out_refs):
-    for t, out_ref in enumerate(out_refs):
-        out_ref[...] = (a_ref[t].astype(F32) + b_ref[t].astype(F32)).astype(BF16)
+def pair_kernel(a_ref, b_ref, *out_refs):
+    for f, out_ref in enumerate(out_refs):
+        out_ref[0] = a_ref[f]
+        out_ref[1] = b_ref[f]
+
+
+def gown_kernel(a0_ref, a1_ref, b0_ref, b1_ref, out_ref):
+    for f, (x_ref, y_ref) in enumerate(((a0_ref, a1_ref), (b0_ref, b1_ref))):
+        out_ref[f] = (x_ref[...].astype(F32) + y_ref[...].astype(F32)).astype(BF16)
 
 
 def add_kernel(a_ref, b_ref, out_ref):
@@ -85,12 +86,12 @@
 
 
 def diag_kernel(share, base_ref, gain_ref, wide_ref, flip_ref, *refs):
-    *g_refs, out_ref = refs
+    g_ref, out_ref = refs
     block = base_ref.shape[1]
     half = wide_ref.shape[2] // block
     chunk = out_ref.shape[2]
     for t in range(share):
-        g = g_refs[t // 2][t % 2]
+        g = g_ref[t // 2, t % 2]
         v = dot(g, wide_ref[t]) * gain_ref[t]
         v = jnp.concatenate([v[:, k * block:(k + 1) * block] for k in range(half)], axis=0)
         hi = v.astype(BF16)
@@ -163,19 +164,17 @@
         functools.partial(gsum_kernel, share), "gsum", [vmem] * half, [shape(share // 2, block, block)] * 2
     )(*grams)
     near = lax.ppermute(give, "col", [(c, c ^ 1) for c in range(cols)])
-    ghalf = call(pair_kernel, "pair", [vmem] * 2, [shape(share // 2, 2, block, block)])(keep, near)[0]
-
-    gfull = call(
-        both_kernel, "gboth", [vmem] * 2, [shape(2, block, block)] * (share // 2)
-    )(ghalf, swap(ghalf, 1))
-
-    def to_owner(g, f):
-        return lax.ppermute(
-            g, ("pole", "col"),
-            [(p * cols + c, p * cols + (c ^ (share * (p // 2) + 2 * f))) for p in range(poles) for c in range(cols)],
-        )
-
-    gparts = [to_owner(g, f) for f, g in enumerate(gfull)]
+    here, side = call(pair_kernel, "pair", [vmem] * 2, [shape(2, block, block)] * 2)(keep, near)
+
+    def shift(x, z, flip):
+        pairs = [(p * cols + c, (p ^ z) * cols + (c ^ flip(p))) for p in range(poles) for c in range(cols)]
+        return lax.ppermute(x, ("pole", "col"), pairs)
+
+    line = lambda p: 2
+    gfull = call(gown_kernel, "gown", [vmem] * 4, [shape(2, 2, block, block)])(
+        here, swap(here, 1), shift(side, 0, line), shift(side, 1, line)
+    )[0]
+    gfull = shift(gfull, 0, lambda p: share * (p // 2))
 
     wide = shape(share, block, half * block)
     mhalf, base, gain, wide, flip = call(
@@ -187,9 +186,9 @@
 
     part = call(
         functools.partial(diag_kernel, share), "diag",
-        [vmem] * (4 + share // 2), [shape(poles, share, chunk, block)],
+        [vmem] * 5, [shape(poles, share, chunk, block)],
         6 * owned * block * block * block,
-    )(base, gain, wide, flip, *gparts)[0]
+    )(base, gain, wide, flip, gfull)[0]
     part, moved = lax.optimization_barrier((part, moved))
     part = lax.all_to_all(part, "pole", 0, 0, tiled=True)
     diag = call(functools.partial(finish_kernel, share), "finish", [vmem], [shape(owned, chunk, block)])(part)[0]

time: 60.2 us -> 57.9 us (0.962)
  starting transfers between devices: 36.8 us -> 35.2 us
  waiting for transfers between devices: 14.5 us -> 13.5 us
    all_to_all x1, starting transfers between devices: 7.58 us -> 4.87 us  [shards(): part = lax.all_to_all(part, 'pole', 0, 0, tiled=True)]
    ppermute x11, waiting for transfers between devices: 9.09 us -> 6.68 us  [swap(): return lax.ppermute(x, 'pole', [(i, i ^ k) for i in range(poles)])]
    ppermute x2 -> x3, waiting for transfers between devices: 0.01 us -> 1.42 us  [shift(): return lax.ppermute(x, ('pole', 'col'), pairs)]
    ppermute x2 -> x3, starting transfers between devices: 1.98 us -> 3.14 us  [shift(): return lax.ppermute(x, ('pole', 'col'), pairs)]
  transfers between devices with their start and end apart: 16 -> 17, of which waited for: 7 -> 7; matrix products, arithmetic and copies ran while one was open for 0% -> 0% of each run, Pallas kernels for 10% -> 11%
where the time goes in v5:
time: 57.9 us; the launch traced here: 57.4 us
  starting transfers between devices  35.2 us (61%)
  waiting for transfers between devices  13.5 us (23%)
  Pallas kernels  6.82 us (12%)
  local copies, waits for them, and re-layouts  1.06 us (2%)
  between operations  0.74 us (1%)
    ppermute x11, starting transfers between devices, swap(): return lax.ppermute(x, 'pole', [(i, i ^ k) for i in range(poles)])  19 us
    all_to_all x1, starting transfers between devices, shards(): moved = lax.all_to_all(panel, 'col', 0, 0, tiled=True)  8.11 us
    ppermute x11, waiting for transfers between devices, swap(): return lax.ppermute(x, 'pole', [(i, i ^ k) for i in range(poles)])  6.68 us
    all_to_all x1, starting transfers between devices, shards(): part = lax.all_to_all(part, 'pole', 0, 0, tiled=True)  4.87 us
    all_to_all x1, waiting for transfers between devices, shards(): part = lax.all_to_all(part, 'pole', 0, 0, tiled=True)  4.11 us
    ppermute x3, starting transfers between devices, shift(): return lax.ppermute(x, ('pole', 'col'), pairs)  3.14 us
    pallas_call x1, Pallas kernels, shards(): call(functools.partial(density_kernel, poles, share), 'density', [smem, s...  2.27 us
    pallas_call x1, Pallas kernels, shards(): call(functools.partial(diag_kernel, share), 'diag', [vmem] * 5, [shape(po...  1.75 us
  transfers between devices with their start and end apart: 17, of which 7 were waited for; matrix products, arithmetic and copies ran while one was open for 0% of the time, Pallas kernels for 11%

profile of v5, /device:TPU:0, one launch (start us, length us, event | category | flops | bytes accessed | tf_op | source)
XLA Modules:
  0.0 57.4 jit_solution(8837493864195885425)
XLA Ops:
  0.6 8.1 %all-to-all-start = ((bf16[16,384,128]{2,1,0:T(8,128)(2,1)}), bf16[16,384,128]{2,1,0:T(8,128)(2,1)S(1)}, u32[]{:S(2)}, u32[]{:S(2)}) async-start(bf16[16,384,128]{2,1,0:T(8,128)(2,1)} %panel_ref.1), calls=%async_computation | async-start | bytes 3145728 | tf_op jit(solution)/shard_map/all_to_all | solution.py:153
  8.8 0.0 copy-start.3
  8.8 0.1 pad_add_fusion.at_ref
  8.9 1.0 %copy-done.1 = bf16[1,16,128,128]{3,2,1,0:T(8,128)(2,1)S(1)} copy-done((bf16[1,16,128,128]{3,2,1,0:T(8,128)(2,1)S(1)}, bf16[1,16,128,128]{3,2,1,0:T(8,128)(2,1)}, u32[]{:S(2)}) %copy-start.1) | copy-done | bytes 524312
  9.9 1.2 %gram.1 = (bf16[4,128,128]{2,1,0:T(8,128)(2,1)S(1)}, bf16[4,128,128]{2,1,0:T(8,128)(2,1)S(1)}, bf16[4,128,128]{2,1,0:T(8,128)(2,1)S(1)}, bf16[4,128,128]{2,1,0:T...) custom-call(s32[2]{0:T(128)S(1)} %pad_add_fusion.at_ref, ...), custom_call_target="tpu_custom_call" | custom-call | flops 201326592 | bytes 2097152 | tf_op jit(solution)/shard_map/gram/pallas_call | solution.py:155
  11.1 1.6 %collective-permute-start.3 = (bf16[4,128,128]{2,1,0:T(8,128)(2,1)S(1)}, bf16[4,128,128]{2,1,0:T(8,128)(2,1)S(1)}, u32[]{:S(2)}, u32[]{:S(2)}) collective-permute-start(bf16[4,128,128]{2,1,0:T(8,128)(2,1)S(1)} %get-tuple-element.30), channel_id=1, source_target_pairs={{0,32},{16,48},{32,0},{48,16},{64,96},{80,112},{96,64},{112,80},{1... | collective-permute-start | bytes 393224 | tf_op jit(solution)/shard_map/ppermute | solution.py:151
  12.7 2.7 %collective-permute-start.4 = (bf16[4,128,128]{2,1,0:T(8,128)(2,1)S(1)}, bf16[4,128,128]{2,1,0:T(8,128)(2,1)S(1)}, u32[]{:S(2)}, u32[]{:S(2)}) collective-permute-start(bf16[4,128,128]{2,1,0:T(8,128)(2,1)S(1)} %get-tuple-element.31), channel_id=1, source_target_pairs={{0,64},{16,80},{32,96},{48,112},{64,0},{80,16},{96,32},{112,48},{1... | collective-permute-start | bytes 393224 | tf_op jit(solution)/shard_map/ppermute | solution.py:151
  15.4 0.5 collective-permute-start.5
  15.9 0.3 collective-permute-start
  16.2 3.9 %collective-permute-start.1 = (bf16[4,128,128]{2,1,0:T(8,128)(2,1)S(1)}, bf16[4,128,128]{2,1,0:T(8,128)(2,1)S(1)}, u32[]{:S(2)}, u32[]{:S(2)}) collective-permute-start(bf16[4,128,128]{2,1,0:T(8,128)(2,1)S(1)} %get-tuple-element.23), channel_id=1, source_target_pairs={{0,64},{16,80},{32,96},{48,112},{64,0},{80,16},{96,32},{112,48},{1... | collective-permute-start | bytes 393224 | tf_op jit(solution)/shard_map/ppermute | solution.py:151
  20.1 0.5 collective-permute-start.2
  20.6 1.9 %collective-permute-done.4.refs_2_ = bf16[4,128,128]{2,1,0:T(8,128)(2,1)S(1)} collective-permute-done((bf16[4,128,128]{2,1,0:T(8,128)(2,1)S(1)}, bf16[4,128,128]{2,1,0:T(8,128)(2,1)S(1)}, u32[]{:S(2)}, u32[]{:S(2)}) %collective-permute-start.4) | collective-permute-done | bytes 131104 | tf_op jit(solution)/shard_map/ppermute | solution.py:151
  22.5 2.9 %collective-permute-done.5.refs_3_ = bf16[4,128,128]{2,1,0:T(8,128)(2,1)S(1)} collective-permute-done((bf16[4,128,128]{2,1,0:T(8,128)(2,1)S(1)}, bf16[4,128,128]{2,1,0:T(8,128)(2,1)S(1)}, u32[]{:S(2)}, u32[]{:S(2)}) %collective-permute-start.5) | collective-permute-done | bytes 131104 | tf_op jit(solution)/shard_map/ppermute | solution.py:151
  25.4 0.1 gsum.1
  25.5 0.1 collective-permute-start.6
  25.6 1.2 %collective-permute-done.6.b_ref = bf16[2,128,128]{2,1,0:T(8,128)(2,1)S(1)} collective-permute-done((bf16[2,128,128]{2,1,0:T(8,128)(2,1)S(1)}, bf16[2,128,128]{2,1,0:T(8,128)(2,1)S(1)}, u32[]{:S(2)}, u32[]{:S(2)}) %collective-permute-start.6) | collective-permute-done | bytes 65568 | tf_op jit(solution)/shard_map/ppermute | solution.py:166
  26.8 1.1 %collective-permute-start.7 = (bf16[2,128,128]{2,1,0:T(8,128)(2,1)S(1)}, bf16[2,128,128]{2,1,0:T(8,128)(2,1)S(1)}, u32[]{:S(2)}, u32[]{:S(2)}) collective-permute-start(bf16[2,128,128]{2,1,0:T(8,128)(2,1)S(1)} %get-tuple-element.35.a0_ref), channel_id=1, source_target_pairs={{0,16},{16,0},{32,48},{48,32},{64,80},{80,64},{96,112},{112,96},{1... | collective-permute-start | bytes 196616 | tf_op jit(solution)/shard_map/ppermute | solution.py:151
  27.9 2.4 %collective-permute-start.9 = (bf16[2,128,128]{2,1,0:T(8,128)(2,1)S(1)}, bf16[2,128,128]{2,1,0:T(8,128)(2,1)S(1)}, u32[]{:S(2)}, u32[]{:S(2)}) collective-permute-start(bf16[2,128,128]{2,1,0:T(8,128)(2,1)S(1)} %get-tuple-element.36), channel_id=1, source_target_pairs={{0,18},{1,19},{2,16},{3,17},{4,22},{5,23},{6,20},{7,21},{8,26},{9,... | collective-permute-start | bytes 196616 | tf_op jit(solution)/shard_map/ppermute | solution.py:171
  30.4 0.0 collective-permute-start.8
  30.4 0.8 %prep.1 = (bf16[4,128,128]{2,1,0:T(8,128)(2,1)S(1)}, f32[4,128,128]{2,1,0:T(8,128)S(1)}, f32[4,1,512]{2,1,0:T(1,128)S(1)}, bf16[4,128,512]{2,1,0:T(8,128)(2,1)S(1)}, bf16[4,128,512]{2,1,0:T(8,128)(2,1)S(1)}) custom-call(s32[2]{0:T(128)S(1)} %pad_add_fusion.at_ref, f32[8]{0:T(128)S(1)} %copy-done.3, s32[256]{0:T(256)S(1)} %copy-done.2, ...), custom_call_target="tpu_custom_call" | custom-call | bytes 2629632 | tf_op jit(solution)/shard_map/prep/pallas_call | solution.py:180
  31.2 1.1 %collective-permute-start.11 = (bf16[4,128,128]{2,1,0:T(8,128)(2,1)S(1)}, bf16[4,128,128]{2,1,0:T(8,128)(2,1)S(1)}, u32[]{:S(2)}, u32[]{:S(2)}) collective-permute-start(bf16[4,128,128]{2,1,0:T(8,128)(2,1)S(1)} %get-tuple-element.38.a_ref), channel_id=1, source_target_pairs={{0,16},{16,0},{32,48},{48,32},{64,80},{80,64},{96,112},{112,96},{1... | collective-permute-start | bytes 393224 | tf_op jit(solution)/shard_map/ppermute | solution.py:151
  32.3 0.9 %collective-permute-done.7.a1_ref = bf16[2,128,128]{2,1,0:T(8,128)(2,1)S(1)} collective-permute-done((bf16[2,128,128]{2,1,0:T(8,128)(2,1)S(1)}, bf16[2,128,128]{2,1,0:T(8,128)(2,1)S(1)}, u32[]{:S(2)}, u32[]{:S(2)}) %collective-permute-start.7) | collective-permute-done | bytes 65568 | tf_op jit(solution)/shard_map/ppermute | solution.py:151
  33.2 1.4 %collective-permute-done.8.b0_ref = bf16[2,128,128]{2,1,0:T(8,128)(2,1)S(1)} collective-permute-done((bf16[2,128,128]{2,1,0:T(8,128)(2,1)S(1)}, bf16[2,128,128]{2,1,0:T(8,128)(2,1)S(1)}, u32[]{:S(2)}, u32[]{:S(2)}) %collective-permute-start.8) | collective-permute-done | bytes 65568 | tf_op jit(solution)/shard_map/ppermute | solution.py:171
  34.7 0.7 %collective-permute-start.10 = (bf16[2,2,128,128]{3,2,1,0:T(8,128)(2,1)S(1)}, bf16[2,2,128,128]{3,2,1,0:T(8,128)(2,1)S(1)}, u32[]{:S(2)}, u32[]{:S(2)}) collective-permute-start(bf16[2,2,128,128]{3,2,1,0:T(8,128)(2,1)S(1)} %gown.1), channel_id=1, source_target_pairs={{0,0},{1,1},{2,2},{3,3},{4,4},{5,5},{6,6},{7,7},{8,8},{9,9},{10,10... | collective-permute-start | bytes 393224 | tf_op jit(solution)/shard_map/ppermute | solution.py:171
  35.4 1.0 %collective-permute-done.11.b_ref = bf16[4,128,128]{2,1,0:T(8,128)(2,1)S(1)} collective-permute-done((bf16[4,128,128]{2,1,0:T(8,128)(2,1)S(1)}, bf16[4,128,128]{2,1,0:T(8,128)(2,1)S(1)}, u32[]{:S(2)}, u32[]{:S(2)}) %collective-permute-start.11) | collective-permute-done | bytes 131104 | tf_op jit(solution)/shard_map/ppermute | solution.py:151
  36.4 6.4 %collective-permute-start.14 = (bf16[4,128,128]{2,1,0:T(8,128)(2,1)S(1)}, bf16[4,128,128]{2,1,0:T(8,128)(2,1)S(1)}, u32[]{:S(2)}, u32[]{:S(2)}) collective-permute-start(bf16[4,128,128]{2,1,0:T(8,128)(2,1)S(1)} %weights.1.refs_0_), channel_id=1, source_target_pairs={{0,96},{16,112},{32,64},{48,80},{64,32},{80,48},{96,0},{112,16},{1... | collective-permute-start | bytes 393224 | tf_op jit(solution)/shard_map/ppermute | solution.py:151
  42.7 0.9 %collective-permute-start.12 = (bf16[4,128,128]{2,1,0:T(8,128)(2,1)S(1)}, bf16[4,128,128]{2,1,0:T(8,128)(2,1)S(1)}, u32[]{:S(2)}, u32[]{:S(2)}) collective-permute-start(bf16[4,128,128]{2,1,0:T(8,128)(2,1)S(1)} %weights.1.refs_0_), channel_id=1, source_target_pairs={{0,32},{16,48},{32,0},{48,16},{64,96},{80,112},{96,64},{112,80},{1... | collective-permute-start | bytes 393224 | tf_op jit(solution)/shard_map/ppermute | solution.py:151
  43.7 1.8 %diag.1 = bf16[8,4,16,128]{3,2,1,0:T(8,128)(2,1)} custom-call(f32[4,128,128]{2,1,0:T(8,128)S(1)} %get-tuple-element.25.base_ref, f32[4,1,512]{2,1,0:T(1,128)S(1)} %get-tuple-element.26.gain_ref, bf16[4,128,512]{2,1,0:T(8,128)(2,1)S(1)} %get-tuple-element.27.wide_ref, bf16[4,128,512]{2,1,0:T(8,128)(2,1)S(1)} %get-tuple-element.28.flip_ref, ...), custom_call_target="tpu_custom_call" | custom-call | flops 201326592 | bytes 262144 | tf_op jit(solution)/shard_map/diag/pallas_call | solution.py:187
  45.4 4.9 %all-to-all-start.1 = ((bf16[8,4,16,128]{3,2,1,0:T(8,128)(2,1)}), bf16[8,4,16,128]{3,2,1,0:T(8,128)(2,1)S(1)}, u32[]{:S(2)}, u32[]{:S(2)}) async-start(bf16[8,4,16,128]{3,2,1,0:T(8,128)(2,1)} %diag.1), calls=%async_computation.1 | async-start | bytes 262144 | tf_op jit(solution)/shard_map/all_to_all | solution.py:193
  50.3 2.3 %density.1 = bf16[16,384,128]{2,1,0:T(8,128)(2,1)} custom-call(s32[2]{0:T(128)S(1)} %pad_add_fusion.at_ref, s32[256]{0:T(256)S(1)} %copy-done.2, bf16[16,384,128]{2,1,0:T(8,128)(2,1)S(1)} %all-to-all-done.moved_ref, bf16[4,128,128]{2,1,0:T(8,128)(2,1)S(1)} %weights.1.refs_0_, bf16[4,128,128]{2,1,0:T(8,128)(2,1)S(1)} %collective-permute-done.12.refs_1_, ...), custom_call_target="tpu_custom_call" | custom-call | flops 201326592 | bytes 3145728 | tf_op jit(solution)/shard_map/density/pallas_call | solution.py:196
  52.6 4.1 %all-to-all-done.1.got_ref = bf16[8,4,16,128]{3,2,1,0:T(8,128)(2,1)S(1)} async-done(((bf16[8,4,16,128]{3,2,1,0:T(8,128)(2,1)}), bf16[8,4,16,128]{3,2,1,0:T(8,128)(2,1)S(1)}, u32[]{:S(2)}, u32[]{:S(2)}) %all-to-all-start.1) | async-done | bytes 131104 | tf_op jit(solution)/shard_map/all_to_all | solution.py:193
  56.7 0.6 %finish.1 = bf16[16,16,128]{2,1,0:T(8,128)(2,1)} custom-call(bf16[8,4,16,128]{3,2,1,0:T(8,128)(2,1)S(1)} %all-to-all-done.1.got_ref), custom_call_target="tpu_custom_call" | custom-call | bytes 131072 | tf_op jit(solution)/shard_map/finish/pallas_call | solution.py:194
  (20 shorter events, 0.1 us)
Async XLA Ops:
  0.6 8.2 %copy-start = (bf16[16,384,128]{2,1,0:T(8,128)(2,1)S(1)}, bf16[16,384,128]{2,1,0:T(8,128)(2,1)}, u32[]{:S(2)}) copy-start(bf16[16,384,128]{2,1,0:T(8,128)(2,1)} %panel_ref.1) | copy-start | bytes 4718596
  0.6 8.2 %copy-start.2 = (s32[256]{0:T(256)S(1)}, s32[256]{0:T(256)}, u32[]{:S(2)}) copy-start(s32[256]{0:T(256)} %count_ref.5) | copy-start | bytes 3076
  0.6 44.8 %all-to-all-start = ((bf16[16,384,128]{2,1,0:T(8,128)(2,1)}), bf16[16,384,128]{2,1,0:T(8,128)(2,1)S(1)}, u32[]{:S(2)}, u32[]{:S(2)}) async-start(bf16[16,384,128]{2,1,0:T(8,128)(2,1)} %panel_ref.1), calls=%async_computation | async-start | bytes 3145728 | tf_op jit(solution)/shard_map/all_to_all | solution.py:153
  8.8 21.6 %copy-start.3 = (f32[8]{0:T(128)S(1)}, f32[8]{0:T(128)}, u32[]{:S(2)}) copy-start(f32[8]{0:T(128)} %w_ref.1) | copy-start | bytes 100
  8.9 1.0 %copy-start.1 = (bf16[1,16,128,128]{3,2,1,0:T(8,128)(2,1)S(1)}, bf16[1,16,128,128]{3,2,1,0:T(8,128)(2,1)}, u32[]{:S(2)}) copy-start(bf16[1,16,128,128]{3,2,1,0:T(8,128)(2,1)} %param.5) | copy-start | bytes 1572868
  11.1 9.0 %collective-permute-start.3 = (bf16[4,128,128]{2,1,0:T(8,128)(2,1)S(1)}, bf16[4,128,128]{2,1,0:T(8,128)(2,1)S(1)}, u32[]{:S(2)}, u32[]{:S(2)}) collective-permute-start(bf16[4,128,128]{2,1,0:T(8,128)(2,1)S(1)} %get-tuple-element.30), channel_id=1, source_target_pairs={{0,32},{16,48},{32,0},{48,16},{64,96},{80,112},{96,64},{112,80},{1... | collective-permute-start | bytes 393224 | tf_op jit(solution)/shard_map/ppermute | solution.py:151
  12.7 9.9 %collective-permute-start.4 = (bf16[4,128,128]{2,1,0:T(8,128)(2,1)S(1)}, bf16[4,128,128]{2,1,0:T(8,128)(2,1)S(1)}, u32[]{:S(2)}, u32[]{:S(2)}) collective-permute-start(bf16[4,128,128]{2,1,0:T(8,128)(2,1)S(1)} %get-tuple-element.31), channel_id=1, source_target_pairs={{0,64},{16,80},{32,96},{48,112},{64,0},{80,16},{96,32},{112,48},{1... | collective-permute-start | bytes 393224 | tf_op jit(solution)/shard_map/ppermute | solution.py:151
  15.4 10.0 %collective-permute-start.5 = (bf16[4,128,128]{2,1,0:T(8,128)(2,1)S(1)}, bf16[4,128,128]{2,1,0:T(8,128)(2,1)S(1)}, u32[]{:S(2)}, u32[]{:S(2)}) collective-permute-start(bf16[4,128,128]{2,1,0:T(8,128)(2,1)S(1)} %get-tuple-element.32), channel_id=1, source_target_pairs={{0,96},{16,112},{32,64},{48,80},{64,32},{80,48},{96,0},{112,16},{1... | collective-permute-start | bytes 393224 | tf_op jit(solution)/shard_map/ppermute | solution.py:151
  15.9 14.5 %collective-permute-start = (bf16[4,128,128]{2,1,0:T(8,128)(2,1)S(1)}, bf16[4,128,128]{2,1,0:T(8,128)(2,1)S(1)}, u32[]{:S(2)}, u32[]{:S(2)}) collective-permute-start(bf16[4,128,128]{2,1,0:T(8,128)(2,1)S(1)} %get-tuple-element.22), channel_id=1, source_target_pairs={{0,32},{16,48},{32,0},{48,16},{64,96},{80,112},{96,64},{112,80},{1... | collective-permute-start | bytes 393224 | tf_op jit(solution)/shard_map/ppermute | solution.py:151
  16.2 14.2 %collective-permute-start.1 = (bf16[4,128,128]{2,1,0:T(8,128)(2,1)S(1)}, bf16[4,128,128]{2,1,0:T(8,128)(2,1)S(1)}, u32[]{:S(2)}, u32[]{:S(2)}) collective-permute-start(bf16[4,128,128]{2,1,0:T(8,128)(2,1)S(1)} %get-tuple-element.23), channel_id=1, source_target_pairs={{0,64},{16,80},{32,96},{48,112},{64,0},{80,16},{96,32},{112,48},{1... | collective-permute-start | bytes 393224 | tf_op jit(solution)/shard_map/ppermute | solution.py:151
  20.1 10.3 %collective-permute-start.2 = (bf16[4,128,128]{2,1,0:T(8,128)(2,1)S(1)}, bf16[4,128,128]{2,1,0:T(8,128)(2,1)S(1)}, u32[]{:S(2)}, u32[]{:S(2)}) collective-permute-start(bf16[4,128,128]{2,1,0:T(8,128)(2,1)S(1)} %get-tuple-element.24), channel_id=1, source_target_pairs={{0,96},{16,112},{32,64},{48,80},{64,32},{80,48},{96,0},{112,16},{1... | collective-permute-start | bytes 393224 | tf_op jit(solution)/shard_map/ppermute | solution.py:151
  25.5 1.3 %collective-permute-start.6 = (bf16[2,128,128]{2,1,0:T(8,128)(2,1)S(1)}, bf16[2,128,128]{2,1,0:T(8,128)(2,1)S(1)}, u32[]{:S(2)}, u32[]{:S(2)}) collective-permute-start(bf16[2,128,128]{2,1,0:T(8,128)(2,1)S(1)} %get-tuple-element.34), channel_id=1, source_target_pairs={{0,1},{1,0},{2,3},{3,2},{4,5},{5,4},{6,7},{7,6},{8,9},{9,8},{10,11... | collective-permute-start | bytes 196616 | tf_op jit(solution)/shard_map/ppermute | solution.py:166
  26.8 6.4 %collective-permute-start.7 = (bf16[2,128,128]{2,1,0:T(8,128)(2,1)S(1)}, bf16[2,128,128]{2,1,0:T(8,128)(2,1)S(1)}, u32[]{:S(2)}, u32[]{:S(2)}) collective-permute-start(bf16[2,128,128]{2,1,0:T(8,128)(2,1)S(1)} %get-tuple-element.35.a0_ref), channel_id=1, source_target_pairs={{0,16},{16,0},{32,48},{48,32},{64,80},{80,64},{96,112},{112,96},{1... | collective-permute-start | bytes 196616 | tf_op jit(solution)/shard_map/ppermute | solution.py:151
  27.9 5.3 %collective-permute-start.9 = (bf16[2,128,128]{2,1,0:T(8,128)(2,1)S(1)}, bf16[2,128,128]{2,1,0:T(8,128)(2,1)S(1)}, u32[]{:S(2)}, u32[]{:S(2)}) collective-permute-start(bf16[2,128,128]{2,1,0:T(8,128)(2,1)S(1)} %get-tuple-element.36), channel_id=1, source_target_pairs={{0,18},{1,19},{2,16},{3,17},{4,22},{5,23},{6,20},{7,21},{8,26},{9,... | collective-permute-start | bytes 196616 | tf_op jit(solution)/shard_map/ppermute | solution.py:171
  30.4 4.3 %collective-permute-start.8 = (bf16[2,128,128]{2,1,0:T(8,128)(2,1)S(1)}, bf16[2,128,128]{2,1,0:T(8,128)(2,1)S(1)}, u32[]{:S(2)}, u32[]{:S(2)}) collective-permute-start(bf16[2,128,128]{2,1,0:T(8,128)(2,1)S(1)} %get-tuple-element.36), channel_id=1, source_target_pairs={{0,2},{1,3},{2,0},{3,1},{4,6},{5,7},{6,4},{7,5},{8,10},{9,11},{10,... | collective-permute-start | bytes 196616 | tf_op jit(solution)/shard_map/ppermute | solution.py:171
  31.2 5.1 %collective-permute-start.11 = (bf16[4,128,128]{2,1,0:T(8,128)(2,1)S(1)}, bf16[4,128,128]{2,1,0:T(8,128)(2,1)S(1)}, u32[]{:S(2)}, u32[]{:S(2)}) collective-permute-start(bf16[4,128,128]{2,1,0:T(8,128)(2,1)S(1)} %get-tuple-element.38.a_ref), channel_id=1, source_target_pairs={{0,16},{16,0},{32,48},{48,32},{64,80},{80,64},{96,112},{112,96},{1... | collective-permute-start | bytes 393224 | tf_op jit(solution)/shard_map/ppermute | solution.py:151
  34.7 9.0 %collective-permute-start.10 = (bf16[2,2,128,128]{3,2,1,0:T(8,128)(2,1)S(1)}, bf16[2,2,128,128]{3,2,1,0:T(8,128)(2,1)S(1)}, u32[]{:S(2)}, u32[]{:S(2)}) collective-permute-start(bf16[2,2,128,128]{3,2,1,0:T(8,128)(2,1)S(1)} %gown.1), channel_id=1, source_target_pairs={{0,0},{1,1},{2,2},{3,3},{4,4},{5,5},{6,6},{7,7},{8,8},{9,9},{10,10... | collective-permute-start | bytes 393224 | tf_op jit(solution)/shard_map/ppermute | solution.py:171
  36.4 14.0 %collective-permute-start.14 = (bf16[4,128,128]{2,1,0:T(8,128)(2,1)S(1)}, bf16[4,128,128]{2,1,0:T(8,128)(2,1)S(1)}, u32[]{:S(2)}, u32[]{:S(2)}) collective-permute-start(bf16[4,128,128]{2,1,0:T(8,128)(2,1)S(1)} %weights.1.refs_0_), channel_id=1, source_target_pairs={{0,96},{16,112},{32,64},{48,80},{64,32},{80,48},{96,0},{112,16},{1... | collective-permute-start | bytes 393224 | tf_op jit(solution)/shard_map/ppermute | solution.py:151
  42.7 7.6 %collective-permute-start.13 = (bf16[4,128,128]{2,1,0:T(8,128)(2,1)S(1)}, bf16[4,128,128]{2,1,0:T(8,128)(2,1)S(1)}, u32[]{:S(2)}, u32[]{:S(2)}) collective-permute-start(bf16[4,128,128]{2,1,0:T(8,128)(2,1)S(1)} %weights.1.refs_0_), channel_id=1, source_target_pairs={{0,64},{16,80},{32,96},{48,112},{64,0},{80,16},{96,32},{112,48},{1... | collective-permute-start | bytes 393224 | tf_op jit(solution)/shard_map/ppermute | solution.py:151
  42.7 7.6 %collective-permute-start.12 = (bf16[4,128,128]{2,1,0:T(8,128)(2,1)S(1)}, bf16[4,128,128]{2,1,0:T(8,128)(2,1)S(1)}, u32[]{:S(2)}, u32[]{:S(2)}) collective-permute-start(bf16[4,128,128]{2,1,0:T(8,128)(2,1)S(1)} %weights.1.refs_0_), channel_id=1, source_target_pairs={{0,32},{16,48},{32,0},{48,16},{64,96},{80,112},{96,64},{112,80},{1... | collective-permute-start | bytes 393224 | tf_op jit(solution)/shard_map/ppermute | solution.py:151
  45.4 11.3 %all-to-all-start.1 = ((bf16[8,4,16,128]{3,2,1,0:T(8,128)(2,1)}), bf16[8,4,16,128]{3,2,1,0:T(8,128)(2,1)S(1)}, u32[]{:S(2)}, u32[]{:S(2)}) async-start(bf16[8,4,16,128]{3,2,1,0:T(8,128)(2,1)} %diag.1), calls=%async_computation.1 | async-start | bytes 262144 | tf_op jit(solution)/shard_map/all_to_all | solution.py:193

commit v6 on v5

--- a/solution.py
+++ b/solution.py
@@ -17,6 +17,10 @@
 
 def dot_t(a, b):
     return lax.dot_general(a, b, (((0,), (0,)), ((), ())), preferred_element_type=F32)
+
+
+def slot(share, x, t):
+    return 2 * x + 2 * share * (t // 2) + t % 2
 
 
 def kept_rows(source, count, pole, poles, block):
@@ -31,16 +35,21 @@
     )
 
 
-def gram_kernel(poles, share, at_ref, count_ref, panel_ref, inv_ref, *out_refs):
+def gram_kernel(poles, share, at_ref, count_ref, panel_ref, *out_refs):
     pole, col = at_ref[0], at_ref[1]
-    owned, block = inv_ref.shape[0], inv_ref.shape[1]
-    half = len(out_refs) // 2
-    for k in range(half):
-        for t in range(share):
-            i = col ^ (share * ((pole // 2) ^ k) + t)
+    owned, block = panel_ref.shape[0], panel_ref.shape[2]
+    for k, out_ref in enumerate(out_refs):
+        for t in range(share):
+            i = col ^ slot(share, (pole // 2) ^ k, t)
             x = kept_rows(panel_ref.at[i], count_ref[i * owned + col], pole, poles, block)
-            out_refs[k][t] = dot_t(x, x).astype(BF16)
-            out_refs[half + k][t] = inv_ref[i]
+            out_ref[t] = dot_t(x, x).astype(BF16)
+
+
+def turn_kernel(share, inv_ref, *out_refs):
+    pole, col = lax.axis_index("pole"), lax.axis_index("col")
+    for k, out_ref in enumerate(out_refs):
+        for t in range(share):
+            out_ref[t] = inv_ref[col ^ slot(share, (pole // 2) ^ k, t)]
 
 
 def gsum_kernel(share, *refs):
@@ -71,7 +80,7 @@
     block = m_ref.shape[1]
     owned = share * len(got_refs)
     for t in range(share):
-        count = count_ref[col * owned + (col ^ (share * (pole // 2) + t))]
+        count = count_ref[col * owned + (col ^ slot(share, pole // 2, t))]
         scale = 1.0 / (jnp.full((1, block), block, F32) * count.astype(F32))
         base = jnp.zeros((block, block), F32)
         for k, got_ref in enumerate(got_refs):
@@ -107,7 +116,7 @@
     for x in range(got_ref.shape[0] // 2):
         for t in range(share):
             d = got_ref[2 * x, t].astype(F32) + got_ref[2 * x + 1, t].astype(F32)
-            out_ref[col ^ (share * x + t)] = d.astype(BF16)
+            out_ref[col ^ slot(share, x, t)] = d.astype(BF16)
 
 
 def density_kernel(poles, share, at_ref, count_ref, moved_ref, *refs):
@@ -116,7 +125,7 @@
     owned, block = moved_ref.shape[0], moved_ref.shape[2]
     for k, m_ref in enumerate(m_refs):
         for t in range(share):
-            i = col ^ (share * ((pole // 2) ^ k) + t)
+            i = col ^ slot(share, (pole // 2) ^ k, t)
             x = kept_rows(moved_ref.at[i], count_ref[col * owned + i], pole, poles, block)
             out_ref[i] = dot(x, m_ref[t]).astype(BF16)
 
@@ -152,13 +161,16 @@
 
     moved = lax.all_to_all(panel, "col", 0, 0, tiled=True)
 
+    turned = call(
+        functools.partial(turn_kernel, share), "turn", [vmem], [shape(share, block, block)] * half
+    )(pivot_inverse[0])
     sent = call(
         functools.partial(gram_kernel, poles, share), "gram",
-        [smem, smem, vmem, vmem], [shape(share, block, block)] * poles,
+        [smem, smem, vmem], [shape(share, block, block)] * half,
         2 * owned * rows * block * block,
-    )(at, row_count, panel, pivot_inverse[0])
+    )(at, row_count, panel)
     grams = [sent[0]] + [swap(sent[k], 2 * k) for k in range(1, half)]
-    inverses = [sent[half]] + [swap(sent[half + k], 2 * k) for k in range(1, half)]
+    inverses = [turned[0]] + [swap(turned[k], 2 * k) for k in range(1, half)]
 
     keep, give = call(
         functools.partial(gsum_kernel, share), "gsum", [vmem] * half, [shape(share // 2, block, block)] * 2
@@ -170,11 +182,11 @@
         pairs = [(p * cols + c, (p ^ z) * cols + (c ^ flip(p))) for p in range(poles) for c in range(cols)]
         return lax.ppermute(x, ("pole", "col"), pairs)
 
-    line = lambda p: 2
+    over = lambda p: 2 * share
     gfull = call(gown_kernel, "gown", [vmem] * 4, [shape(2, 2, block, block)])(
-        here, swap(here, 1), shift(side, 0, line), shift(side, 1, line)
+        here, swap(here, 1), shift(side, 0, over), shift(side, 1, over)
     )[0]
-    gfull = shift(gfull, 0, lambda p: share * (p // 2))
+    gfull = shift(gfull, 0, lambda p: 2 * (p // 2))
 
     wide = shape(share, block, half * block)
     mhalf, base, gain, wide, flip = call(

time: 57.9 us -> 56.9 us (0.983)
  local copies, waits for them, and re-layouts: 1.06 us -> 0.02 us
  waiting for transfers between devices: 13.5 us -> 14.3 us
  starting transfers between devices: 35.2 us -> 34.5 us
    ppermute x11, starting transfers between devices: 19 us -> 15.9 us  [swap(): return lax.ppermute(x, 'pole', [(i, i ^ k) for i in range(poles)])]
    ppermute x3, waiting for transfers between devices: 1.42 us -> 3.76 us  [shift(): return lax.ppermute(x, ('pole', 'col'), pairs)]
    ppermute x3, starting transfers between devices: 3.14 us -> 4.78 us  [shift(): return lax.ppermute(x, ('pole', 'col'), pairs)]
    ppermute x11, waiting for transfers between devices: 6.68 us -> 5.23 us  [swap(): return lax.ppermute(x, 'pole', [(i, i ^ k) for i in range(poles)])]
    unnamed x8, local copies, waits for them, and re-layouts: 1.06 us -> 0.02 us
    all_to_all x1, starting transfers between devices: 4.87 us -> 5.68 us  [shards(): part = lax.all_to_all(part, 'pole', 0, 0, tiled=True)]
where the time goes in v6:
time: 56.9 us; the launch traced here: 56.6 us
  starting transfers between devices  34.5 us (61%)
  waiting for transfers between devices  14.3 us (25%)
  Pallas kernels  6.85 us (12%)
  between operations  0.77 us (1%)
    ppermute x11, starting transfers between devices, swap(): return lax.ppermute(x, 'pole', [(i, i ^ k) for i in range(poles)])  15.9 us
    all_to_all x1, starting transfers between devices, shards(): moved = lax.all_to_all(panel, 'col', 0, 0, tiled=True)  8.11 us
    all_to_all x1, starting transfers between devices, shards(): part = lax.all_to_all(part, 'pole', 0, 0, tiled=True)  5.68 us
    ppermute x11, waiting for transfers between devices, swap(): return lax.ppermute(x, 'pole', [(i, i ^ k) for i in range(poles)])  5.23 us
    ppermute x3, starting transfers between devices, shift(): return lax.ppermute(x, ('pole', 'col'), pairs)  4.78 us
    all_to_all x1, waiting for transfers between devices, shards(): part = lax.all_to_all(part, 'pole', 0, 0, tiled=True)  4.11 us
    ppermute x3, waiting for transfers between devices, shift(): return lax.ppermute(x, ('pole', 'col'), pairs)  3.76 us
    pallas_call x1, Pallas kernels, shards(): call(functools.partial(density_kernel, poles, share), 'density', [smem, s...  2.27 us
  transfers between devices with their start and end apart: 17, of which 7 were waited for; matrix products, arithmetic and copies ran while one was open for 0% of the time, Pallas kernels for 11%

profile of v6, /device:TPU:0, one launch (start us, length us, event | category | flops | bytes accessed | tf_op | source)
XLA Modules:
  0.0 56.6 jit_solution(13584438383102042847)
XLA Ops:
  0.6 8.1 %all-to-all-start = ((bf16[16,384,128]{2,1,0:T(8,128)(2,1)}), bf16[16,384,128]{2,1,0:T(8,128)(2,1)S(1)}, u32[]{:S(2)}, u32[]{:S(2)}) async-start(bf16[16,384,128]{2,1,0:T(8,128)(2,1)} %panel_ref.1), calls=%async_computation | async-start | bytes 3145728 | tf_op jit(solution)/shard_map/all_to_all | solution.py:162
  8.8 0.0 copy-start.3
  8.8 0.1 pad_add_fusion.at_ref
  8.9 1.2 %gram.1 = (bf16[4,128,128]{2,1,0:T(8,128)(2,1)S(1)}, bf16[4,128,128]{2,1,0:T(8,128)(2,1)S(1)}, bf16[4,128,128]{2,1,0:T(8,128)(2,1)S(1)}, bf16[4,128,128]{2,1,0:T(8,128)(2,1)S(1)}) custom-call(s32[2]{0:T(128)S(1)} %pad_add_fusion.at_ref, s32[256]{0:T(256)S(1)} %copy-done.2, bf16[16,384,128]{2,1,0:T(8,128)(2,1)S(1)} %copy-done), custom_call_target="tpu_custom_call" | custom-call | flops 201326592 | bytes 1048576 | tf_op jit(solution)/shard_map/gram/pallas_call | solution.py:167
  10.1 1.6 %collective-permute-start.3 = (bf16[4,128,128]{2,1,0:T(8,128)(2,1)S(1)}, bf16[4,128,128]{2,1,0:T(8,128)(2,1)S(1)}, u32[]{:S(2)}, u32[]{:S(2)}) collective-permute-start(bf16[4,128,128]{2,1,0:T(8,128)(2,1)S(1)} %get-tuple-element.30), channel_id=1, source_target_pairs={{0,32},{16,48},{32,0},{48,16},{64,96},{80,112},{96,64},{112,80},{1... | collective-permute-start | bytes 393224 | tf_op jit(solution)/shard_map/ppermute | solution.py:160
  11.6 2.7 %collective-permute-start.4 = (bf16[4,128,128]{2,1,0:T(8,128)(2,1)S(1)}, bf16[4,128,128]{2,1,0:T(8,128)(2,1)S(1)}, u32[]{:S(2)}, u32[]{:S(2)}) collective-permute-start(bf16[4,128,128]{2,1,0:T(8,128)(2,1)S(1)} %get-tuple-element.31), channel_id=1, source_target_pairs={{0,64},{16,80},{32,96},{48,112},{64,0},{80,16},{96,32},{112,48},{1... | collective-permute-start | bytes 393224 | tf_op jit(solution)/shard_map/ppermute | solution.py:160
  14.4 0.5 collective-permute-start.5
  14.9 0.4 collective-permute-start
  15.3 3.9 %collective-permute-start.1 = (bf16[4,128,128]{2,1,0:T(8,128)(2,1)S(1)}, bf16[4,128,128]{2,1,0:T(8,128)(2,1)S(1)}, u32[]{:S(2)}, u32[]{:S(2)}) collective-permute-start(bf16[4,128,128]{2,1,0:T(8,128)(2,1)S(1)} %get-tuple-element.23), channel_id=1, source_target_pairs={{0,64},{16,80},{32,96},{48,112},{64,0},{80,16},{96,32},{112,48},{1... | collective-permute-start | bytes 393224 | tf_op jit(solution)/shard_map/ppermute | solution.py:160
  19.2 0.5 collective-permute-start.2
  19.7 1.8 %collective-permute-done.4.refs_2_ = bf16[4,128,128]{2,1,0:T(8,128)(2,1)S(1)} collective-permute-done((bf16[4,128,128]{2,1,0:T(8,128)(2,1)S(1)}, bf16[4,128,128]{2,1,0:T(8,128)(2,1)S(1)}, u32[]{:S(2)}, u32[]{:S(2)}) %collective-permute-start.4) | collective-permute-done | bytes 131104 | tf_op jit(solution)/shard_map/ppermute | solution.py:160
  21.5 2.9 %collective-permute-done.5.refs_3_ = bf16[4,128,128]{2,1,0:T(8,128)(2,1)S(1)} collective-permute-done((bf16[4,128,128]{2,1,0:T(8,128)(2,1)S(1)}, bf16[4,128,128]{2,1,0:T(8,128)(2,1)S(1)}, u32[]{:S(2)}, u32[]{:S(2)}) %collective-permute-start.5) | collective-permute-done | bytes 131104 | tf_op jit(solution)/shard_map/ppermute | solution.py:160
  24.4 0.1 gsum.1
  24.5 0.1 collective-permute-start.6
  24.5 1.2 %collective-permute-done.6.b_ref = bf16[2,128,128]{2,1,0:T(8,128)(2,1)S(1)} collective-permute-done((bf16[2,128,128]{2,1,0:T(8,128)(2,1)S(1)}, bf16[2,128,128]{2,1,0:T(8,128)(2,1)S(1)}, u32[]{:S(2)}, u32[]{:S(2)}) %collective-permute-start.6) | collective-permute-done | bytes 65568 | tf_op jit(solution)/shard_map/ppermute | solution.py:178
  25.8 1.1 %collective-permute-start.7 = (bf16[2,128,128]{2,1,0:T(8,128)(2,1)S(1)}, bf16[2,128,128]{2,1,0:T(8,128)(2,1)S(1)}, u32[]{:S(2)}, u32[]{:S(2)}) collective-permute-start(bf16[2,128,128]{2,1,0:T(8,128)(2,1)S(1)} %get-tuple-element.35.a0_ref), channel_id=1, source_target_pairs={{0,16},{16,0},{32,48},{48,32},{64,80},{80,64},{96,112},{112,96},{1... | collective-permute-start | bytes 196616 | tf_op jit(solution)/shard_map/ppermute | solution.py:160
  26.9 3.1 %collective-permute-start.9 = (bf16[2,128,128]{2,1,0:T(8,128)(2,1)S(1)}, bf16[2,128,128]{2,1,0:T(8,128)(2,1)S(1)}, u32[]{:S(2)}, u32[]{:S(2)}) collective-permute-start(bf16[2,128,128]{2,1,0:T(8,128)(2,1)S(1)} %get-tuple-element.36), channel_id=1, source_target_pairs={{0,24},{1,25},{2,26},{3,27},{4,28},{5,29},{6,30},{7,31},{8,16},{9,... | collective-permute-start | bytes 196616 | tf_op jit(solution)/shard_map/ppermute | solution.py:183
  30.0 1.1 %collective-permute-start.8 = (bf16[2,128,128]{2,1,0:T(8,128)(2,1)S(1)}, bf16[2,128,128]{2,1,0:T(8,128)(2,1)S(1)}, u32[]{:S(2)}, u32[]{:S(2)}) collective-permute-start(bf16[2,128,128]{2,1,0:T(8,128)(2,1)S(1)} %get-tuple-element.36), channel_id=1, source_target_pairs={{0,8},{1,9},{2,10},{3,11},{4,12},{5,13},{6,14},{7,15},{8,0},{9,1},... | collective-permute-start | bytes 196616 | tf_op jit(solution)/shard_map/ppermute | solution.py:183
  31.0 0.8 %prep.1 = (bf16[4,128,128]{2,1,0:T(8,128)(2,1)S(1)}, f32[4,128,128]{2,1,0:T(8,128)S(1)}, f32[4,1,512]{2,1,0:T(1,128)S(1)}, bf16[4,128,512]{2,1,0:T(8,128)(2,1)S(1)}, bf16[4,128,512]{2,1,0:T(8,128)(2,1)S(1)}) custom-call(s32[2]{0:T(128)S(1)} %pad_add_fusion.at_ref, f32[8]{0:T(128)S(1)} %copy-done.3, s32[256]{0:T(256)S(1)} %copy-done.2, ...), custom_call_target="tpu_custom_call" | custom-call | bytes 2629632 | tf_op jit(solution)/shard_map/prep/pallas_call | solution.py:192
  31.9 0.1 collective-permute-start.11
  32.0 1.5 %collective-permute-done.9.b1_ref = bf16[2,128,128]{2,1,0:T(8,128)(2,1)S(1)} collective-permute-done((bf16[2,128,128]{2,1,0:T(8,128)(2,1)S(1)}, bf16[2,128,128]{2,1,0:T(8,128)(2,1)S(1)}, u32[]{:S(2)}, u32[]{:S(2)}) %collective-permute-start.9) | collective-permute-done | bytes 65568 | tf_op jit(solution)/shard_map/ppermute | solution.py:183
  33.5 2.2 %collective-permute-done.8.b0_ref = bf16[2,128,128]{2,1,0:T(8,128)(2,1)S(1)} collective-permute-done((bf16[2,128,128]{2,1,0:T(8,128)(2,1)S(1)}, bf16[2,128,128]{2,1,0:T(8,128)(2,1)S(1)}, u32[]{:S(2)}, u32[]{:S(2)}) %collective-permute-start.8) | collective-permute-done | bytes 65568 | tf_op jit(solution)/shard_map/ppermute | solution.py:183
  35.8 0.7 %collective-permute-start.10 = (bf16[2,2,128,128]{3,2,1,0:T(8,128)(2,1)S(1)}, bf16[2,2,128,128]{3,2,1,0:T(8,128)(2,1)S(1)}, u32[]{:S(2)}, u32[]{:S(2)}) collective-permute-start(bf16[2,2,128,128]{3,2,1,0:T(8,128)(2,1)S(1)} %gown.1), channel_id=1, source_target_pairs={{0,0},{1,1},{2,2},{3,3},{4,4},{5,5},{6,6},{7,7},{8,8},{9,9},{10,10... | collective-permute-start | bytes 393224 | tf_op jit(solution)/shard_map/ppermute | solution.py:183
  36.4 0.5 collective-permute-done.11.b_ref
  37.0 4.2 %collective-permute-start.14 = (bf16[4,128,128]{2,1,0:T(8,128)(2,1)S(1)}, bf16[4,128,128]{2,1,0:T(8,128)(2,1)S(1)}, u32[]{:S(2)}, u32[]{:S(2)}) collective-permute-start(bf16[4,128,128]{2,1,0:T(8,128)(2,1)S(1)} %weights.1.refs_0_), channel_id=1, source_target_pairs={{0,96},{16,112},{32,64},{48,80},{64,32},{80,48},{96,0},{112,16},{1... | collective-permute-start | bytes 393224 | tf_op jit(solution)/shard_map/ppermute | solution.py:160
  41.1 0.1 collective-permute-start.13
  41.3 0.8 %collective-permute-start.12 = (bf16[4,128,128]{2,1,0:T(8,128)(2,1)S(1)}, bf16[4,128,128]{2,1,0:T(8,128)(2,1)S(1)}, u32[]{:S(2)}, u32[]{:S(2)}) collective-permute-start(bf16[4,128,128]{2,1,0:T(8,128)(2,1)S(1)} %weights.1.refs_0_), channel_id=1, source_target_pairs={{0,32},{16,48},{32,0},{48,16},{64,96},{80,112},{96,64},{112,80},{1... | collective-permute-start | bytes 393224 | tf_op jit(solution)/shard_map/ppermute | solution.py:160
  42.1 1.7 %diag.1 = bf16[8,4,16,128]{3,2,1,0:T(8,128)(2,1)} custom-call(f32[4,128,128]{2,1,0:T(8,128)S(1)} %get-tuple-element.25.base_ref, f32[4,1,512]{2,1,0:T(1,128)S(1)} %get-tuple-element.26.gain_ref, bf16[4,128,512]{2,1,0:T(8,128)(2,1)S(1)} %get-tuple-element.27.wide_ref, bf16[4,128,512]{2,1,0:T(8,128)(2,1)S(1)} %get-tuple-element.28.flip_ref, ...), custom_call_target="tpu_custom_call" | custom-call | flops 201326592 | bytes 262144 | tf_op jit(solution)/shard_map/diag/pallas_call | solution.py:199
  43.8 5.7 %all-to-all-start.1 = ((bf16[8,4,16,128]{3,2,1,0:T(8,128)(2,1)}), bf16[8,4,16,128]{3,2,1,0:T(8,128)(2,1)S(1)}, u32[]{:S(2)}, u32[]{:S(2)}) async-start(bf16[8,4,16,128]{3,2,1,0:T(8,128)(2,1)} %diag.1), calls=%async_computation.1 | async-start | bytes 262144 | tf_op jit(solution)/shard_map/all_to_all | solution.py:205
  49.6 2.3 %density.1 = bf16[16,384,128]{2,1,0:T(8,128)(2,1)} custom-call(s32[2]{0:T(128)S(1)} %pad_add_fusion.at_ref, s32[256]{0:T(256)S(1)} %copy-done.2, bf16[16,384,128]{2,1,0:T(8,128)(2,1)S(1)} %all-to-all-done.moved_ref, bf16[4,128,128]{2,1,0:T(8,128)(2,1)S(1)} %weights.1.refs_0_, bf16[4,128,128]{2,1,0:T(8,128)(2,1)S(1)} %collective-permute-done.12.refs_1_, ...), custom_call_target="tpu_custom_call" | custom-call | flops 201326592 | bytes 3145728 | tf_op jit(solution)/shard_map/density/pallas_call | solution.py:208
  51.8 4.1 %all-to-all-done.1.got_ref = bf16[8,4,16,128]{3,2,1,0:T(8,128)(2,1)S(1)} async-done(((bf16[8,4,16,128]{3,2,1,0:T(8,128)(2,1)}), bf16[8,4,16,128]{3,2,1,0:T(8,128)(2,1)S(1)}, u32[]{:S(2)}, u32[]{:S(2)}) %all-to-all-start.1) | async-done | bytes 131104 | tf_op jit(solution)/shard_map/all_to_all | solution.py:205
  55.9 0.6 %finish.1 = bf16[16,16,128]{2,1,0:T(8,128)(2,1)} custom-call(bf16[8,4,16,128]{3,2,1,0:T(8,128)(2,1)S(1)} %all-to-all-done.1.got_ref), custom_call_target="tpu_custom_call" | custom-call | bytes 131072 | tf_op jit(solution)/shard_map/finish/pallas_call | solution.py:206
  (21 shorter events, 0.2 us)
Async XLA Ops:
  0.6 8.2 %copy-start = (bf16[16,384,128]{2,1,0:T(8,128)(2,1)S(1)}, bf16[16,384,128]{2,1,0:T(8,128)(2,1)}, u32[]{:S(2)}) copy-start(bf16[16,384,128]{2,1,0:T(8,128)(2,1)} %panel_ref.1) | copy-start | bytes 4718596
  0.6 8.2 %copy-start.2 = (s32[256]{0:T(256)S(1)}, s32[256]{0:T(256)}, u32[]{:S(2)}) copy-start(s32[256]{0:T(256)} %count_ref.5) | copy-start | bytes 3076
  0.6 43.2 %all-to-all-start = ((bf16[16,384,128]{2,1,0:T(8,128)(2,1)}), bf16[16,384,128]{2,1,0:T(8,128)(2,1)S(1)}, u32[]{:S(2)}, u32[]{:S(2)}) async-start(bf16[16,384,128]{2,1,0:T(8,128)(2,1)} %panel_ref.1), calls=%async_computation | async-start | bytes 3145728 | tf_op jit(solution)/shard_map/all_to_all | solution.py:162
  8.8 22.3 %copy-start.3 = (f32[8]{0:T(128)S(1)}, f32[8]{0:T(128)}, u32[]{:S(2)}) copy-start(f32[8]{0:T(128)} %w_ref.1) | copy-start | bytes 100
  8.8 6.1 %copy-start.1 = (bf16[1,16,128,128]{3,2,1,0:T(8,128)(2,1)S(1)}, bf16[1,16,128,128]{3,2,1,0:T(8,128)(2,1)}, u32[]{:S(2)}) copy-start(bf16[1,16,128,128]{3,2,1,0:T(8,128)(2,1)} %param.5) | copy-start | bytes 1572868
  10.1 9.1 %collective-permute-start.3 = (bf16[4,128,128]{2,1,0:T(8,128)(2,1)S(1)}, bf16[4,128,128]{2,1,0:T(8,128)(2,1)S(1)}, u32[]{:S(2)}, u32[]{:S(2)}) collective-permute-start(bf16[4,128,128]{2,1,0:T(8,128)(2,1)S(1)} %get-tuple-element.30), channel_id=1, source_target_pairs={{0,32},{16,48},{32,0},{48,16},{64,96},{80,112},{96,64},{112,80},{1... | collective-permute-start | bytes 393224 | tf_op jit(solution)/shard_map/ppermute | solution.py:160
  11.6 9.9 %collective-permute-start.4 = (bf16[4,128,128]{2,1,0:T(8,128)(2,1)S(1)}, bf16[4,128,128]{2,1,0:T(8,128)(2,1)S(1)}, u32[]{:S(2)}, u32[]{:S(2)}) collective-permute-start(bf16[4,128,128]{2,1,0:T(8,128)(2,1)S(1)} %get-tuple-element.31), channel_id=1, source_target_pairs={{0,64},{16,80},{32,96},{48,112},{64,0},{80,16},{96,32},{112,48},{1... | collective-permute-start | bytes 393224 | tf_op jit(solution)/shard_map/ppermute | solution.py:160
  14.4 10.0 %collective-permute-start.5 = (bf16[4,128,128]{2,1,0:T(8,128)(2,1)S(1)}, bf16[4,128,128]{2,1,0:T(8,128)(2,1)S(1)}, u32[]{:S(2)}, u32[]{:S(2)}) collective-permute-start(bf16[4,128,128]{2,1,0:T(8,128)(2,1)S(1)} %get-tuple-element.32), channel_id=1, source_target_pairs={{0,96},{16,112},{32,64},{48,80},{64,32},{80,48},{96,0},{112,16},{1... | collective-permute-start | bytes 393224 | tf_op jit(solution)/shard_map/ppermute | solution.py:160
  14.9 15.1 %collective-permute-start = (bf16[4,128,128]{2,1,0:T(8,128)(2,1)S(1)}, bf16[4,128,128]{2,1,0:T(8,128)(2,1)S(1)}, u32[]{:S(2)}, u32[]{:S(2)}) collective-permute-start(bf16[4,128,128]{2,1,0:T(8,128)(2,1)S(1)} %get-tuple-element.22), channel_id=1, source_target_pairs={{0,32},{16,48},{32,0},{48,16},{64,96},{80,112},{96,64},{112,80},{1... | collective-permute-start | bytes 393224 | tf_op jit(solution)/shard_map/ppermute | solution.py:160
  15.3 15.8 %collective-permute-start.1 = (bf16[4,128,128]{2,1,0:T(8,128)(2,1)S(1)}, bf16[4,128,128]{2,1,0:T(8,128)(2,1)S(1)}, u32[]{:S(2)}, u32[]{:S(2)}) collective-permute-start(bf16[4,128,128]{2,1,0:T(8,128)(2,1)S(1)} %get-tuple-element.23), channel_id=1, source_target_pairs={{0,64},{16,80},{32,96},{48,112},{64,0},{80,16},{96,32},{112,48},{1... | collective-permute-start | bytes 393224 | tf_op jit(solution)/shard_map/ppermute | solution.py:160
  19.2 11.8 %collective-permute-start.2 = (bf16[4,128,128]{2,1,0:T(8,128)(2,1)S(1)}, bf16[4,128,128]{2,1,0:T(8,128)(2,1)S(1)}, u32[]{:S(2)}, u32[]{:S(2)}) collective-permute-start(bf16[4,128,128]{2,1,0:T(8,128)(2,1)S(1)} %get-tuple-element.24), channel_id=1, source_target_pairs={{0,96},{16,112},{32,64},{48,80},{64,32},{80,48},{96,0},{112,16},{1... | collective-permute-start | bytes 393224 | tf_op jit(solution)/shard_map/ppermute | solution.py:160
  24.5 1.3 %collective-permute-start.6 = (bf16[2,128,128]{2,1,0:T(8,128)(2,1)S(1)}, bf16[2,128,128]{2,1,0:T(8,128)(2,1)S(1)}, u32[]{:S(2)}, u32[]{:S(2)}) collective-permute-start(bf16[2,128,128]{2,1,0:T(8,128)(2,1)S(1)} %get-tuple-element.34), channel_id=1, source_target_pairs={{0,1},{1,0},{2,3},{3,2},{4,5},{5,4},{6,7},{7,6},{8,9},{9,8},{10,11... | collective-permute-start | bytes 196616 | tf_op jit(solution)/shard_map/ppermute | solution.py:178
  25.8 6.2 %collective-permute-start.7 = (bf16[2,128,128]{2,1,0:T(8,128)(2,1)S(1)}, bf16[2,128,128]{2,1,0:T(8,128)(2,1)S(1)}, u32[]{:S(2)}, u32[]{:S(2)}) collective-permute-start(bf16[2,128,128]{2,1,0:T(8,128)(2,1)S(1)} %get-tuple-element.35.a0_ref), channel_id=1, source_target_pairs={{0,16},{16,0},{32,48},{48,32},{64,80},{80,64},{96,112},{112,96},{1... | collective-permute-start | bytes 196616 | tf_op jit(solution)/shard_map/ppermute | solution.py:160
  26.9 6.6 %collective-permute-start.9 = (bf16[2,128,128]{2,1,0:T(8,128)(2,1)S(1)}, bf16[2,128,128]{2,1,0:T(8,128)(2,1)S(1)}, u32[]{:S(2)}, u32[]{:S(2)}) collective-permute-start(bf16[2,128,128]{2,1,0:T(8,128)(2,1)S(1)} %get-tuple-element.36), channel_id=1, source_target_pairs={{0,24},{1,25},{2,26},{3,27},{4,28},{5,29},{6,30},{7,31},{8,16},{9,... | collective-permute-start | bytes 196616 | tf_op jit(solution)/shard_map/ppermute | solution.py:183
  30.0 5.8 %collective-permute-start.8 = (bf16[2,128,128]{2,1,0:T(8,128)(2,1)S(1)}, bf16[2,128,128]{2,1,0:T(8,128)(2,1)S(1)}, u32[]{:S(2)}, u32[]{:S(2)}) collective-permute-start(bf16[2,128,128]{2,1,0:T(8,128)(2,1)S(1)} %get-tuple-element.36), channel_id=1, source_target_pairs={{0,8},{1,9},{2,10},{3,11},{4,12},{5,13},{6,14},{7,15},{8,0},{9,1},... | collective-permute-start | bytes 196616 | tf_op jit(solution)/shard_map/ppermute | solution.py:183
  31.9 5.1 %collective-permute-start.11 = (bf16[4,128,128]{2,1,0:T(8,128)(2,1)S(1)}, bf16[4,128,128]{2,1,0:T(8,128)(2,1)S(1)}, u32[]{:S(2)}, u32[]{:S(2)}) collective-permute-start(bf16[4,128,128]{2,1,0:T(8,128)(2,1)S(1)} %get-tuple-element.38.a_ref), channel_id=1, source_target_pairs={{0,16},{16,0},{32,48},{48,32},{64,80},{80,64},{96,112},{112,96},{1... | collective-permute-start | bytes 393224 | tf_op jit(solution)/shard_map/ppermute | solution.py:160
  35.8 6.3 %collective-permute-start.10 = (bf16[2,2,128,128]{3,2,1,0:T(8,128)(2,1)S(1)}, bf16[2,2,128,128]{3,2,1,0:T(8,128)(2,1)S(1)}, u32[]{:S(2)}, u32[]{:S(2)}) collective-permute-start(bf16[2,2,128,128]{3,2,1,0:T(8,128)(2,1)S(1)} %gown.1), channel_id=1, source_target_pairs={{0,0},{1,1},{2,2},{3,3},{4,4},{5,5},{6,6},{7,7},{8,8},{9,9},{10,10... | collective-permute-start | bytes 393224 | tf_op jit(solution)/shard_map/ppermute | solution.py:183
  37.0 12.6 %collective-permute-start.14 = (bf16[4,128,128]{2,1,0:T(8,128)(2,1)S(1)}, bf16[4,128,128]{2,1,0:T(8,128)(2,1)S(1)}, u32[]{:S(2)}, u32[]{:S(2)}) collective-permute-start(bf16[4,128,128]{2,1,0:T(8,128)(2,1)S(1)} %weights.1.refs_0_), channel_id=1, source_target_pairs={{0,96},{16,112},{32,64},{48,80},{64,32},{80,48},{96,0},{112,16},{1... | collective-permute-start | bytes 393224 | tf_op jit(solution)/shard_map/ppermute | solution.py:160
  41.1 8.4 %collective-permute-start.13 = (bf16[4,128,128]{2,1,0:T(8,128)(2,1)S(1)}, bf16[4,128,128]{2,1,0:T(8,128)(2,1)S(1)}, u32[]{:S(2)}, u32[]{:S(2)}) collective-permute-start(bf16[4,128,128]{2,1,0:T(8,128)(2,1)S(1)} %weights.1.refs_0_), channel_id=1, source_target_pairs={{0,64},{16,80},{32,96},{48,112},{64,0},{80,16},{96,32},{112,48},{1... | collective-permute-start | bytes 393224 | tf_op jit(solution)/shard_map/ppermute | solution.py:160
  41.3 8.3 %collective-permute-start.12 = (bf16[4,128,128]{2,1,0:T(8,128)(2,1)S(1)}, bf16[4,128,128]{2,1,0:T(8,128)(2,1)S(1)}, u32[]{:S(2)}, u32[]{:S(2)}) collective-permute-start(bf16[4,128,128]{2,1,0:T(8,128)(2,1)S(1)} %weights.1.refs_0_), channel_id=1, source_target_pairs={{0,32},{16,48},{32,0},{48,16},{64,96},{80,112},{96,64},{112,80},{1... | collective-permute-start | bytes 393224 | tf_op jit(solution)/shard_map/ppermute | solution.py:160
  43.8 12.1 %all-to-all-start.1 = ((bf16[8,4,16,128]{3,2,1,0:T(8,128)(2,1)}), bf16[8,4,16,128]{3,2,1,0:T(8,128)(2,1)S(1)}, u32[]{:S(2)}, u32[]{:S(2)}) async-start(bf16[8,4,16,128]{3,2,1,0:T(8,128)(2,1)} %diag.1), calls=%async_computation.1 | async-start | bytes 262144 | tf_op jit(solution)/shard_map/all_to_all | solution.py:205

commit v7 on v6

--- a/solution.py
+++ b/solution.py
@@ -65,7 +65,7 @@
         out_ref[1] = b_ref[f]
 
 
-def gown_kernel(a0_ref, a1_ref, b0_ref, b1_ref, out_ref):
+def gown_kernel(b0_ref, b1_ref, a0_ref, a1_ref, out_ref):
     for f, (x_ref, y_ref) in enumerate(((a0_ref, a1_ref), (b0_ref, b1_ref))):
         out_ref[f] = (x_ref[...].astype(F32) + y_ref[...].astype(F32)).astype(BF16)
 
@@ -184,7 +184,7 @@
 
     over = lambda p: 2 * share
     gfull = call(gown_kernel, "gown", [vmem] * 4, [shape(2, 2, block, block)])(
-        here, swap(here, 1), shift(side, 0, over), shift(side, 1, over)
+        shift(side, 1, over), shift(side, 0, over), here, swap(here, 1)
     )[0]
     gfull = shift(gfull, 0, lambda p: 2 * (p // 2))
 

time: 56.9 us -> 56.3 us (0.989)
  waiting for transfers between devices: 14.3 us -> 13.6 us
    ppermute x3, waiting for transfers between devices: 3.76 us -> 2.27 us  [shift(): return lax.ppermute(x, ('pole', 'col'), pairs)]
    ppermute x11, starting transfers between devices: 15.9 us -> 16.8 us  [swap(): return lax.ppermute(x, 'pole', [(i, i ^ k) for i in range(poles)])]
    ppermute x11, waiting for transfers between devices: 5.23 us -> 6 us  [swap(): return lax.ppermute(x, 'pole', [(i, i ^ k) for i in range(poles)])]
where the time goes in v7:
time: 56.3 us; the launch traced here: 56 us
  starting transfers between devices  34.7 us (62%)
  waiting for transfers between devices  13.6 us (24%)
  Pallas kernels  6.85 us (12%)
  between operations  0.76 us (1%)
    ppermute x11, starting transfers between devices, swap(): return lax.ppermute(x, 'pole', [(i, i ^ k) for i in range(poles)])  16.8 us
    all_to_all x1, starting transfers between devices, shards(): moved = lax.all_to_all(panel, 'col', 0, 0, tiled=True)  8.11 us
    ppermute x11, waiting for transfers between devices, swap(): return lax.ppermute(x, 'pole', [(i, i ^ k) for i in range(poles)])  6 us
    all_to_all x1, starting transfers between devices, shards(): part = lax.all_to_all(part, 'pole', 0, 0, tiled=True)  5.19 us
    ppermute x3, starting transfers between devices, shift(): return lax.ppermute(x, ('pole', 'col'), pairs)  4.51 us
    all_to_all x1, waiting for transfers between devices, shards(): part = lax.all_to_all(part, 'pole', 0, 0, tiled=True)  4.11 us
    ppermute x3, waiting for transfers between devices, shift(): return lax.ppermute(x, ('pole', 'col'), pairs)  2.27 us
    pallas_call x1, Pallas kernels, shards(): call(functools.partial(density_kernel, poles, share), 'density', [smem, s...  2.27 us
  transfers between devices with their start and end apart: 17, of which 7 were waited for; matrix products, arithmetic and copies ran while one was open for 0% of the time, Pallas kernels for 11%

profile of v7, /device:TPU:0, one launch (start us, length us, event | category | flops | bytes accessed | tf_op | source)
XLA Modules:
  0.0 56.0 jit_solution(18252754262223810315)
XLA Ops:
  0.6 8.1 %all-to-all-start = ((bf16[16,384,128]{2,1,0:T(8,128)(2,1)}), bf16[16,384,128]{2,1,0:T(8,128)(2,1)S(1)}, u32[]{:S(2)}, u32[]{:S(2)}) async-start(bf16[16,384,128]{2,1,0:T(8,128)(2,1)} %panel_ref.1), calls=%async_computation | async-start | bytes 3145728 | tf_op jit(solution)/shard_map/all_to_all | solution.py:162
  8.8 0.0 copy-start.1
  8.8 0.1 pad_add_fusion.at_ref
  8.9 1.2 %gram.1 = (bf16[4,128,128]{2,1,0:T(8,128)(2,1)S(1)}, bf16[4,128,128]{2,1,0:T(8,128)(2,1)S(1)}, bf16[4,128,128]{2,1,0:T(8,128)(2,1)S(1)}, bf16[4,128,128]{2,1,0:T(8,128)(2,1)S(1)}) custom-call(s32[2]{0:T(128)S(1)} %pad_add_fusion.at_ref, s32[256]{0:T(256)S(1)} %copy-done.2, bf16[16,384,128]{2,1,0:T(8,128)(2,1)S(1)} %copy-done), custom_call_target="tpu_custom_call" | custom-call | flops 201326592 | bytes 1048576 | tf_op jit(solution)/shard_map/gram/pallas_call | solution.py:167
  10.1 1.6 %collective-permute-start.3 = (bf16[4,128,128]{2,1,0:T(8,128)(2,1)S(1)}, bf16[4,128,128]{2,1,0:T(8,128)(2,1)S(1)}, u32[]{:S(2)}, u32[]{:S(2)}) collective-permute-start(bf16[4,128,128]{2,1,0:T(8,128)(2,1)S(1)} %get-tuple-element.30), channel_id=1, source_target_pairs={{0,32},{16,48},{32,0},{48,16},{64,96},{80,112},{96,64},{112,80},{1... | collective-permute-start | bytes 393224 | tf_op jit(solution)/shard_map/ppermute | solution.py:160
  11.6 2.7 %collective-permute-start.4 = (bf16[4,128,128]{2,1,0:T(8,128)(2,1)S(1)}, bf16[4,128,128]{2,1,0:T(8,128)(2,1)S(1)}, u32[]{:S(2)}, u32[]{:S(2)}) collective-permute-start(bf16[4,128,128]{2,1,0:T(8,128)(2,1)S(1)} %get-tuple-element.31), channel_id=1, source_target_pairs={{0,64},{16,80},{32,96},{48,112},{64,0},{80,16},{96,32},{112,48},{1... | collective-permute-start | bytes 393224 | tf_op jit(solution)/shard_map/ppermute | solution.py:160
  14.4 0.5 collective-permute-start.5
  14.9 0.4 collective-permute-start
  15.3 3.9 %collective-permute-start.1 = (bf16[4,128,128]{2,1,0:T(8,128)(2,1)S(1)}, bf16[4,128,128]{2,1,0:T(8,128)(2,1)S(1)}, u32[]{:S(2)}, u32[]{:S(2)}) collective-permute-start(bf16[4,128,128]{2,1,0:T(8,128)(2,1)S(1)} %get-tuple-element.23), channel_id=1, source_target_pairs={{0,64},{16,80},{32,96},{48,112},{64,0},{80,16},{96,32},{112,48},{1... | collective-permute-start | bytes 393224 | tf_op jit(solution)/shard_map/ppermute | solution.py:160
  19.2 0.5 collective-permute-start.2
  19.7 1.8 %collective-permute-done.4.refs_2_ = bf16[4,128,128]{2,1,0:T(8,128)(2,1)S(1)} collective-permute-done((bf16[4,128,128]{2,1,0:T(8,128)(2,1)S(1)}, bf16[4,128,128]{2,1,0:T(8,128)(2,1)S(1)}, u32[]{:S(2)}, u32[]{:S(2)}) %collective-permute-start.4) | collective-permute-done | bytes 131104 | tf_op jit(solution)/shard_map/ppermute | solution.py:160
  21.5 2.9 %collective-permute-done.5.refs_3_ = bf16[4,128,128]{2,1,0:T(8,128)(2,1)S(1)} collective-permute-done((bf16[4,128,128]{2,1,0:T(8,128)(2,1)S(1)}, bf16[4,128,128]{2,1,0:T(8,128)(2,1)S(1)}, u32[]{:S(2)}, u32[]{:S(2)}) %collective-permute-start.5) | collective-permute-done | bytes 131104 | tf_op jit(solution)/shard_map/ppermute | solution.py:160
  24.4 0.1 gsum.1
  24.5 0.1 collective-permute-start.6
  24.5 1.2 %collective-permute-done.6.b_ref = bf16[2,128,128]{2,1,0:T(8,128)(2,1)S(1)} collective-permute-done((bf16[2,128,128]{2,1,0:T(8,128)(2,1)S(1)}, bf16[2,128,128]{2,1,0:T(8,128)(2,1)S(1)}, u32[]{:S(2)}, u32[]{:S(2)}) %collective-permute-start.6) | collective-permute-done | bytes 65568 | tf_op jit(solution)/shard_map/ppermute | solution.py:178
  25.8 3.6 %collective-permute-start.8 = (bf16[2,128,128]{2,1,0:T(8,128)(2,1)S(1)}, bf16[2,128,128]{2,1,0:T(8,128)(2,1)S(1)}, u32[]{:S(2)}, u32[]{:S(2)}) collective-permute-start(bf16[2,128,128]{2,1,0:T(8,128)(2,1)S(1)} %get-tuple-element.35), channel_id=1, source_target_pairs={{0,8},{1,9},{2,10},{3,11},{4,12},{5,13},{6,14},{7,15},{8,0},{9,1},... | collective-permute-start | bytes 196616 | tf_op jit(solution)/shard_map/ppermute | solution.py:183
  29.4 0.3 collective-permute-start.7
  29.6 0.8 %collective-permute-start.9 = (bf16[2,128,128]{2,1,0:T(8,128)(2,1)S(1)}, bf16[2,128,128]{2,1,0:T(8,128)(2,1)S(1)}, u32[]{:S(2)}, u32[]{:S(2)}) collective-permute-start(bf16[2,128,128]{2,1,0:T(8,128)(2,1)S(1)} %get-tuple-element.36.a0_ref), channel_id=1, source_target_pairs={{0,16},{16,0},{32,48},{48,32},{64,80},{80,64},{96,112},{112,96},{1... | collective-permute-start | bytes 196616 | tf_op jit(solution)/shard_map/ppermute | solution.py:160
  30.4 0.8 %prep.1 = (bf16[4,128,128]{2,1,0:T(8,128)(2,1)S(1)}, f32[4,128,128]{2,1,0:T(8,128)S(1)}, f32[4,1,512]{2,1,0:T(1,128)S(1)}, bf16[4,128,512]{2,1,0:T(8,128)(2,1)S(1)}, bf16[4,128,512]{2,1,0:T(8,128)(2,1)S(1)}) custom-call(s32[2]{0:T(128)S(1)} %pad_add_fusion.at_ref, f32[8]{0:T(128)S(1)} %copy-done.3, s32[256]{0:T(256)S(1)} %copy-done.2, ...), custom_call_target="tpu_custom_call" | custom-call | bytes 2629632 | tf_op jit(solution)/shard_map/prep/pallas_call | solution.py:192
  31.3 1.3 %collective-permute-start.11 = (bf16[4,128,128]{2,1,0:T(8,128)(2,1)S(1)}, bf16[4,128,128]{2,1,0:T(8,128)(2,1)S(1)}, u32[]{:S(2)}, u32[]{:S(2)}) collective-permute-start(bf16[4,128,128]{2,1,0:T(8,128)(2,1)S(1)} %get-tuple-element.38.a_ref), channel_id=1, source_target_pairs={{0,16},{16,0},{32,48},{48,32},{64,80},{80,64},{96,112},{112,96},{1... | collective-permute-start | bytes 393224 | tf_op jit(solution)/shard_map/ppermute | solution.py:160
  32.6 0.8 %collective-permute-done.8.b1_ref = bf16[2,128,128]{2,1,0:T(8,128)(2,1)S(1)} collective-permute-done((bf16[2,128,128]{2,1,0:T(8,128)(2,1)S(1)}, bf16[2,128,128]{2,1,0:T(8,128)(2,1)S(1)}, u32[]{:S(2)}, u32[]{:S(2)}) %collective-permute-start.8) | collective-permute-done | bytes 65568 | tf_op jit(solution)/shard_map/ppermute | solution.py:183
  33.4 1.5 %collective-permute-done.7.b0_ref = bf16[2,128,128]{2,1,0:T(8,128)(2,1)S(1)} collective-permute-done((bf16[2,128,128]{2,1,0:T(8,128)(2,1)S(1)}, bf16[2,128,128]{2,1,0:T(8,128)(2,1)S(1)}, u32[]{:S(2)}, u32[]{:S(2)}) %collective-permute-start.7) | collective-permute-done | bytes 65568 | tf_op jit(solution)/shard_map/ppermute | solution.py:183
  34.9 0.7 %collective-permute-start.10 = (bf16[2,2,128,128]{3,2,1,0:T(8,128)(2,1)S(1)}, bf16[2,2,128,128]{3,2,1,0:T(8,128)(2,1)S(1)}, u32[]{:S(2)}, u32[]{:S(2)}) collective-permute-start(bf16[2,2,128,128]{3,2,1,0:T(8,128)(2,1)S(1)} %gown.1), channel_id=1, source_target_pairs={{0,0},{1,1},{2,2},{3,3},{4,4},{5,5},{6,6},{7,7},{8,8},{9,9},{10,10... | collective-permute-start | bytes 393224 | tf_op jit(solution)/shard_map/ppermute | solution.py:183
  35.6 1.3 %collective-permute-done.11.b_ref = bf16[4,128,128]{2,1,0:T(8,128)(2,1)S(1)} collective-permute-done((bf16[4,128,128]{2,1,0:T(8,128)(2,1)S(1)}, bf16[4,128,128]{2,1,0:T(8,128)(2,1)S(1)}, u32[]{:S(2)}, u32[]{:S(2)}) %collective-permute-start.11) | collective-permute-done | bytes 131104 | tf_op jit(solution)/shard_map/ppermute | solution.py:160
  36.9 4.2 %collective-permute-start.14 = (bf16[4,128,128]{2,1,0:T(8,128)(2,1)S(1)}, bf16[4,128,128]{2,1,0:T(8,128)(2,1)S(1)}, u32[]{:S(2)}, u32[]{:S(2)}) collective-permute-start(bf16[4,128,128]{2,1,0:T(8,128)(2,1)S(1)} %weights.1.refs_0_), channel_id=1, source_target_pairs={{0,96},{16,112},{32,64},{48,80},{64,32},{80,48},{96,0},{112,16},{1... | collective-permute-start | bytes 393224 | tf_op jit(solution)/shard_map/ppermute | solution.py:160
  41.1 0.2 collective-permute-start.13
  41.2 0.8 %collective-permute-start.12 = (bf16[4,128,128]{2,1,0:T(8,128)(2,1)S(1)}, bf16[4,128,128]{2,1,0:T(8,128)(2,1)S(1)}, u32[]{:S(2)}, u32[]{:S(2)}) collective-permute-start(bf16[4,128,128]{2,1,0:T(8,128)(2,1)S(1)} %weights.1.refs_0_), channel_id=1, source_target_pairs={{0,32},{16,48},{32,0},{48,16},{64,96},{80,112},{96,64},{112,80},{1... | collective-permute-start | bytes 393224 | tf_op jit(solution)/shard_map/ppermute | solution.py:160
  42.0 1.7 %diag.1 = bf16[8,4,16,128]{3,2,1,0:T(8,128)(2,1)} custom-call(f32[4,128,128]{2,1,0:T(8,128)S(1)} %get-tuple-element.25.base_ref, f32[4,1,512]{2,1,0:T(1,128)S(1)} %get-tuple-element.26.gain_ref, bf16[4,128,512]{2,1,0:T(8,128)(2,1)S(1)} %get-tuple-element.27.wide_ref, bf16[4,128,512]{2,1,0:T(8,128)(2,1)S(1)} %get-tuple-element.28.flip_ref, ...), custom_call_target="tpu_custom_call" | custom-call | flops 201326592 | bytes 262144 | tf_op jit(solution)/shard_map/diag/pallas_call | solution.py:199
  43.8 5.2 %all-to-all-start.1 = ((bf16[8,4,16,128]{3,2,1,0:T(8,128)(2,1)}), bf16[8,4,16,128]{3,2,1,0:T(8,128)(2,1)S(1)}, u32[]{:S(2)}, u32[]{:S(2)}) async-start(bf16[8,4,16,128]{3,2,1,0:T(8,128)(2,1)} %diag.1), calls=%async_computation.1 | async-start | bytes 262144 | tf_op jit(solution)/shard_map/all_to_all | solution.py:205
  49.0 2.3 %density.1 = bf16[16,384,128]{2,1,0:T(8,128)(2,1)} custom-call(s32[2]{0:T(128)S(1)} %pad_add_fusion.at_ref, s32[256]{0:T(256)S(1)} %copy-done.2, bf16[16,384,128]{2,1,0:T(8,128)(2,1)S(1)} %all-to-all-done.moved_ref, bf16[4,128,128]{2,1,0:T(8,128)(2,1)S(1)} %weights.1.refs_0_, bf16[4,128,128]{2,1,0:T(8,128)(2,1)S(1)} %collective-permute-done.12.refs_1_, ...), custom_call_target="tpu_custom_call" | custom-call | flops 201326592 | bytes 3145728 | tf_op jit(solution)/shard_map/density/pallas_call | solution.py:208
  51.3 4.1 %all-to-all-done.1.got_ref = bf16[8,4,16,128]{3,2,1,0:T(8,128)(2,1)S(1)} async-done(((bf16[8,4,16,128]{3,2,1,0:T(8,128)(2,1)}), bf16[8,4,16,128]{3,2,1,0:T(8,128)(2,1)S(1)}, u32[]{:S(2)}, u32[]{:S(2)}) %all-to-all-start.1) | async-done | bytes 131104 | tf_op jit(solution)/shard_map/all_to_all | solution.py:205
  55.4 0.6 %finish.1 = bf16[16,16,128]{2,1,0:T(8,128)(2,1)} custom-call(bf16[8,4,16,128]{3,2,1,0:T(8,128)(2,1)S(1)} %all-to-all-done.1.got_ref), custom_call_target="tpu_custom_call" | custom-call | bytes 131072 | tf_op jit(solution)/shard_map/finish/pallas_call | solution.py:206
  (21 shorter events, 0.2 us)
Async XLA Ops:
  0.6 8.2 %copy-start = (bf16[16,384,128]{2,1,0:T(8,128)(2,1)S(1)}, bf16[16,384,128]{2,1,0:T(8,128)(2,1)}, u32[]{:S(2)}) copy-start(bf16[16,384,128]{2,1,0:T(8,128)(2,1)} %panel_ref.1) | copy-start | bytes 4718596
  0.6 8.2 %copy-start.2 = (s32[256]{0:T(256)S(1)}, s32[256]{0:T(256)}, u32[]{:S(2)}) copy-start(s32[256]{0:T(256)} %count_ref.5) | copy-start | bytes 3076
  0.6 43.1 %all-to-all-start = ((bf16[16,384,128]{2,1,0:T(8,128)(2,1)}), bf16[16,384,128]{2,1,0:T(8,128)(2,1)S(1)}, u32[]{:S(2)}, u32[]{:S(2)}) async-start(bf16[16,384,128]{2,1,0:T(8,128)(2,1)} %panel_ref.1), calls=%async_computation | async-start | bytes 3145728 | tf_op jit(solution)/shard_map/all_to_all | solution.py:162
  8.8 21.6 %copy-start.3 = (f32[8]{0:T(128)S(1)}, f32[8]{0:T(128)}, u32[]{:S(2)}) copy-start(f32[8]{0:T(128)} %w_ref.1) | copy-start | bytes 100
  8.8 6.1 %copy-start.1 = (bf16[1,16,128,128]{3,2,1,0:T(8,128)(2,1)S(1)}, bf16[1,16,128,128]{3,2,1,0:T(8,128)(2,1)}, u32[]{:S(2)}) copy-start(bf16[1,16,128,128]{3,2,1,0:T(8,128)(2,1)} %param.5) | copy-start | bytes 1572868
  10.1 9.1 %collective-permute-start.3 = (bf16[4,128,128]{2,1,0:T(8,128)(2,1)S(1)}, bf16[4,128,128]{2,1,0:T(8,128)(2,1)S(1)}, u32[]{:S(2)}, u32[]{:S(2)}) collective-permute-start(bf16[4,128,128]{2,1,0:T(8,128)(2,1)S(1)} %get-tuple-element.30), channel_id=1, source_target_pairs={{0,32},{16,48},{32,0},{48,16},{64,96},{80,112},{96,64},{112,80},{1... | collective-permute-start | bytes 393224 | tf_op jit(solution)/shard_map/ppermute | solution.py:160
  11.6 9.9 %collective-permute-start.4 = (bf16[4,128,128]{2,1,0:T(8,128)(2,1)S(1)}, bf16[4,128,128]{2,1,0:T(8,128)(2,1)S(1)}, u32[]{:S(2)}, u32[]{:S(2)}) collective-permute-start(bf16[4,128,128]{2,1,0:T(8,128)(2,1)S(1)} %get-tuple-element.31), channel_id=1, source_target_pairs={{0,64},{16,80},{32,96},{48,112},{64,0},{80,16},{96,32},{112,48},{1... | collective-permute-start | bytes 393224 | tf_op jit(solution)/shard_map/ppermute | solution.py:160
  14.4 10.0 %collective-permute-start.5 = (bf16[4,128,128]{2,1,0:T(8,128)(2,1)S(1)}, bf16[4,128,128]{2,1,0:T(8,128)(2,1)S(1)}, u32[]{:S(2)}, u32[]{:S(2)}) collective-permute-start(bf16[4,128,128]{2,1,0:T(8,128)(2,1)S(1)} %get-tuple-element.32), channel_id=1, source_target_pairs={{0,96},{16,112},{32,64},{48,80},{64,32},{80,48},{96,0},{112,16},{1... | collective-permute-start | bytes 393224 | tf_op jit(solution)/shard_map/ppermute | solution.py:160
  14.9 14.8 %collective-permute-start = (bf16[4,128,128]{2,1,0:T(8,128)(2,1)S(1)}, bf16[4,128,128]{2,1,0:T(8,128)(2,1)S(1)}, u32[]{:S(2)}, u32[]{:S(2)}) collective-permute-start(bf16[4,128,128]{2,1,0:T(8,128)(2,1)S(1)} %get-tuple-element.22), channel_id=1, source_target_pairs={{0,32},{16,48},{32,0},{48,16},{64,96},{80,112},{96,64},{112,80},{1... | collective-permute-start | bytes 393224 | tf_op jit(solution)/shard_map/ppermute | solution.py:160
  15.3 15.2 %collective-permute-start.1 = (bf16[4,128,128]{2,1,0:T(8,128)(2,1)S(1)}, bf16[4,128,128]{2,1,0:T(8,128)(2,1)S(1)}, u32[]{:S(2)}, u32[]{:S(2)}) collective-permute-start(bf16[4,128,128]{2,1,0:T(8,128)(2,1)S(1)} %get-tuple-element.23), channel_id=1, source_target_pairs={{0,64},{16,80},{32,96},{48,112},{64,0},{80,16},{96,32},{112,48},{1... | collective-permute-start | bytes 393224 | tf_op jit(solution)/shard_map/ppermute | solution.py:160
  19.2 11.2 %collective-permute-start.2 = (bf16[4,128,128]{2,1,0:T(8,128)(2,1)S(1)}, bf16[4,128,128]{2,1,0:T(8,128)(2,1)S(1)}, u32[]{:S(2)}, u32[]{:S(2)}) collective-permute-start(bf16[4,128,128]{2,1,0:T(8,128)(2,1)S(1)} %get-tuple-element.24), channel_id=1, source_target_pairs={{0,96},{16,112},{32,64},{48,80},{64,32},{80,48},{96,0},{112,16},{1... | collective-permute-start | bytes 393224 | tf_op jit(solution)/shard_map/ppermute | solution.py:160
  24.5 1.3 %collective-permute-start.6 = (bf16[2,128,128]{2,1,0:T(8,128)(2,1)S(1)}, bf16[2,128,128]{2,1,0:T(8,128)(2,1)S(1)}, u32[]{:S(2)}, u32[]{:S(2)}) collective-permute-start(bf16[2,128,128]{2,1,0:T(8,128)(2,1)S(1)} %get-tuple-element.34), channel_id=1, source_target_pairs={{0,1},{1,0},{2,3},{3,2},{4,5},{5,4},{6,7},{7,6},{8,9},{9,8},{10,11... | collective-permute-start | bytes 196616 | tf_op jit(solution)/shard_map/ppermute | solution.py:178
  25.8 7.6 %collective-permute-start.8 = (bf16[2,128,128]{2,1,0:T(8,128)(2,1)S(1)}, bf16[2,128,128]{2,1,0:T(8,128)(2,1)S(1)}, u32[]{:S(2)}, u32[]{:S(2)}) collective-permute-start(bf16[2,128,128]{2,1,0:T(8,128)(2,1)S(1)} %get-tuple-element.35), channel_id=1, source_target_pairs={{0,8},{1,9},{2,10},{3,11},{4,12},{5,13},{6,14},{7,15},{8,0},{9,1},... | collective-permute-start | bytes 196616 | tf_op jit(solution)/shard_map/ppermute | solution.py:183
  29.4 5.5 %collective-permute-start.7 = (bf16[2,128,128]{2,1,0:T(8,128)(2,1)S(1)}, bf16[2,128,128]{2,1,0:T(8,128)(2,1)S(1)}, u32[]{:S(2)}, u32[]{:S(2)}) collective-permute-start(bf16[2,128,128]{2,1,0:T(8,128)(2,1)S(1)} %get-tuple-element.35), channel_id=1, source_target_pairs={{0,24},{1,25},{2,26},{3,27},{4,28},{5,29},{6,30},{7,31},{8,16},{9,... | collective-permute-start | bytes 196616 | tf_op jit(solution)/shard_map/ppermute | solution.py:183
  29.6 5.2 %collective-permute-start.9 = (bf16[2,128,128]{2,1,0:T(8,128)(2,1)S(1)}, bf16[2,128,128]{2,1,0:T(8,128)(2,1)S(1)}, u32[]{:S(2)}, u32[]{:S(2)}) collective-permute-start(bf16[2,128,128]{2,1,0:T(8,128)(2,1)S(1)} %get-tuple-element.36.a0_ref), channel_id=1, source_target_pairs={{0,16},{16,0},{32,48},{48,32},{64,80},{80,64},{96,112},{112,96},{1... | collective-permute-start | bytes 196616 | tf_op jit(solution)/shard_map/ppermute | solution.py:160
  31.3 5.6 %collective-permute-start.11 = (bf16[4,128,128]{2,1,0:T(8,128)(2,1)S(1)}, bf16[4,128,128]{2,1,0:T(8,128)(2,1)S(1)}, u32[]{:S(2)}, u32[]{:S(2)}) collective-permute-start(bf16[4,128,128]{2,1,0:T(8,128)(2,1)S(1)} %get-tuple-element.38.a_ref), channel_id=1, source_target_pairs={{0,16},{16,0},{32,48},{48,32},{64,80},{80,64},{96,112},{112,96},{1... | collective-permute-start | bytes 393224 | tf_op jit(solution)/shard_map/ppermute | solution.py:160
  34.9 7.1 %collective-permute-start.10 = (bf16[2,2,128,128]{3,2,1,0:T(8,128)(2,1)S(1)}, bf16[2,2,128,128]{3,2,1,0:T(8,128)(2,1)S(1)}, u32[]{:S(2)}, u32[]{:S(2)}) collective-permute-start(bf16[2,2,128,128]{3,2,1,0:T(8,128)(2,1)S(1)} %gown.1), channel_id=1, source_target_pairs={{0,0},{1,1},{2,2},{3,3},{4,4},{5,5},{6,6},{7,7},{8,8},{9,9},{10,10... | collective-permute-start | bytes 393224 | tf_op jit(solution)/shard_map/ppermute | solution.py:183
  36.9 12.1 %collective-permute-start.14 = (bf16[4,128,128]{2,1,0:T(8,128)(2,1)S(1)}, bf16[4,128,128]{2,1,0:T(8,128)(2,1)S(1)}, u32[]{:S(2)}, u32[]{:S(2)}) collective-permute-start(bf16[4,128,128]{2,1,0:T(8,128)(2,1)S(1)} %weights.1.refs_0_), channel_id=1, source_target_pairs={{0,96},{16,112},{32,64},{48,80},{64,32},{80,48},{96,0},{112,16},{1... | collective-permute-start | bytes 393224 | tf_op jit(solution)/shard_map/ppermute | solution.py:160
  41.1 7.9 %collective-permute-start.13 = (bf16[4,128,128]{2,1,0:T(8,128)(2,1)S(1)}, bf16[4,128,128]{2,1,0:T(8,128)(2,1)S(1)}, u32[]{:S(2)}, u32[]{:S(2)}) collective-permute-start(bf16[4,128,128]{2,1,0:T(8,128)(2,1)S(1)} %weights.1.refs_0_), channel_id=1, source_target_pairs={{0,64},{16,80},{32,96},{48,112},{64,0},{80,16},{96,32},{112,48},{1... | collective-permute-start | bytes 393224 | tf_op jit(solution)/shard_map/ppermute | solution.py:160
  41.2 7.7 %collective-permute-start.12 = (bf16[4,128,128]{2,1,0:T(8,128)(2,1)S(1)}, bf16[4,128,128]{2,1,0:T(8,128)(2,1)S(1)}, u32[]{:S(2)}, u32[]{:S(2)}) collective-permute-start(bf16[4,128,128]{2,1,0:T(8,128)(2,1)S(1)} %weights.1.refs_0_), channel_id=1, source_target_pairs={{0,32},{16,48},{32,0},{48,16},{64,96},{80,112},{96,64},{112,80},{1... | collective-permute-start | bytes 393224 | tf_op jit(solution)/shard_map/ppermute | solution.py:160
  43.8 11.6 %all-to-all-start.1 = ((bf16[8,4,16,128]{3,2,1,0:T(8,128)(2,1)}), bf16[8,4,16,128]{3,2,1,0:T(8,128)(2,1)S(1)}, u32[]{:S(2)}, u32[]{:S(2)}) async-start(bf16[8,4,16,128]{3,2,1,0:T(8,128)(2,1)} %diag.1), calls=%async_computation.1 | async-start | bytes 262144 | tf_op jit(solution)/shard_map/all_to_all | solution.py:205

commit v8 on v7

--- a/solution.py
+++ b/solution.py
@@ -35,8 +35,8 @@
     )
 
 
-def gram_kernel(poles, share, at_ref, count_ref, panel_ref, *out_refs):
-    pole, col = at_ref[0], at_ref[1]
+def gram_kernel(poles, share, count_ref, panel_ref, *out_refs):
+    pole, col = lax.axis_index("pole"), lax.axis_index("col")
     owned, block = panel_ref.shape[0], panel_ref.shape[2]
     for k, out_ref in enumerate(out_refs):
         for t in range(share):
@@ -74,9 +74,9 @@
     out_ref[...] = (a_ref[...].astype(F32) + b_ref[...].astype(F32)).astype(BF16)
 
 
-def prep_kernel(share, at_ref, w_ref, count_ref, *refs):
+def prep_kernel(share, w_ref, count_ref, *refs):
     *got_refs, m_ref, base_ref, gain_ref, wide_ref, flip_ref = refs
-    pole, col = at_ref[0], at_ref[1]
+    pole, col = lax.axis_index("pole"), lax.axis_index("col")
     block = m_ref.shape[1]
     owned = share * len(got_refs)
     for t in range(share):
@@ -103,10 +103,7 @@
         g = g_ref[t // 2, t % 2]
         v = dot(g, wide_ref[t]) * gain_ref[t]
         v = jnp.concatenate([v[:, k * block:(k + 1) * block] for k in range(half)], axis=0)
-        hi = v.astype(BF16)
-        lo = (v - hi.astype(F32)).astype(BF16)
-        flip = flip_ref[t]
-        d = (base_ref[t] + dot(flip, hi) + dot(flip, lo)).astype(BF16)
+        d = (base_ref[t] + dot(flip_ref[t], v.astype(BF16))).astype(BF16)
         for p in range(out_ref.shape[0]):
             out_ref[p, t] = d[p * chunk:(p + 1) * chunk]
 
@@ -119,9 +116,9 @@
             out_ref[col ^ slot(share, x, t)] = d.astype(BF16)
 
 
-def density_kernel(poles, share, at_ref, count_ref, moved_ref, *refs):
+def density_kernel(poles, share, count_ref, moved_ref, *refs):
     *m_refs, out_ref = refs
-    pole, col = at_ref[0], at_ref[1]
+    pole, col = lax.axis_index("pole"), lax.axis_index("col")
     owned, block = moved_ref.shape[0], moved_ref.shape[2]
     for k, m_ref in enumerate(m_refs):
         for t in range(share):
@@ -139,7 +136,6 @@
     half = poles // 2
     share = owned // half
     chunk = block // poles
-    at = jnp.stack([pole_at, col_at]).astype(jnp.int32)
     smem = pl.BlockSpec(memory_space=pltpu.SMEM)
     vmem = pl.BlockSpec(memory_space=pltpu.VMEM)
     shape = lambda *s: jax.ShapeDtypeStruct(s, BF16)
@@ -166,9 +162,9 @@
     )(pivot_inverse[0])
     sent = call(
         functools.partial(gram_kernel, poles, share), "gram",
-        [smem, smem, vmem], [shape(share, block, block)] * half,
+        [smem, vmem], [shape(share, block, block)] * half,
         2 * owned * rows * block * block,
-    )(at, row_count, panel)
+    )(row_count, panel)
     grams = [sent[0]] + [swap(sent[k], 2 * k) for k in range(1, half)]
     inverses = [turned[0]] + [swap(turned[k], 2 * k) for k in range(1, half)]
 
@@ -190,9 +186,9 @@
 
     wide = shape(share, block, half * block)
     mhalf, base, gain, wide, flip = call(
-        functools.partial(prep_kernel, share), "prep", [smem] * 3 + [vmem] * half,
+        functools.partial(prep_kernel, share), "prep", [smem] * 2 + [vmem] * half,
         [shape(share, block, block), jax.ShapeDtypeStruct((share, block, block), F32), jax.ShapeDtypeStruct((share, 1, half * block), F32), wide, wide],
-    )(at, pole_weight, row_count, *inverses)
+    )(pole_weight, row_count, *inverses)
     mfull = call(add_kernel, "weights", [vmem] * 2, [shape(share, block, block)])(mhalf, swap(mhalf, 1))[0]
     mparts = [mfull] + [swap(mfull, 2 * k) for k in range(1, half)]
 
@@ -207,9 +203,9 @@
 
     density = call(
         functools.partial(density_kernel, poles, share), "density",
-        [smem, smem, vmem] + [vmem] * half, [shape(owned, rows, block)],
+        [smem, vmem] + [vmem] * half, [shape(owned, rows, block)],
         2 * owned * rows * block * block,
-    )(at, row_count, moved, *mparts)[0]
+    )(row_count, moved, *mparts)[0]
     return density, diag
 
 

time: 56.3 us -> 56.1 us (level)
  no operation moved by 1% of the time
where the time goes in v8:
time: 56.1 us; the launch traced here: 55.8 us
  starting transfers between devices  34.7 us (62%)
  waiting for transfers between devices  13.7 us (24%)
  Pallas kernels  6.68 us (12%)
  between operations  0.75 us (1%)
    ppermute x11, starting transfers between devices, swap(): return lax.ppermute(x, 'pole', [(i, i ^ k) for i in range(poles)])  16.8 us
    all_to_all x1, starting transfers between devices, shards(): moved = lax.all_to_all(panel, 'col', 0, 0, tiled=True)  8.11 us
    ppermute x11, waiting for transfers between devices, swap(): return lax.ppermute(x, 'pole', [(i, i ^ k) for i in range(poles)])  6.04 us
    all_to_all x1, starting transfers between devices, shards(): part = lax.all_to_all(part, 'pole', 0, 0, tiled=True)  5.19 us
    ppermute x3, starting transfers between devices, shift(): return lax.ppermute(x, ('pole', 'col'), pairs)  4.5 us
    all_to_all x1, waiting for transfers between devices, shards(): part = lax.all_to_all(part, 'pole', 0, 0, tiled=True)  4.09 us
    ppermute x3, waiting for transfers between devices, shift(): return lax.ppermute(x, ('pole', 'col'), pairs)  2.28 us
    pallas_call x1, Pallas kernels, shards(): call(functools.partial(density_kernel, poles, share), 'density', [smem, v...  2.27 us
  transfers between devices with their start and end apart: 17, of which 7 were waited for; matrix products, arithmetic and copies ran while one was open for 0% of the time, Pallas kernels for 11%

profile of v8, /device:TPU:0, one launch (start us, length us, event | category | flops | bytes accessed | tf_op | source)
XLA Modules:
  0.0 55.8 jit_solution(16295327023598274234)
XLA Ops:
  0.6 8.1 %all-to-all-start = ((bf16[16,384,128]{2,1,0:T(8,128)(2,1)}), bf16[16,384,128]{2,1,0:T(8,128)(2,1)S(1)}, u32[]{:S(2)}, u32[]{:S(2)}) async-start(bf16[16,384,128]{2,1,0:T(8,128)(2,1)} %panel_ref.1), calls=%async_computation | async-start | bytes 3145728 | tf_op jit(solution)/shard_map/all_to_all | solution.py:158
  8.8 0.0 copy-start.1
  8.8 1.2 %gram.1 = (bf16[4,128,128]{2,1,0:T(8,128)(2,1)S(1)}, bf16[4,128,128]{2,1,0:T(8,128)(2,1)S(1)}, bf16[4,128,128]{2,1,0:T(8,128)(2,1)S(1)}, bf16[4,128,128]{2,1,0:T(8,128)(2,1)S(1)}) custom-call(s32[256]{0:T(256)S(1)} %copy-done.2, bf16[16,384,128]{2,1,0:T(8,128)(2,1)S(1)} %copy-done), custom_call_target="tpu_custom_call" | custom-call | flops 201326592 | bytes 1048576 | tf_op jit(solution)/shard_map/gram/pallas_call | solution.py:163
  10.0 1.6 %collective-permute-start.3 = (bf16[4,128,128]{2,1,0:T(8,128)(2,1)S(1)}, bf16[4,128,128]{2,1,0:T(8,128)(2,1)S(1)}, u32[]{:S(2)}, u32[]{:S(2)}) collective-permute-start(bf16[4,128,128]{2,1,0:T(8,128)(2,1)S(1)} %get-tuple-element.30), channel_id=1, source_target_pairs={{0,32},{16,48},{32,0},{48,16},{64,96},{80,112},{96,64},{112,80},{1... | collective-permute-start | bytes 393224 | tf_op jit(solution)/shard_map/ppermute | solution.py:156
  11.6 2.7 %collective-permute-start.4 = (bf16[4,128,128]{2,1,0:T(8,128)(2,1)S(1)}, bf16[4,128,128]{2,1,0:T(8,128)(2,1)S(1)}, u32[]{:S(2)}, u32[]{:S(2)}) collective-permute-start(bf16[4,128,128]{2,1,0:T(8,128)(2,1)S(1)} %get-tuple-element.31), channel_id=1, source_target_pairs={{0,64},{16,80},{32,96},{48,112},{64,0},{80,16},{96,32},{112,48},{1... | collective-permute-start | bytes 393224 | tf_op jit(solution)/shard_map/ppermute | solution.py:156
  14.3 0.5 collective-permute-start.5
  14.8 0.4 collective-permute-start
  15.2 3.9 %collective-permute-start.1 = (bf16[4,128,128]{2,1,0:T(8,128)(2,1)S(1)}, bf16[4,128,128]{2,1,0:T(8,128)(2,1)S(1)}, u32[]{:S(2)}, u32[]{:S(2)}) collective-permute-start(bf16[4,128,128]{2,1,0:T(8,128)(2,1)S(1)} %get-tuple-element.23), channel_id=1, source_target_pairs={{0,64},{16,80},{32,96},{48,112},{64,0},{80,16},{96,32},{112,48},{1... | collective-permute-start | bytes 393224 | tf_op jit(solution)/shard_map/ppermute | solution.py:156
  19.1 0.5 collective-permute-start.2
  19.6 1.8 %collective-permute-done.4.refs_2_ = bf16[4,128,128]{2,1,0:T(8,128)(2,1)S(1)} collective-permute-done((bf16[4,128,128]{2,1,0:T(8,128)(2,1)S(1)}, bf16[4,128,128]{2,1,0:T(8,128)(2,1)S(1)}, u32[]{:S(2)}, u32[]{:S(2)}) %collective-permute-start.4) | collective-permute-done | bytes 131104 | tf_op jit(solution)/shard_map/ppermute | solution.py:156
  21.4 2.9 %collective-permute-done.5.refs_3_ = bf16[4,128,128]{2,1,0:T(8,128)(2,1)S(1)} collective-permute-done((bf16[4,128,128]{2,1,0:T(8,128)(2,1)S(1)}, bf16[4,128,128]{2,1,0:T(8,128)(2,1)S(1)}, u32[]{:S(2)}, u32[]{:S(2)}) %collective-permute-start.5) | collective-permute-done | bytes 131104 | tf_op jit(solution)/shard_map/ppermute | solution.py:156
  24.3 0.1 gsum.1
  24.4 0.1 collective-permute-start.6
  24.5 1.2 %collective-permute-done.6.b_ref = bf16[2,128,128]{2,1,0:T(8,128)(2,1)S(1)} collective-permute-done((bf16[2,128,128]{2,1,0:T(8,128)(2,1)S(1)}, bf16[2,128,128]{2,1,0:T(8,128)(2,1)S(1)}, u32[]{:S(2)}, u32[]{:S(2)}) %collective-permute-start.6) | collective-permute-done | bytes 65568 | tf_op jit(solution)/shard_map/ppermute | solution.py:174
  25.7 3.6 %collective-permute-start.8 = (bf16[2,128,128]{2,1,0:T(8,128)(2,1)S(1)}, bf16[2,128,128]{2,1,0:T(8,128)(2,1)S(1)}, u32[]{:S(2)}, u32[]{:S(2)}) collective-permute-start(bf16[2,128,128]{2,1,0:T(8,128)(2,1)S(1)} %get-tuple-element.35), channel_id=1, source_target_pairs={{0,8},{1,9},{2,10},{3,11},{4,12},{5,13},{6,14},{7,15},{8,0},{9,1},... | collective-permute-start | bytes 196616 | tf_op jit(solution)/shard_map/ppermute | solution.py:179
  29.3 0.3 collective-permute-start.7
  29.6 0.8 %collective-permute-start.9 = (bf16[2,128,128]{2,1,0:T(8,128)(2,1)S(1)}, bf16[2,128,128]{2,1,0:T(8,128)(2,1)S(1)}, u32[]{:S(2)}, u32[]{:S(2)}) collective-permute-start(bf16[2,128,128]{2,1,0:T(8,128)(2,1)S(1)} %get-tuple-element.36.a0_ref), channel_id=1, source_target_pairs={{0,16},{16,0},{32,48},{48,32},{64,80},{80,64},{96,112},{112,96},{1... | collective-permute-start | bytes 196616 | tf_op jit(solution)/shard_map/ppermute | solution.py:156
  30.4 0.8 %prep.1 = (bf16[4,128,128]{2,1,0:T(8,128)(2,1)S(1)}, f32[4,128,128]{2,1,0:T(8,128)S(1)}, f32[4,1,512]{2,1,0:T(1,128)S(1)}, bf16[4,128,512]{2,1,0:T(8,128)(2,1)S(1)}, bf16[4,128,512]{2,1,0:T(8,128)(2,1)S(1)}) custom-call(f32[8]{0:T(128)S(1)} %copy-done.3, s32[256]{0:T(256)S(1)} %copy-done.2, bf16[4,128,128]{2,1,0:T(8,128)(2,1)S(1)} %get-tuple-element.21.refs_0_, ...), custom_call_target="tpu_custom_call" | custom-call | bytes 2629632 | tf_op jit(solution)/shard_map/prep/pallas_call | solution.py:188
  31.2 1.3 %collective-permute-start.11 = (bf16[4,128,128]{2,1,0:T(8,128)(2,1)S(1)}, bf16[4,128,128]{2,1,0:T(8,128)(2,1)S(1)}, u32[]{:S(2)}, u32[]{:S(2)}) collective-permute-start(bf16[4,128,128]{2,1,0:T(8,128)(2,1)S(1)} %get-tuple-element.38.a_ref), channel_id=1, source_target_pairs={{0,16},{16,0},{32,48},{48,32},{64,80},{80,64},{96,112},{112,96},{1... | collective-permute-start | bytes 393224 | tf_op jit(solution)/shard_map/ppermute | solution.py:156
  32.5 0.8 %collective-permute-done.8.b1_ref = bf16[2,128,128]{2,1,0:T(8,128)(2,1)S(1)} collective-permute-done((bf16[2,128,128]{2,1,0:T(8,128)(2,1)S(1)}, bf16[2,128,128]{2,1,0:T(8,128)(2,1)S(1)}, u32[]{:S(2)}, u32[]{:S(2)}) %collective-permute-start.8) | collective-permute-done | bytes 65568 | tf_op jit(solution)/shard_map/ppermute | solution.py:179
  33.3 1.5 %collective-permute-done.7.b0_ref = bf16[2,128,128]{2,1,0:T(8,128)(2,1)S(1)} collective-permute-done((bf16[2,128,128]{2,1,0:T(8,128)(2,1)S(1)}, bf16[2,128,128]{2,1,0:T(8,128)(2,1)S(1)}, u32[]{:S(2)}, u32[]{:S(2)}) %collective-permute-start.7) | collective-permute-done | bytes 65568 | tf_op jit(solution)/shard_map/ppermute | solution.py:179
  34.8 0.7 %collective-permute-start.10 = (bf16[2,2,128,128]{3,2,1,0:T(8,128)(2,1)S(1)}, bf16[2,2,128,128]{3,2,1,0:T(8,128)(2,1)S(1)}, u32[]{:S(2)}, u32[]{:S(2)}) collective-permute-start(bf16[2,2,128,128]{3,2,1,0:T(8,128)(2,1)S(1)} %gown.1), channel_id=1, source_target_pairs={{0,0},{1,1},{2,2},{3,3},{4,4},{5,5},{6,6},{7,7},{8,8},{9,9},{10,10... | collective-permute-start | bytes 393224 | tf_op jit(solution)/shard_map/ppermute | solution.py:179
  35.5 1.3 %collective-permute-done.11.b_ref = bf16[4,128,128]{2,1,0:T(8,128)(2,1)S(1)} collective-permute-done((bf16[4,128,128]{2,1,0:T(8,128)(2,1)S(1)}, bf16[4,128,128]{2,1,0:T(8,128)(2,1)S(1)}, u32[]{:S(2)}, u32[]{:S(2)}) %collective-permute-start.11) | collective-permute-done | bytes 131104 | tf_op jit(solution)/shard_map/ppermute | solution.py:156
  36.8 4.2 %collective-permute-start.14 = (bf16[4,128,128]{2,1,0:T(8,128)(2,1)S(1)}, bf16[4,128,128]{2,1,0:T(8,128)(2,1)S(1)}, u32[]{:S(2)}, u32[]{:S(2)}) collective-permute-start(bf16[4,128,128]{2,1,0:T(8,128)(2,1)S(1)} %weights.1.refs_0_), channel_id=1, source_target_pairs={{0,96},{16,112},{32,64},{48,80},{64,32},{80,48},{96,0},{112,16},{1... | collective-permute-start | bytes 393224 | tf_op jit(solution)/shard_map/ppermute | solution.py:156
  41.1 0.2 collective-permute-start.13
  41.2 0.8 %collective-permute-start.12 = (bf16[4,128,128]{2,1,0:T(8,128)(2,1)S(1)}, bf16[4,128,128]{2,1,0:T(8,128)(2,1)S(1)}, u32[]{:S(2)}, u32[]{:S(2)}) collective-permute-start(bf16[4,128,128]{2,1,0:T(8,128)(2,1)S(1)} %weights.1.refs_0_), channel_id=1, source_target_pairs={{0,32},{16,48},{32,0},{48,16},{64,96},{80,112},{96,64},{112,80},{1... | collective-permute-start | bytes 393224 | tf_op jit(solution)/shard_map/ppermute | solution.py:156
  42.0 1.6 %diag.1 = bf16[8,4,16,128]{3,2,1,0:T(8,128)(2,1)} custom-call(f32[4,128,128]{2,1,0:T(8,128)S(1)} %get-tuple-element.25.base_ref, f32[4,1,512]{2,1,0:T(1,128)S(1)} %get-tuple-element.26.gain_ref, bf16[4,128,512]{2,1,0:T(8,128)(2,1)S(1)} %get-tuple-element.27.wide_ref, bf16[4,128,512]{2,1,0:T(8,128)(2,1)S(1)} %get-tuple-element.28.flip_ref, ...), custom_call_target="tpu_custom_call" | custom-call | flops 201326592 | bytes 262144 | tf_op jit(solution)/shard_map/diag/pallas_call | solution.py:195
  43.6 5.2 %all-to-all-start.1 = ((bf16[8,4,16,128]{3,2,1,0:T(8,128)(2,1)}), bf16[8,4,16,128]{3,2,1,0:T(8,128)(2,1)S(1)}, u32[]{:S(2)}, u32[]{:S(2)}) async-start(bf16[8,4,16,128]{3,2,1,0:T(8,128)(2,1)} %diag.1), calls=%async_computation.1 | async-start | bytes 262144 | tf_op jit(solution)/shard_map/all_to_all | solution.py:201
  48.8 0.0 collective-permute-done.13.refs_2_
  48.8 2.3 %density.1 = bf16[16,384,128]{2,1,0:T(8,128)(2,1)} custom-call(s32[256]{0:T(256)S(1)} %copy-done.2, bf16[16,384,128]{2,1,0:T(8,128)(2,1)S(1)} %all-to-all-done.moved_ref, bf16[4,128,128]{2,1,0:T(8,128)(2,1)S(1)} %weights.1.refs_0_, bf16[4,128,128]{2,1,0:T(8,128)(2,1)S(1)} %collective-permute-done.12.refs_1_, ...), custom_call_target="tpu_custom_call" | custom-call | flops 201326592 | bytes 3145728 | tf_op jit(solution)/shard_map/density/pallas_call | solution.py:204
  51.1 4.1 %all-to-all-done.1.got_ref = bf16[8,4,16,128]{3,2,1,0:T(8,128)(2,1)S(1)} async-done(((bf16[8,4,16,128]{3,2,1,0:T(8,128)(2,1)}), bf16[8,4,16,128]{3,2,1,0:T(8,128)(2,1)S(1)}, u32[]{:S(2)}, u32[]{:S(2)}) %all-to-all-start.1) | async-done | bytes 131104 | tf_op jit(solution)/shard_map/all_to_all | solution.py:201
  55.2 0.6 %finish.1 = bf16[16,16,128]{2,1,0:T(8,128)(2,1)} custom-call(bf16[8,4,16,128]{3,2,1,0:T(8,128)(2,1)S(1)} %all-to-all-done.1.got_ref), custom_call_target="tpu_custom_call" | custom-call | bytes 131072 | tf_op jit(solution)/shard_map/finish/pallas_call | solution.py:202
  (20 shorter events, 0.2 us)
Async XLA Ops:
  0.6 8.1 %copy-start = (bf16[16,384,128]{2,1,0:T(8,128)(2,1)S(1)}, bf16[16,384,128]{2,1,0:T(8,128)(2,1)}, u32[]{:S(2)}) copy-start(bf16[16,384,128]{2,1,0:T(8,128)(2,1)} %panel_ref.1) | copy-start | bytes 4718596
  0.6 8.1 %copy-start.2 = (s32[256]{0:T(256)S(1)}, s32[256]{0:T(256)}, u32[]{:S(2)}) copy-start(s32[256]{0:T(256)} %count_ref.5) | copy-start | bytes 3076
  0.6 42.9 %all-to-all-start = ((bf16[16,384,128]{2,1,0:T(8,128)(2,1)}), bf16[16,384,128]{2,1,0:T(8,128)(2,1)S(1)}, u32[]{:S(2)}, u32[]{:S(2)}) async-start(bf16[16,384,128]{2,1,0:T(8,128)(2,1)} %panel_ref.1), calls=%async_computation | async-start | bytes 3145728 | tf_op jit(solution)/shard_map/all_to_all | solution.py:158
  8.8 6.0 %copy-start.1 = (bf16[1,16,128,128]{3,2,1,0:T(8,128)(2,1)S(1)}, bf16[1,16,128,128]{3,2,1,0:T(8,128)(2,1)}, u32[]{:S(2)}) copy-start(bf16[1,16,128,128]{3,2,1,0:T(8,128)(2,1)} %param.5) | copy-start | bytes 1572868
  8.8 21.6 %copy-start.3 = (f32[8]{0:T(128)S(1)}, f32[8]{0:T(128)}, u32[]{:S(2)}) copy-start(f32[8]{0:T(128)} %w_ref.1) | copy-start | bytes 100
  10.0 9.1 %collective-permute-start.3 = (bf16[4,128,128]{2,1,0:T(8,128)(2,1)S(1)}, bf16[4,128,128]{2,1,0:T(8,128)(2,1)S(1)}, u32[]{:S(2)}, u32[]{:S(2)}) collective-permute-start(bf16[4,128,128]{2,1,0:T(8,128)(2,1)S(1)} %get-tuple-element.30), channel_id=1, source_target_pairs={{0,32},{16,48},{32,0},{48,16},{64,96},{80,112},{96,64},{112,80},{1... | collective-permute-start | bytes 393224 | tf_op jit(solution)/shard_map/ppermute | solution.py:156
  11.6 9.9 %collective-permute-start.4 = (bf16[4,128,128]{2,1,0:T(8,128)(2,1)S(1)}, bf16[4,128,128]{2,1,0:T(8,128)(2,1)S(1)}, u32[]{:S(2)}, u32[]{:S(2)}) collective-permute-start(bf16[4,128,128]{2,1,0:T(8,128)(2,1)S(1)} %get-tuple-element.31), channel_id=1, source_target_pairs={{0,64},{16,80},{32,96},{48,112},{64,0},{80,16},{96,32},{112,48},{1... | collective-permute-start | bytes 393224 | tf_op jit(solution)/shard_map/ppermute | solution.py:156
  14.3 10.0 %collective-permute-start.5 = (bf16[4,128,128]{2,1,0:T(8,128)(2,1)S(1)}, bf16[4,128,128]{2,1,0:T(8,128)(2,1)S(1)}, u32[]{:S(2)}, u32[]{:S(2)}) collective-permute-start(bf16[4,128,128]{2,1,0:T(8,128)(2,1)S(1)} %get-tuple-element.32), channel_id=1, source_target_pairs={{0,96},{16,112},{32,64},{48,80},{64,32},{80,48},{96,0},{112,16},{1... | collective-permute-start | bytes 393224 | tf_op jit(solution)/shard_map/ppermute | solution.py:156
  14.8 14.8 %collective-permute-start = (bf16[4,128,128]{2,1,0:T(8,128)(2,1)S(1)}, bf16[4,128,128]{2,1,0:T(8,128)(2,1)S(1)}, u32[]{:S(2)}, u32[]{:S(2)}) collective-permute-start(bf16[4,128,128]{2,1,0:T(8,128)(2,1)S(1)} %get-tuple-element.22), channel_id=1, source_target_pairs={{0,32},{16,48},{32,0},{48,16},{64,96},{80,112},{96,64},{112,80},{1... | collective-permute-start | bytes 393224 | tf_op jit(solution)/shard_map/ppermute | solution.py:156
  15.2 15.2 %collective-permute-start.1 = (bf16[4,128,128]{2,1,0:T(8,128)(2,1)S(1)}, bf16[4,128,128]{2,1,0:T(8,128)(2,1)S(1)}, u32[]{:S(2)}, u32[]{:S(2)}) collective-permute-start(bf16[4,128,128]{2,1,0:T(8,128)(2,1)S(1)} %get-tuple-element.23), channel_id=1, source_target_pairs={{0,64},{16,80},{32,96},{48,112},{64,0},{80,16},{96,32},{112,48},{1... | collective-permute-start | bytes 393224 | tf_op jit(solution)/shard_map/ppermute | solution.py:156
  19.1 11.2 %collective-permute-start.2 = (bf16[4,128,128]{2,1,0:T(8,128)(2,1)S(1)}, bf16[4,128,128]{2,1,0:T(8,128)(2,1)S(1)}, u32[]{:S(2)}, u32[]{:S(2)}) collective-permute-start(bf16[4,128,128]{2,1,0:T(8,128)(2,1)S(1)} %get-tuple-element.24), channel_id=1, source_target_pairs={{0,96},{16,112},{32,64},{48,80},{64,32},{80,48},{96,0},{112,16},{1... | collective-permute-start | bytes 393224 | tf_op jit(solution)/shard_map/ppermute | solution.py:156
  24.4 1.3 %collective-permute-start.6 = (bf16[2,128,128]{2,1,0:T(8,128)(2,1)S(1)}, bf16[2,128,128]{2,1,0:T(8,128)(2,1)S(1)}, u32[]{:S(2)}, u32[]{:S(2)}) collective-permute-start(bf16[2,128,128]{2,1,0:T(8,128)(2,1)S(1)} %get-tuple-element.34), channel_id=1, source_target_pairs={{0,1},{1,0},{2,3},{3,2},{4,5},{5,4},{6,7},{7,6},{8,9},{9,8},{10,11... | collective-permute-start | bytes 196616 | tf_op jit(solution)/shard_map/ppermute | solution.py:174
  25.7 7.6 %collective-permute-start.8 = (bf16[2,128,128]{2,1,0:T(8,128)(2,1)S(1)}, bf16[2,128,128]{2,1,0:T(8,128)(2,1)S(1)}, u32[]{:S(2)}, u32[]{:S(2)}) collective-permute-start(bf16[2,128,128]{2,1,0:T(8,128)(2,1)S(1)} %get-tuple-element.35), channel_id=1, source_target_pairs={{0,8},{1,9},{2,10},{3,11},{4,12},{5,13},{6,14},{7,15},{8,0},{9,1},... | collective-permute-start | bytes 196616 | tf_op jit(solution)/shard_map/ppermute | solution.py:179
  29.3 5.5 %collective-permute-start.7 = (bf16[2,128,128]{2,1,0:T(8,128)(2,1)S(1)}, bf16[2,128,128]{2,1,0:T(8,128)(2,1)S(1)}, u32[]{:S(2)}, u32[]{:S(2)}) collective-permute-start(bf16[2,128,128]{2,1,0:T(8,128)(2,1)S(1)} %get-tuple-element.35), channel_id=1, source_target_pairs={{0,24},{1,25},{2,26},{3,27},{4,28},{5,29},{6,30},{7,31},{8,16},{9,... | collective-permute-start | bytes 196616 | tf_op jit(solution)/shard_map/ppermute | solution.py:179
  29.6 5.2 %collective-permute-start.9 = (bf16[2,128,128]{2,1,0:T(8,128)(2,1)S(1)}, bf16[2,128,128]{2,1,0:T(8,128)(2,1)S(1)}, u32[]{:S(2)}, u32[]{:S(2)}) collective-permute-start(bf16[2,128,128]{2,1,0:T(8,128)(2,1)S(1)} %get-tuple-element.36.a0_ref), channel_id=1, source_target_pairs={{0,16},{16,0},{32,48},{48,32},{64,80},{80,64},{96,112},{112,96},{1... | collective-permute-start | bytes 196616 | tf_op jit(solution)/shard_map/ppermute | solution.py:156
  31.2 5.6 %collective-permute-start.11 = (bf16[4,128,128]{2,1,0:T(8,128)(2,1)S(1)}, bf16[4,128,128]{2,1,0:T(8,128)(2,1)S(1)}, u32[]{:S(2)}, u32[]{:S(2)}) collective-permute-start(bf16[4,128,128]{2,1,0:T(8,128)(2,1)S(1)} %get-tuple-element.38.a_ref), channel_id=1, source_target_pairs={{0,16},{16,0},{32,48},{48,32},{64,80},{80,64},{96,112},{112,96},{1... | collective-permute-start | bytes 393224 | tf_op jit(solution)/shard_map/ppermute | solution.py:156
  34.8 7.2 %collective-permute-start.10 = (bf16[2,2,128,128]{3,2,1,0:T(8,128)(2,1)S(1)}, bf16[2,2,128,128]{3,2,1,0:T(8,128)(2,1)S(1)}, u32[]{:S(2)}, u32[]{:S(2)}) collective-permute-start(bf16[2,2,128,128]{3,2,1,0:T(8,128)(2,1)S(1)} %gown.1), channel_id=1, source_target_pairs={{0,0},{1,1},{2,2},{3,3},{4,4},{5,5},{6,6},{7,7},{8,8},{9,9},{10,10... | collective-permute-start | bytes 393224 | tf_op jit(solution)/shard_map/ppermute | solution.py:179
  36.8 12.0 %collective-permute-start.14 = (bf16[4,128,128]{2,1,0:T(8,128)(2,1)S(1)}, bf16[4,128,128]{2,1,0:T(8,128)(2,1)S(1)}, u32[]{:S(2)}, u32[]{:S(2)}) collective-permute-start(bf16[4,128,128]{2,1,0:T(8,128)(2,1)S(1)} %weights.1.refs_0_), channel_id=1, source_target_pairs={{0,96},{16,112},{32,64},{48,80},{64,32},{80,48},{96,0},{112,16},{1... | collective-permute-start | bytes 393224 | tf_op jit(solution)/shard_map/ppermute | solution.py:156
  41.1 7.8 %collective-permute-start.13 = (bf16[4,128,128]{2,1,0:T(8,128)(2,1)S(1)}, bf16[4,128,128]{2,1,0:T(8,128)(2,1)S(1)}, u32[]{:S(2)}, u32[]{:S(2)}) collective-permute-start(bf16[4,128,128]{2,1,0:T(8,128)(2,1)S(1)} %weights.1.refs_0_), channel_id=1, source_target_pairs={{0,64},{16,80},{32,96},{48,112},{64,0},{80,16},{96,32},{112,48},{1... | collective-permute-start | bytes 393224 | tf_op jit(solution)/shard_map/ppermute | solution.py:156
  41.2 7.6 %collective-permute-start.12 = (bf16[4,128,128]{2,1,0:T(8,128)(2,1)S(1)}, bf16[4,128,128]{2,1,0:T(8,128)(2,1)S(1)}, u32[]{:S(2)}, u32[]{:S(2)}) collective-permute-start(bf16[4,128,128]{2,1,0:T(8,128)(2,1)S(1)} %weights.1.refs_0_), channel_id=1, source_target_pairs={{0,32},{16,48},{32,0},{48,16},{64,96},{80,112},{96,64},{112,80},{1... | collective-permute-start | bytes 393224 | tf_op jit(solution)/shard_map/ppermute | solution.py:156
  43.6 11.6 %all-to-all-start.1 = ((bf16[8,4,16,128]{3,2,1,0:T(8,128)(2,1)}), bf16[8,4,16,128]{3,2,1,0:T(8,128)(2,1)S(1)}, u32[]{:S(2)}, u32[]{:S(2)}) async-start(bf16[8,4,16,128]{3,2,1,0:T(8,128)(2,1)} %diag.1), calls=%async_computation.1 | async-start | bytes 262144 | tf_op jit(solution)/shard_map/all_to_all | solution.py:201

commit v9 on v8

--- a/solution.py
+++ b/solution.py
@@ -99,11 +99,12 @@
     block = base_ref.shape[1]
     half = wide_ref.shape[2] // block
     chunk = out_ref.shape[2]
+    middle = []
     for t in range(share):
-        g = g_ref[t // 2, t % 2]
-        v = dot(g, wide_ref[t]) * gain_ref[t]
-        v = jnp.concatenate([v[:, k * block:(k + 1) * block] for k in range(half)], axis=0)
-        d = (base_ref[t] + dot(flip_ref[t], v.astype(BF16))).astype(BF16)
+        v = (dot(g_ref[t // 2, t % 2], wide_ref[t]) * gain_ref[t]).astype(BF16)
+        middle.append(jnp.concatenate([v[:, k * block:(k + 1) * block] for k in range(half)], axis=0))
+    for t, v in enumerate(middle):
+        d = (base_ref[t] + dot(flip_ref[t], v)).astype(BF16)
         for p in range(out_ref.shape[0]):
             out_ref[p, t] = d[p * chunk:(p + 1) * chunk]
 

time: 56.1 us -> 55.7 us (level)
  transfers between devices with their start and end apart: 17 -> 17, of which waited for: 7 -> 8; matrix products, arithmetic and copies ran while one was open for 0% -> 0% of each run, Pallas kernels for 11% -> 10%
where the time goes in v9:
time: 55.7 us; the launch traced here: 55.4 us
  starting transfers between devices  34.8 us (62%)
  waiting for transfers between devices  13.7 us (25%)
  Pallas kernels  6.21 us (11%)
  between operations  0.75 us (1%)
    ppermute x11, starting transfers between devices, swap(): return lax.ppermute(x, 'pole', [(i, i ^ k) for i in range(poles)])  16.8 us
    all_to_all x1, starting transfers between devices, shards(): moved = lax.all_to_all(panel, 'col', 0, 0, tiled=True)  8.11 us
    ppermute x11, waiting for transfers between devices, swap(): return lax.ppermute(x, 'pole', [(i, i ^ k) for i in range(poles)])  6.49 us
    all_to_all x1, starting transfers between devices, shards(): part = lax.all_to_all(part, 'pole', 0, 0, tiled=True)  5.21 us
    ppermute x3, starting transfers between devices, shift(): return lax.ppermute(x, ('pole', 'col'), pairs)  4.5 us
    all_to_all x1, waiting for transfers between devices, shards(): part = lax.all_to_all(part, 'pole', 0, 0, tiled=True)  3.64 us
    ppermute x3, waiting for transfers between devices, shift(): return lax.ppermute(x, ('pole', 'col'), pairs)  2.28 us
    pallas_call x1, Pallas kernels, shards(): call(functools.partial(density_kernel, poles, share), 'density', [smem, v...  2.27 us
  transfers between devices with their start and end apart: 17, of which 8 were waited for; matrix products, arithmetic and copies ran while one was open for 0% of the time, Pallas kernels for 10%

profile of v9, /device:TPU:0, one launch (start us, length us, event | category | flops | bytes accessed | tf_op | source)
XLA Modules:
  0.0 55.4 jit_solution(6880377812632887682)
XLA Ops:
  0.6 8.1 %all-to-all-start = ((bf16[16,384,128]{2,1,0:T(8,128)(2,1)}), bf16[16,384,128]{2,1,0:T(8,128)(2,1)S(1)}, u32[]{:S(2)}, u32[]{:S(2)}) async-start(bf16[16,384,128]{2,1,0:T(8,128)(2,1)} %panel_ref.1), calls=%async_computation | async-start | bytes 3145728 | tf_op jit(solution)/shard_map/all_to_all | solution.py:159
  8.8 0.0 copy-start.3
  8.8 1.2 %gram.1 = (bf16[4,128,128]{2,1,0:T(8,128)(2,1)S(1)}, bf16[4,128,128]{2,1,0:T(8,128)(2,1)S(1)}, bf16[4,128,128]{2,1,0:T(8,128)(2,1)S(1)}, bf16[4,128,128]{2,1,0:T(8,128)(2,1)S(1)}) custom-call(s32[256]{0:T(256)S(1)} %copy-done.2, bf16[16,384,128]{2,1,0:T(8,128)(2,1)S(1)} %copy-done), custom_call_target="tpu_custom_call" | custom-call | flops 201326592 | bytes 1048576 | tf_op jit(solution)/shard_map/gram/pallas_call | solution.py:164
  10.0 1.6 %collective-permute-start.3 = (bf16[4,128,128]{2,1,0:T(8,128)(2,1)S(1)}, bf16[4,128,128]{2,1,0:T(8,128)(2,1)S(1)}, u32[]{:S(2)}, u32[]{:S(2)}) collective-permute-start(bf16[4,128,128]{2,1,0:T(8,128)(2,1)S(1)} %get-tuple-element.30), channel_id=1, source_target_pairs={{0,32},{16,48},{32,0},{48,16},{64,96},{80,112},{96,64},{112,80},{1... | collective-permute-start | bytes 393224 | tf_op jit(solution)/shard_map/ppermute | solution.py:157
  11.6 2.7 %collective-permute-start.4 = (bf16[4,128,128]{2,1,0:T(8,128)(2,1)S(1)}, bf16[4,128,128]{2,1,0:T(8,128)(2,1)S(1)}, u32[]{:S(2)}, u32[]{:S(2)}) collective-permute-start(bf16[4,128,128]{2,1,0:T(8,128)(2,1)S(1)} %get-tuple-element.31), channel_id=1, source_target_pairs={{0,64},{16,80},{32,96},{48,112},{64,0},{80,16},{96,32},{112,48},{1... | collective-permute-start | bytes 393224 | tf_op jit(solution)/shard_map/ppermute | solution.py:157
  14.3 0.5 collective-permute-start.5
  14.8 0.4 collective-permute-start
  15.2 3.9 %collective-permute-start.1 = (bf16[4,128,128]{2,1,0:T(8,128)(2,1)S(1)}, bf16[4,128,128]{2,1,0:T(8,128)(2,1)S(1)}, u32[]{:S(2)}, u32[]{:S(2)}) collective-permute-start(bf16[4,128,128]{2,1,0:T(8,128)(2,1)S(1)} %get-tuple-element.23), channel_id=1, source_target_pairs={{0,64},{16,80},{32,96},{48,112},{64,0},{80,16},{96,32},{112,48},{1... | collective-permute-start | bytes 393224 | tf_op jit(solution)/shard_map/ppermute | solution.py:157
  19.1 0.5 collective-permute-start.2
  19.6 1.8 %collective-permute-done.4.refs_2_ = bf16[4,128,128]{2,1,0:T(8,128)(2,1)S(1)} collective-permute-done((bf16[4,128,128]{2,1,0:T(8,128)(2,1)S(1)}, bf16[4,128,128]{2,1,0:T(8,128)(2,1)S(1)}, u32[]{:S(2)}, u32[]{:S(2)}) %collective-permute-start.4) | collective-permute-done | bytes 131104 | tf_op jit(solution)/shard_map/ppermute | solution.py:157
  21.4 2.9 %collective-permute-done.5.refs_3_ = bf16[4,128,128]{2,1,0:T(8,128)(2,1)S(1)} collective-permute-done((bf16[4,128,128]{2,1,0:T(8,128)(2,1)S(1)}, bf16[4,128,128]{2,1,0:T(8,128)(2,1)S(1)}, u32[]{:S(2)}, u32[]{:S(2)}) %collective-permute-start.5) | collective-permute-done | bytes 131104 | tf_op jit(solution)/shard_map/ppermute | solution.py:157
  24.3 0.1 gsum.1
  24.4 0.1 collective-permute-start.6
  24.5 1.2 %collective-permute-done.6.b_ref = bf16[2,128,128]{2,1,0:T(8,128)(2,1)S(1)} collective-permute-done((bf16[2,128,128]{2,1,0:T(8,128)(2,1)S(1)}, bf16[2,128,128]{2,1,0:T(8,128)(2,1)S(1)}, u32[]{:S(2)}, u32[]{:S(2)}) %collective-permute-start.6) | collective-permute-done | bytes 65568 | tf_op jit(solution)/shard_map/ppermute | solution.py:175
  25.7 3.6 %collective-permute-start.8 = (bf16[2,128,128]{2,1,0:T(8,128)(2,1)S(1)}, bf16[2,128,128]{2,1,0:T(8,128)(2,1)S(1)}, u32[]{:S(2)}, u32[]{:S(2)}) collective-permute-start(bf16[2,128,128]{2,1,0:T(8,128)(2,1)S(1)} %get-tuple-element.35), channel_id=1, source_target_pairs={{0,8},{1,9},{2,10},{3,11},{4,12},{5,13},{6,14},{7,15},{8,0},{9,1},... | collective-permute-start | bytes 196616 | tf_op jit(solution)/shard_map/ppermute | solution.py:180
  29.3 0.3 collective-permute-start.7
  29.6 0.8 %collective-permute-start.9 = (bf16[2,128,128]{2,1,0:T(8,128)(2,1)S(1)}, bf16[2,128,128]{2,1,0:T(8,128)(2,1)S(1)}, u32[]{:S(2)}, u32[]{:S(2)}) collective-permute-start(bf16[2,128,128]{2,1,0:T(8,128)(2,1)S(1)} %get-tuple-element.36.a0_ref), channel_id=1, source_target_pairs={{0,16},{16,0},{32,48},{48,32},{64,80},{80,64},{96,112},{112,96},{1... | collective-permute-start | bytes 196616 | tf_op jit(solution)/shard_map/ppermute | solution.py:157
  30.4 0.8 %prep.1 = (bf16[4,128,128]{2,1,0:T(8,128)(2,1)S(1)}, f32[4,128,128]{2,1,0:T(8,128)S(1)}, f32[4,1,512]{2,1,0:T(1,128)S(1)}, bf16[4,128,512]{2,1,0:T(8,128)(2,1)S(1)}, bf16[4,128,512]{2,1,0:T(8,128)(2,1)S(1)}) custom-call(f32[8]{0:T(128)S(1)} %copy-done.3, s32[256]{0:T(256)S(1)} %copy-done.2, bf16[4,128,128]{2,1,0:T(8,128)(2,1)S(1)} %get-tuple-element.21.refs_0_, ...), custom_call_target="tpu_custom_call" | custom-call | bytes 2629632 | tf_op jit(solution)/shard_map/prep/pallas_call | solution.py:189
  31.2 1.3 %collective-permute-start.11 = (bf16[4,128,128]{2,1,0:T(8,128)(2,1)S(1)}, bf16[4,128,128]{2,1,0:T(8,128)(2,1)S(1)}, u32[]{:S(2)}, u32[]{:S(2)}) collective-permute-start(bf16[4,128,128]{2,1,0:T(8,128)(2,1)S(1)} %get-tuple-element.38.a_ref), channel_id=1, source_target_pairs={{0,16},{16,0},{32,48},{48,32},{64,80},{80,64},{96,112},{112,96},{1... | collective-permute-start | bytes 393224 | tf_op jit(solution)/shard_map/ppermute | solution.py:157
  32.5 0.8 %collective-permute-done.8.b1_ref = bf16[2,128,128]{2,1,0:T(8,128)(2,1)S(1)} collective-permute-done((bf16[2,128,128]{2,1,0:T(8,128)(2,1)S(1)}, bf16[2,128,128]{2,1,0:T(8,128)(2,1)S(1)}, u32[]{:S(2)}, u32[]{:S(2)}) %collective-permute-start.8) | collective-permute-done | bytes 65568 | tf_op jit(solution)/shard_map/ppermute | solution.py:180
  33.3 1.5 %collective-permute-done.7.b0_ref = bf16[2,128,128]{2,1,0:T(8,128)(2,1)S(1)} collective-permute-done((bf16[2,128,128]{2,1,0:T(8,128)(2,1)S(1)}, bf16[2,128,128]{2,1,0:T(8,128)(2,1)S(1)}, u32[]{:S(2)}, u32[]{:S(2)}) %collective-permute-start.7) | collective-permute-done | bytes 65568 | tf_op jit(solution)/shard_map/ppermute | solution.py:180
  34.8 0.7 %collective-permute-start.10 = (bf16[2,2,128,128]{3,2,1,0:T(8,128)(2,1)S(1)}, bf16[2,2,128,128]{3,2,1,0:T(8,128)(2,1)S(1)}, u32[]{:S(2)}, u32[]{:S(2)}) collective-permute-start(bf16[2,2,128,128]{3,2,1,0:T(8,128)(2,1)S(1)} %gown.1), channel_id=1, source_target_pairs={{0,0},{1,1},{2,2},{3,3},{4,4},{5,5},{6,6},{7,7},{8,8},{9,9},{10,10... | collective-permute-start | bytes 393224 | tf_op jit(solution)/shard_map/ppermute | solution.py:180
  35.5 1.3 %collective-permute-done.11.b_ref = bf16[4,128,128]{2,1,0:T(8,128)(2,1)S(1)} collective-permute-done((bf16[4,128,128]{2,1,0:T(8,128)(2,1)S(1)}, bf16[4,128,128]{2,1,0:T(8,128)(2,1)S(1)}, u32[]{:S(2)}, u32[]{:S(2)}) %collective-permute-start.11) | collective-permute-done | bytes 131104 | tf_op jit(solution)/shard_map/ppermute | solution.py:157
  36.8 4.2 %collective-permute-start.14 = (bf16[4,128,128]{2,1,0:T(8,128)(2,1)S(1)}, bf16[4,128,128]{2,1,0:T(8,128)(2,1)S(1)}, u32[]{:S(2)}, u32[]{:S(2)}) collective-permute-start(bf16[4,128,128]{2,1,0:T(8,128)(2,1)S(1)} %weights.1.refs_0_), channel_id=1, source_target_pairs={{0,96},{16,112},{32,64},{48,80},{64,32},{80,48},{96,0},{112,16},{1... | collective-permute-start | bytes 393224 | tf_op jit(solution)/shard_map/ppermute | solution.py:157
  41.1 0.2 collective-permute-start.13
  41.2 0.8 %collective-permute-start.12 = (bf16[4,128,128]{2,1,0:T(8,128)(2,1)S(1)}, bf16[4,128,128]{2,1,0:T(8,128)(2,1)S(1)}, u32[]{:S(2)}, u32[]{:S(2)}) collective-permute-start(bf16[4,128,128]{2,1,0:T(8,128)(2,1)S(1)} %weights.1.refs_0_), channel_id=1, source_target_pairs={{0,32},{16,48},{32,0},{48,16},{64,96},{80,112},{96,64},{112,80},{1... | collective-permute-start | bytes 393224 | tf_op jit(solution)/shard_map/ppermute | solution.py:157
  42.0 1.1 %diag.1 = bf16[8,4,16,128]{3,2,1,0:T(8,128)(2,1)} custom-call(f32[4,128,128]{2,1,0:T(8,128)S(1)} %get-tuple-element.25.base_ref, f32[4,1,512]{2,1,0:T(1,128)S(1)} %get-tuple-element.26.gain_ref, bf16[4,128,512]{2,1,0:T(8,128)(2,1)S(1)} %get-tuple-element.27.wide_ref, bf16[4,128,512]{2,1,0:T(8,128)(2,1)S(1)} %get-tuple-element.28.flip_ref, ...), custom_call_target="tpu_custom_call" | custom-call | flops 201326592 | bytes 262144 | tf_op jit(solution)/shard_map/diag/pallas_call | solution.py:196
  43.1 5.2 %all-to-all-start.1 = ((bf16[8,4,16,128]{3,2,1,0:T(8,128)(2,1)}), bf16[8,4,16,128]{3,2,1,0:T(8,128)(2,1)S(1)}, u32[]{:S(2)}, u32[]{:S(2)}) async-start(bf16[8,4,16,128]{3,2,1,0:T(8,128)(2,1)} %diag.1), calls=%async_computation.1 | async-start | bytes 262144 | tf_op jit(solution)/shard_map/all_to_all | solution.py:202
  48.3 0.5 collective-permute-done.13.refs_2_
  48.8 2.3 %density.1 = bf16[16,384,128]{2,1,0:T(8,128)(2,1)} custom-call(s32[256]{0:T(256)S(1)} %copy-done.2, bf16[16,384,128]{2,1,0:T(8,128)(2,1)S(1)} %all-to-all-done.moved_ref, bf16[4,128,128]{2,1,0:T(8,128)(2,1)S(1)} %weights.1.refs_0_, bf16[4,128,128]{2,1,0:T(8,128)(2,1)S(1)} %collective-permute-done.12.refs_1_, ...), custom_call_target="tpu_custom_call" | custom-call | flops 201326592 | bytes 3145728 | tf_op jit(solution)/shard_map/density/pallas_call | solution.py:205
  51.1 3.6 %all-to-all-done.1.got_ref = bf16[8,4,16,128]{3,2,1,0:T(8,128)(2,1)S(1)} async-done(((bf16[8,4,16,128]{3,2,1,0:T(8,128)(2,1)}), bf16[8,4,16,128]{3,2,1,0:T(8,128)(2,1)S(1)}, u32[]{:S(2)}, u32[]{:S(2)}) %all-to-all-start.1) | async-done | bytes 131104 | tf_op jit(solution)/shard_map/all_to_all | solution.py:202
  54.7 0.6 %finish.1 = bf16[16,16,128]{2,1,0:T(8,128)(2,1)} custom-call(bf16[8,4,16,128]{3,2,1,0:T(8,128)(2,1)S(1)} %all-to-all-done.1.got_ref), custom_call_target="tpu_custom_call" | custom-call | bytes 131072 | tf_op jit(solution)/shard_map/finish/pallas_call | solution.py:203
  (20 shorter events, 0.2 us)
Async XLA Ops:
  0.6 8.1 %copy-start = (bf16[16,384,128]{2,1,0:T(8,128)(2,1)S(1)}, bf16[16,384,128]{2,1,0:T(8,128)(2,1)}, u32[]{:S(2)}) copy-start(bf16[16,384,128]{2,1,0:T(8,128)(2,1)} %panel_ref.1) | copy-start | bytes 4718596
  0.6 8.1 %copy-start.2 = (s32[256]{0:T(256)S(1)}, s32[256]{0:T(256)}, u32[]{:S(2)}) copy-start(s32[256]{0:T(256)} %count_ref.5) | copy-start | bytes 3076
  0.6 42.5 %all-to-all-start = ((bf16[16,384,128]{2,1,0:T(8,128)(2,1)}), bf16[16,384,128]{2,1,0:T(8,128)(2,1)S(1)}, u32[]{:S(2)}, u32[]{:S(2)}) async-start(bf16[16,384,128]{2,1,0:T(8,128)(2,1)} %panel_ref.1), calls=%async_computation | async-start | bytes 3145728 | tf_op jit(solution)/shard_map/all_to_all | solution.py:159
  8.8 6.0 %copy-start.1 = (bf16[1,16,128,128]{3,2,1,0:T(8,128)(2,1)S(1)}, bf16[1,16,128,128]{3,2,1,0:T(8,128)(2,1)}, u32[]{:S(2)}) copy-start(bf16[1,16,128,128]{3,2,1,0:T(8,128)(2,1)} %param.5) | copy-start | bytes 1572868
  8.8 21.6 %copy-start.3 = (f32[8]{0:T(128)S(1)}, f32[8]{0:T(128)}, u32[]{:S(2)}) copy-start(f32[8]{0:T(128)} %w_ref.1) | copy-start | bytes 100
  10.0 9.1 %collective-permute-start.3 = (bf16[4,128,128]{2,1,0:T(8,128)(2,1)S(1)}, bf16[4,128,128]{2,1,0:T(8,128)(2,1)S(1)}, u32[]{:S(2)}, u32[]{:S(2)}) collective-permute-start(bf16[4,128,128]{2,1,0:T(8,128)(2,1)S(1)} %get-tuple-element.30), channel_id=1, source_target_pairs={{0,32},{16,48},{32,0},{48,16},{64,96},{80,112},{96,64},{112,80},{1... | collective-permute-start | bytes 393224 | tf_op jit(solution)/shard_map/ppermute | solution.py:157
  11.6 9.9 %collective-permute-start.4 = (bf16[4,128,128]{2,1,0:T(8,128)(2,1)S(1)}, bf16[4,128,128]{2,1,0:T(8,128)(2,1)S(1)}, u32[]{:S(2)}, u32[]{:S(2)}) collective-permute-start(bf16[4,128,128]{2,1,0:T(8,128)(2,1)S(1)} %get-tuple-element.31), channel_id=1, source_target_pairs={{0,64},{16,80},{32,96},{48,112},{64,0},{80,16},{96,32},{112,48},{1... | collective-permute-start | bytes 393224 | tf_op jit(solution)/shard_map/ppermute | solution.py:157
  14.3 10.0 %collective-permute-start.5 = (bf16[4,128,128]{2,1,0:T(8,128)(2,1)S(1)}, bf16[4,128,128]{2,1,0:T(8,128)(2,1)S(1)}, u32[]{:S(2)}, u32[]{:S(2)}) collective-permute-start(bf16[4,128,128]{2,1,0:T(8,128)(2,1)S(1)} %get-tuple-element.32), channel_id=1, source_target_pairs={{0,96},{16,112},{32,64},{48,80},{64,32},{80,48},{96,0},{112,16},{1... | collective-permute-start | bytes 393224 | tf_op jit(solution)/shard_map/ppermute | solution.py:157
  14.8 14.8 %collective-permute-start = (bf16[4,128,128]{2,1,0:T(8,128)(2,1)S(1)}, bf16[4,128,128]{2,1,0:T(8,128)(2,1)S(1)}, u32[]{:S(2)}, u32[]{:S(2)}) collective-permute-start(bf16[4,128,128]{2,1,0:T(8,128)(2,1)S(1)} %get-tuple-element.22), channel_id=1, source_target_pairs={{0,32},{16,48},{32,0},{48,16},{64,96},{80,112},{96,64},{112,80},{1... | collective-permute-start | bytes 393224 | tf_op jit(solution)/shard_map/ppermute | solution.py:157
  15.2 15.2 %collective-permute-start.1 = (bf16[4,128,128]{2,1,0:T(8,128)(2,1)S(1)}, bf16[4,128,128]{2,1,0:T(8,128)(2,1)S(1)}, u32[]{:S(2)}, u32[]{:S(2)}) collective-permute-start(bf16[4,128,128]{2,1,0:T(8,128)(2,1)S(1)} %get-tuple-element.23), channel_id=1, source_target_pairs={{0,64},{16,80},{32,96},{48,112},{64,0},{80,16},{96,32},{112,48},{1... | collective-permute-start | bytes 393224 | tf_op jit(solution)/shard_map/ppermute | solution.py:157
  19.1 11.2 %collective-permute-start.2 = (bf16[4,128,128]{2,1,0:T(8,128)(2,1)S(1)}, bf16[4,128,128]{2,1,0:T(8,128)(2,1)S(1)}, u32[]{:S(2)}, u32[]{:S(2)}) collective-permute-start(bf16[4,128,128]{2,1,0:T(8,128)(2,1)S(1)} %get-tuple-element.24), channel_id=1, source_target_pairs={{0,96},{16,112},{32,64},{48,80},{64,32},{80,48},{96,0},{112,16},{1... | collective-permute-start | bytes 393224 | tf_op jit(solution)/shard_map/ppermute | solution.py:157
  24.4 1.3 %collective-permute-start.6 = (bf16[2,128,128]{2,1,0:T(8,128)(2,1)S(1)}, bf16[2,128,128]{2,1,0:T(8,128)(2,1)S(1)}, u32[]{:S(2)}, u32[]{:S(2)}) collective-permute-start(bf16[2,128,128]{2,1,0:T(8,128)(2,1)S(1)} %get-tuple-element.34), channel_id=1, source_target_pairs={{0,1},{1,0},{2,3},{3,2},{4,5},{5,4},{6,7},{7,6},{8,9},{9,8},{10,11... | collective-permute-start | bytes 196616 | tf_op jit(solution)/shard_map/ppermute | solution.py:175
  25.7 7.6 %collective-permute-start.8 = (bf16[2,128,128]{2,1,0:T(8,128)(2,1)S(1)}, bf16[2,128,128]{2,1,0:T(8,128)(2,1)S(1)}, u32[]{:S(2)}, u32[]{:S(2)}) collective-permute-start(bf16[2,128,128]{2,1,0:T(8,128)(2,1)S(1)} %get-tuple-element.35), channel_id=1, source_target_pairs={{0,8},{1,9},{2,10},{3,11},{4,12},{5,13},{6,14},{7,15},{8,0},{9,1},... | collective-permute-start | bytes 196616 | tf_op jit(solution)/shard_map/ppermute | solution.py:180
  29.3 5.5 %collective-permute-start.7 = (bf16[2,128,128]{2,1,0:T(8,128)(2,1)S(1)}, bf16[2,128,128]{2,1,0:T(8,128)(2,1)S(1)}, u32[]{:S(2)}, u32[]{:S(2)}) collective-permute-start(bf16[2,128,128]{2,1,0:T(8,128)(2,1)S(1)} %get-tuple-element.35), channel_id=1, source_target_pairs={{0,24},{1,25},{2,26},{3,27},{4,28},{5,29},{6,30},{7,31},{8,16},{9,... | collective-permute-start | bytes 196616 | tf_op jit(solution)/shard_map/ppermute | solution.py:180
  29.6 5.2 %collective-permute-start.9 = (bf16[2,128,128]{2,1,0:T(8,128)(2,1)S(1)}, bf16[2,128,128]{2,1,0:T(8,128)(2,1)S(1)}, u32[]{:S(2)}, u32[]{:S(2)}) collective-permute-start(bf16[2,128,128]{2,1,0:T(8,128)(2,1)S(1)} %get-tuple-element.36.a0_ref), channel_id=1, source_target_pairs={{0,16},{16,0},{32,48},{48,32},{64,80},{80,64},{96,112},{112,96},{1... | collective-permute-start | bytes 196616 | tf_op jit(solution)/shard_map/ppermute | solution.py:157
  31.2 5.6 %collective-permute-start.11 = (bf16[4,128,128]{2,1,0:T(8,128)(2,1)S(1)}, bf16[4,128,128]{2,1,0:T(8,128)(2,1)S(1)}, u32[]{:S(2)}, u32[]{:S(2)}) collective-permute-start(bf16[4,128,128]{2,1,0:T(8,128)(2,1)S(1)} %get-tuple-element.38.a_ref), channel_id=1, source_target_pairs={{0,16},{16,0},{32,48},{48,32},{64,80},{80,64},{96,112},{112,96},{1... | collective-permute-start | bytes 393224 | tf_op jit(solution)/shard_map/ppermute | solution.py:157
  34.8 7.2 %collective-permute-start.10 = (bf16[2,2,128,128]{3,2,1,0:T(8,128)(2,1)S(1)}, bf16[2,2,128,128]{3,2,1,0:T(8,128)(2,1)S(1)}, u32[]{:S(2)}, u32[]{:S(2)}) collective-permute-start(bf16[2,2,128,128]{3,2,1,0:T(8,128)(2,1)S(1)} %gown.1), channel_id=1, source_target_pairs={{0,0},{1,1},{2,2},{3,3},{4,4},{5,5},{6,6},{7,7},{8,8},{9,9},{10,10... | collective-permute-start | bytes 393224 | tf_op jit(solution)/shard_map/ppermute | solution.py:180
  36.8 11.5 %collective-permute-start.14 = (bf16[4,128,128]{2,1,0:T(8,128)(2,1)S(1)}, bf16[4,128,128]{2,1,0:T(8,128)(2,1)S(1)}, u32[]{:S(2)}, u32[]{:S(2)}) collective-permute-start(bf16[4,128,128]{2,1,0:T(8,128)(2,1)S(1)} %weights.1.refs_0_), channel_id=1, source_target_pairs={{0,96},{16,112},{32,64},{48,80},{64,32},{80,48},{96,0},{112,16},{1... | collective-permute-start | bytes 393224 | tf_op jit(solution)/shard_map/ppermute | solution.py:157
  41.1 7.8 %collective-permute-start.13 = (bf16[4,128,128]{2,1,0:T(8,128)(2,1)S(1)}, bf16[4,128,128]{2,1,0:T(8,128)(2,1)S(1)}, u32[]{:S(2)}, u32[]{:S(2)}) collective-permute-start(bf16[4,128,128]{2,1,0:T(8,128)(2,1)S(1)} %weights.1.refs_0_), channel_id=1, source_target_pairs={{0,64},{16,80},{32,96},{48,112},{64,0},{80,16},{96,32},{112,48},{1... | collective-permute-start | bytes 393224 | tf_op jit(solution)/shard_map/ppermute | solution.py:157
  41.2 7.6 %collective-permute-start.12 = (bf16[4,128,128]{2,1,0:T(8,128)(2,1)S(1)}, bf16[4,128,128]{2,1,0:T(8,128)(2,1)S(1)}, u32[]{:S(2)}, u32[]{:S(2)}) collective-permute-start(bf16[4,128,128]{2,1,0:T(8,128)(2,1)S(1)} %weights.1.refs_0_), channel_id=1, source_target_pairs={{0,32},{16,48},{32,0},{48,16},{64,96},{80,112},{96,64},{112,80},{1... | collective-permute-start | bytes 393224 | tf_op jit(solution)/shard_map/ppermute | solution.py:157
  43.1 11.6 %all-to-all-start.1 = ((bf16[8,4,16,128]{3,2,1,0:T(8,128)(2,1)}), bf16[8,4,16,128]{3,2,1,0:T(8,128)(2,1)S(1)}, u32[]{:S(2)}, u32[]{:S(2)}) async-start(bf16[8,4,16,128]{3,2,1,0:T(8,128)(2,1)} %diag.1), calls=%async_computation.1 | async-start | bytes 262144 | tf_op jit(solution)/shard_map/all_to_all | solution.py:202

commit v10 on v9

--- a/solution.py
+++ b/solution.py
@@ -94,27 +94,33 @@
         m_ref[t] = (-base).astype(BF16)
 
 
-def diag_kernel(share, base_ref, gain_ref, wide_ref, flip_ref, *refs):
-    g_ref, out_ref = refs
+def diag_kernel(share, base_ref, gain_ref, wide_ref, flip_ref, g_ref, out_ref, rows_ref, done):
     block = base_ref.shape[1]
     half = wide_ref.shape[2] // block
-    chunk = out_ref.shape[2]
+    poles, chunk = rows_ref.shape[1], rows_ref.shape[2]
+    copies = []
     middle = []
     for t in range(share):
         v = (dot(g_ref[t // 2, t % 2], wide_ref[t]) * gain_ref[t]).astype(BF16)
         middle.append(jnp.concatenate([v[:, k * block:(k + 1) * block] for k in range(half)], axis=0))
     for t, v in enumerate(middle):
         d = (base_ref[t] + dot(flip_ref[t], v)).astype(BF16)
-        for p in range(out_ref.shape[0]):
-            out_ref[p, t] = d[p * chunk:(p + 1) * chunk]
+        for p in range(poles):
+            rows_ref[t, p] = d[p * chunk:(p + 1) * chunk]
+        copies.append(pltpu.make_async_copy(rows_ref.at[t], out_ref.at[:, t], done.at[t]))
+        copies[-1].start()
+    for copy in copies:
+        copy.wait()
 
 
 def finish_kernel(share, got_ref, out_ref):
     col = lax.axis_index("col")
-    for x in range(got_ref.shape[0] // 2):
-        for t in range(share):
-            d = got_ref[2 * x, t].astype(F32) + got_ref[2 * x + 1, t].astype(F32)
-            out_ref[col ^ slot(share, x, t)] = d.astype(BF16)
+    sums = [
+        (got_ref[2 * x].astype(F32) + got_ref[2 * x + 1].astype(F32)).astype(BF16) for x in range(got_ref.shape[0] // 2)
+    ]
+    for x, d in enumerate(sums):
+        for t in range(share):
+            out_ref[col ^ slot(share, x, t)] = d[t]
 
 
 def density_kernel(poles, share, count_ref, moved_ref, *refs):
@@ -193,11 +199,18 @@
     mfull = call(add_kernel, "weights", [vmem] * 2, [shape(share, block, block)])(mhalf, swap(mhalf, 1))[0]
     mparts = [mfull] + [swap(mfull, 2 * k) for k in range(1, half)]
 
-    part = call(
-        functools.partial(diag_kernel, share), "diag",
-        [vmem] * 5, [shape(poles, share, chunk, block)],
-        6 * owned * block * block * block,
-    )(base, gain, wide, flip, gfull)[0]
+    part = pl.pallas_call(
+        functools.partial(diag_kernel, share),
+        in_specs=[vmem] * 5,
+        out_specs=pl.BlockSpec(memory_space=pl.ANY),
+        out_shape=shape(poles, share, chunk, block),
+        scratch_shapes=[pltpu.VMEM((share, poles, chunk, block), BF16), pltpu.SemaphoreType.DMA((share,))],
+        compiler_params=pltpu.CompilerParams(vmem_limit_bytes=32 * 1024 * 1024),
+        cost_estimate=pl.CostEstimate(
+            flops=6 * owned * block * block * block, bytes_accessed=4 * owned * block * block, transcendentals=0
+        ),
+        name="diag",
+    )(base, gain, wide, flip, gfull)
     part, moved = lax.optimization_barrier((part, moved))
     part = lax.all_to_all(part, "pole", 0, 0, tiled=True)
     diag = call(functools.partial(finish_kernel, share), "finish", [vmem], [shape(owned, chunk, block)])(part)[0]

time: 55.7 us -> 55.7 us (level)
  no operation moved by 1% of the time
where the time goes in v10:
time: 55.7 us; the launch traced here: 55.4 us
  starting transfers between devices  34.8 us (62%)
  waiting for transfers between devices  13.7 us (25%)
  Pallas kernels  6.23 us (11%)
  between operations  0.77 us (1%)
    ppermute x11, starting transfers between devices, swap(): return lax.ppermute(x, 'pole', [(i, i ^ k) for i in range(poles)])  16.8 us
    all_to_all x1, starting transfers between devices, shards(): moved = lax.all_to_all(panel, 'col', 0, 0, tiled=True)  8.11 us
    ppermute x11, waiting for transfers between devices, swap(): return lax.ppermute(x, 'pole', [(i, i ^ k) for i in range(poles)])  6.45 us
    all_to_all x1, starting transfers between devices, shards(): part = lax.all_to_all(part, 'pole', 0, 0, tiled=True)  5.22 us
    ppermute x3, starting transfers between devices, shift(): return lax.ppermute(x, ('pole', 'col'), pairs)  4.5 us
    all_to_all x1, waiting for transfers between devices, shards(): part = lax.all_to_all(part, 'pole', 0, 0, tiled=True)  3.68 us
    ppermute x3, waiting for transfers between devices, shift(): return lax.ppermute(x, ('pole', 'col'), pairs)  2.28 us
    pallas_call x1, Pallas kernels, shards(): call(functools.partial(density_kernel, poles, share), 'density', [smem, v...  2.27 us
  transfers between devices with their start and end apart: 17, of which 8 were waited for; matrix products, arithmetic and copies ran while one was open for 0% of the time, Pallas kernels for 10%

profile of v10, /device:TPU:0, one launch (start us, length us, event | category | flops | bytes accessed | tf_op | source)
XLA Modules:
  0.0 55.4 jit_solution(14822473507506303217)
XLA Ops:
  0.6 8.1 %all-to-all-start = ((bf16[16,384,128]{2,1,0:T(8,128)(2,1)}), bf16[16,384,128]{2,1,0:T(8,128)(2,1)S(1)}, u32[]{:S(2)}, u32[]{:S(2)}) async-start(bf16[16,384,128]{2,1,0:T(8,128)(2,1)} %panel_ref.1), calls=%async_computation | async-start | bytes 3145728 | tf_op jit(solution)/shard_map/all_to_all | solution.py:165
  8.8 0.0 copy-start.3
  8.8 1.2 %gram.1 = (bf16[4,128,128]{2,1,0:T(8,128)(2,1)S(1)}, bf16[4,128,128]{2,1,0:T(8,128)(2,1)S(1)}, bf16[4,128,128]{2,1,0:T(8,128)(2,1)S(1)}, bf16[4,128,128]{2,1,0:T(8,128)(2,1)S(1)}) custom-call(s32[256]{0:T(256)S(1)} %copy-done.2, bf16[16,384,128]{2,1,0:T(8,128)(2,1)S(1)} %copy-done), custom_call_target="tpu_custom_call" | custom-call | flops 201326592 | bytes 1048576 | tf_op jit(solution)/shard_map/gram/pallas_call | solution.py:170
  10.0 1.6 %collective-permute-start.3 = (bf16[4,128,128]{2,1,0:T(8,128)(2,1)S(1)}, bf16[4,128,128]{2,1,0:T(8,128)(2,1)S(1)}, u32[]{:S(2)}, u32[]{:S(2)}) collective-permute-start(bf16[4,128,128]{2,1,0:T(8,128)(2,1)S(1)} %get-tuple-element.30), channel_id=1, source_target_pairs={{0,32},{16,48},{32,0},{48,16},{64,96},{80,112},{96,64},{112,80},{1... | collective-permute-start | bytes 393224 | tf_op jit(solution)/shard_map/ppermute | solution.py:163
  11.6 2.7 %collective-permute-start.4 = (bf16[4,128,128]{2,1,0:T(8,128)(2,1)S(1)}, bf16[4,128,128]{2,1,0:T(8,128)(2,1)S(1)}, u32[]{:S(2)}, u32[]{:S(2)}) collective-permute-start(bf16[4,128,128]{2,1,0:T(8,128)(2,1)S(1)} %get-tuple-element.31), channel_id=1, source_target_pairs={{0,64},{16,80},{32,96},{48,112},{64,0},{80,16},{96,32},{112,48},{1... | collective-permute-start | bytes 393224 | tf_op jit(solution)/shard_map/ppermute | solution.py:163
  14.3 0.5 collective-permute-start.5
  14.8 0.4 collective-permute-start
  15.2 3.9 %collective-permute-start.1 = (bf16[4,128,128]{2,1,0:T(8,128)(2,1)S(1)}, bf16[4,128,128]{2,1,0:T(8,128)(2,1)S(1)}, u32[]{:S(2)}, u32[]{:S(2)}) collective-permute-start(bf16[4,128,128]{2,1,0:T(8,128)(2,1)S(1)} %get-tuple-element.23), channel_id=1, source_target_pairs={{0,64},{16,80},{32,96},{48,112},{64,0},{80,16},{96,32},{112,48},{1... | collective-permute-start | bytes 393224 | tf_op jit(solution)/shard_map/ppermute | solution.py:163
  19.1 0.5 collective-permute-start.2
  19.6 1.8 %collective-permute-done.4.refs_2_ = bf16[4,128,128]{2,1,0:T(8,128)(2,1)S(1)} collective-permute-done((bf16[4,128,128]{2,1,0:T(8,128)(2,1)S(1)}, bf16[4,128,128]{2,1,0:T(8,128)(2,1)S(1)}, u32[]{:S(2)}, u32[]{:S(2)}) %collective-permute-start.4) | collective-permute-done | bytes 131104 | tf_op jit(solution)/shard_map/ppermute | solution.py:163
  21.4 2.9 %collective-permute-done.5.refs_3_ = bf16[4,128,128]{2,1,0:T(8,128)(2,1)S(1)} collective-permute-done((bf16[4,128,128]{2,1,0:T(8,128)(2,1)S(1)}, bf16[4,128,128]{2,1,0:T(8,128)(2,1)S(1)}, u32[]{:S(2)}, u32[]{:S(2)}) %collective-permute-start.5) | collective-permute-done | bytes 131104 | tf_op jit(solution)/shard_map/ppermute | solution.py:163
  24.3 0.1 gsum.1
  24.4 0.1 collective-permute-start.6
  24.5 1.2 %collective-permute-done.6.b_ref = bf16[2,128,128]{2,1,0:T(8,128)(2,1)S(1)} collective-permute-done((bf16[2,128,128]{2,1,0:T(8,128)(2,1)S(1)}, bf16[2,128,128]{2,1,0:T(8,128)(2,1)S(1)}, u32[]{:S(2)}, u32[]{:S(2)}) %collective-permute-start.6) | collective-permute-done | bytes 65568 | tf_op jit(solution)/shard_map/ppermute | solution.py:181
  25.7 3.6 %collective-permute-start.8 = (bf16[2,128,128]{2,1,0:T(8,128)(2,1)S(1)}, bf16[2,128,128]{2,1,0:T(8,128)(2,1)S(1)}, u32[]{:S(2)}, u32[]{:S(2)}) collective-permute-start(bf16[2,128,128]{2,1,0:T(8,128)(2,1)S(1)} %get-tuple-element.35), channel_id=1, source_target_pairs={{0,8},{1,9},{2,10},{3,11},{4,12},{5,13},{6,14},{7,15},{8,0},{9,1},... | collective-permute-start | bytes 196616 | tf_op jit(solution)/shard_map/ppermute | solution.py:186
  29.3 0.3 collective-permute-start.7
  29.6 0.8 %collective-permute-start.9 = (bf16[2,128,128]{2,1,0:T(8,128)(2,1)S(1)}, bf16[2,128,128]{2,1,0:T(8,128)(2,1)S(1)}, u32[]{:S(2)}, u32[]{:S(2)}) collective-permute-start(bf16[2,128,128]{2,1,0:T(8,128)(2,1)S(1)} %get-tuple-element.36.a0_ref), channel_id=1, source_target_pairs={{0,16},{16,0},{32,48},{48,32},{64,80},{80,64},{96,112},{112,96},{1... | collective-permute-start | bytes 196616 | tf_op jit(solution)/shard_map/ppermute | solution.py:163
  30.4 0.8 %prep.1 = (bf16[4,128,128]{2,1,0:T(8,128)(2,1)S(1)}, f32[4,128,128]{2,1,0:T(8,128)S(1)}, f32[4,1,512]{2,1,0:T(1,128)S(1)}, bf16[4,128,512]{2,1,0:T(8,128)(2,1)S(1)}, bf16[4,128,512]{2,1,0:T(8,128)(2,1)S(1)}) custom-call(f32[8]{0:T(128)S(1)} %copy-done.3, s32[256]{0:T(256)S(1)} %copy-done.2, bf16[4,128,128]{2,1,0:T(8,128)(2,1)S(1)} %get-tuple-element.21.refs_0_, ...), custom_call_target="tpu_custom_call" | custom-call | bytes 2629632 | tf_op jit(solution)/shard_map/prep/pallas_call | solution.py:195
  31.2 1.3 %collective-permute-start.11 = (bf16[4,128,128]{2,1,0:T(8,128)(2,1)S(1)}, bf16[4,128,128]{2,1,0:T(8,128)(2,1)S(1)}, u32[]{:S(2)}, u32[]{:S(2)}) collective-permute-start(bf16[4,128,128]{2,1,0:T(8,128)(2,1)S(1)} %get-tuple-element.38.a_ref), channel_id=1, source_target_pairs={{0,16},{16,0},{32,48},{48,32},{64,80},{80,64},{96,112},{112,96},{1... | collective-permute-start | bytes 393224 | tf_op jit(solution)/shard_map/ppermute | solution.py:163
  32.5 0.8 %collective-permute-done.8.b1_ref = bf16[2,128,128]{2,1,0:T(8,128)(2,1)S(1)} collective-permute-done((bf16[2,128,128]{2,1,0:T(8,128)(2,1)S(1)}, bf16[2,128,128]{2,1,0:T(8,128)(2,1)S(1)}, u32[]{:S(2)}, u32[]{:S(2)}) %collective-permute-start.8) | collective-permute-done | bytes 65568 | tf_op jit(solution)/shard_map/ppermute | solution.py:186
  33.3 1.5 %collective-permute-done.7.b0_ref = bf16[2,128,128]{2,1,0:T(8,128)(2,1)S(1)} collective-permute-done((bf16[2,128,128]{2,1,0:T(8,128)(2,1)S(1)}, bf16[2,128,128]{2,1,0:T(8,128)(2,1)S(1)}, u32[]{:S(2)}, u32[]{:S(2)}) %collective-permute-start.7) | collective-permute-done | bytes 65568 | tf_op jit(solution)/shard_map/ppermute | solution.py:186
  34.8 0.7 %collective-permute-start.10 = (bf16[2,2,128,128]{3,2,1,0:T(8,128)(2,1)S(1)}, bf16[2,2,128,128]{3,2,1,0:T(8,128)(2,1)S(1)}, u32[]{:S(2)}, u32[]{:S(2)}) collective-permute-start(bf16[2,2,128,128]{3,2,1,0:T(8,128)(2,1)S(1)} %gown.1), channel_id=1, source_target_pairs={{0,0},{1,1},{2,2},{3,3},{4,4},{5,5},{6,6},{7,7},{8,8},{9,9},{10,10... | collective-permute-start | bytes 393224 | tf_op jit(solution)/shard_map/ppermute | solution.py:186
  35.5 1.3 %collective-permute-done.11.b_ref = bf16[4,128,128]{2,1,0:T(8,128)(2,1)S(1)} collective-permute-done((bf16[4,128,128]{2,1,0:T(8,128)(2,1)S(1)}, bf16[4,128,128]{2,1,0:T(8,128)(2,1)S(1)}, u32[]{:S(2)}, u32[]{:S(2)}) %collective-permute-start.11) | collective-permute-done | bytes 131104 | tf_op jit(solution)/shard_map/ppermute | solution.py:163
  36.8 4.2 %collective-permute-start.14 = (bf16[4,128,128]{2,1,0:T(8,128)(2,1)S(1)}, bf16[4,128,128]{2,1,0:T(8,128)(2,1)S(1)}, u32[]{:S(2)}, u32[]{:S(2)}) collective-permute-start(bf16[4,128,128]{2,1,0:T(8,128)(2,1)S(1)} %weights.1.refs_0_), channel_id=1, source_target_pairs={{0,96},{16,112},{32,64},{48,80},{64,32},{80,48},{96,0},{112,16},{1... | collective-permute-start | bytes 393224 | tf_op jit(solution)/shard_map/ppermute | solution.py:163
  41.1 0.2 collective-permute-start.13
  41.2 0.8 %collective-permute-start.12 = (bf16[4,128,128]{2,1,0:T(8,128)(2,1)S(1)}, bf16[4,128,128]{2,1,0:T(8,128)(2,1)S(1)}, u32[]{:S(2)}, u32[]{:S(2)}) collective-permute-start(bf16[4,128,128]{2,1,0:T(8,128)(2,1)S(1)} %weights.1.refs_0_), channel_id=1, source_target_pairs={{0,32},{16,48},{32,0},{48,16},{64,96},{80,112},{96,64},{112,80},{1... | collective-permute-start | bytes 393224 | tf_op jit(solution)/shard_map/ppermute | solution.py:163
  42.0 1.1 %diag.1 = bf16[8,4,16,128]{3,2,1,0:T(8,128)(2,1)} custom-call(f32[4,128,128]{2,1,0:T(8,128)S(1)} %get-tuple-element.25.base_ref, f32[4,1,512]{2,1,0:T(1,128)S(1)} %get-tuple-element.26.gain_ref, bf16[4,128,512]{2,1,0:T(8,128)(2,1)S(1)} %get-tuple-element.27.wide_ref, bf16[4,128,512]{2,1,0:T(8,128)(2,1)S(1)} %get-tuple-element.28.flip_ref, ...), custom_call_target="tpu_custom_call" | custom-call | flops 201326592 | bytes 1048576 | tf_op jit(solution)/shard_map/diag/pallas_call | solution.py:202
  43.2 5.2 %all-to-all-start.1 = ((bf16[8,4,16,128]{3,2,1,0:T(8,128)(2,1)}), bf16[8,4,16,128]{3,2,1,0:T(8,128)(2,1)S(1)}, u32[]{:S(2)}, u32[]{:S(2)}) async-start(bf16[8,4,16,128]{3,2,1,0:T(8,128)(2,1)} %diag.1), calls=%async_computation.1 | async-start | bytes 262144 | tf_op jit(solution)/shard_map/all_to_all | solution.py:215
  48.4 0.4 collective-permute-done.13.refs_2_
  48.8 2.3 %density.1 = bf16[16,384,128]{2,1,0:T(8,128)(2,1)} custom-call(s32[256]{0:T(256)S(1)} %copy-done.2, bf16[16,384,128]{2,1,0:T(8,128)(2,1)S(1)} %all-to-all-done.moved_ref, bf16[4,128,128]{2,1,0:T(8,128)(2,1)S(1)} %weights.1.refs_0_, bf16[4,128,128]{2,1,0:T(8,128)(2,1)S(1)} %collective-permute-done.12.refs_1_, ...), custom_call_target="tpu_custom_call" | custom-call | flops 201326592 | bytes 3145728 | tf_op jit(solution)/shard_map/density/pallas_call | solution.py:218
  51.1 3.7 %all-to-all-done.1.got_ref = bf16[8,4,16,128]{3,2,1,0:T(8,128)(2,1)S(1)} async-done(((bf16[8,4,16,128]{3,2,1,0:T(8,128)(2,1)}), bf16[8,4,16,128]{3,2,1,0:T(8,128)(2,1)S(1)}, u32[]{:S(2)}, u32[]{:S(2)}) %all-to-all-start.1) | async-done | bytes 131104 | tf_op jit(solution)/shard_map/all_to_all | solution.py:215
  54.8 0.6 %finish.1 = bf16[16,16,128]{2,1,0:T(8,128)(2,1)} custom-call(bf16[8,4,16,128]{3,2,1,0:T(8,128)(2,1)S(1)} %all-to-all-done.1.got_ref), custom_call_target="tpu_custom_call" | custom-call | bytes 131072 | tf_op jit(solution)/shard_map/finish/pallas_call | solution.py:216
  (20 shorter events, 0.2 us)
Async XLA Ops:
  0.6 8.1 %copy-start = (bf16[16,384,128]{2,1,0:T(8,128)(2,1)S(1)}, bf16[16,384,128]{2,1,0:T(8,128)(2,1)}, u32[]{:S(2)}) copy-start(bf16[16,384,128]{2,1,0:T(8,128)(2,1)} %panel_ref.1) | copy-start | bytes 4718596
  0.6 8.1 %copy-start.2 = (s32[256]{0:T(256)S(1)}, s32[256]{0:T(256)}, u32[]{:S(2)}) copy-start(s32[256]{0:T(256)} %count_ref.5) | copy-start | bytes 3076
  0.6 42.5 %all-to-all-start = ((bf16[16,384,128]{2,1,0:T(8,128)(2,1)}), bf16[16,384,128]{2,1,0:T(8,128)(2,1)S(1)}, u32[]{:S(2)}, u32[]{:S(2)}) async-start(bf16[16,384,128]{2,1,0:T(8,128)(2,1)} %panel_ref.1), calls=%async_computation | async-start | bytes 3145728 | tf_op jit(solution)/shard_map/all_to_all | solution.py:165
  8.8 6.0 %copy-start.1 = (bf16[1,16,128,128]{3,2,1,0:T(8,128)(2,1)S(1)}, bf16[1,16,128,128]{3,2,1,0:T(8,128)(2,1)}, u32[]{:S(2)}) copy-start(bf16[1,16,128,128]{3,2,1,0:T(8,128)(2,1)} %param.5) | copy-start | bytes 1572868
  8.8 21.6 %copy-start.3 = (f32[8]{0:T(128)S(1)}, f32[8]{0:T(128)}, u32[]{:S(2)}) copy-start(f32[8]{0:T(128)} %w_ref.1) | copy-start | bytes 100
  10.0 9.1 %collective-permute-start.3 = (bf16[4,128,128]{2,1,0:T(8,128)(2,1)S(1)}, bf16[4,128,128]{2,1,0:T(8,128)(2,1)S(1)}, u32[]{:S(2)}, u32[]{:S(2)}) collective-permute-start(bf16[4,128,128]{2,1,0:T(8,128)(2,1)S(1)} %get-tuple-element.30), channel_id=1, source_target_pairs={{0,32},{16,48},{32,0},{48,16},{64,96},{80,112},{96,64},{112,80},{1... | collective-permute-start | bytes 393224 | tf_op jit(solution)/shard_map/ppermute | solution.py:163
  11.6 9.9 %collective-permute-start.4 = (bf16[4,128,128]{2,1,0:T(8,128)(2,1)S(1)}, bf16[4,128,128]{2,1,0:T(8,128)(2,1)S(1)}, u32[]{:S(2)}, u32[]{:S(2)}) collective-permute-start(bf16[4,128,128]{2,1,0:T(8,128)(2,1)S(1)} %get-tuple-element.31), channel_id=1, source_target_pairs={{0,64},{16,80},{32,96},{48,112},{64,0},{80,16},{96,32},{112,48},{1... | collective-permute-start | bytes 393224 | tf_op jit(solution)/shard_map/ppermute | solution.py:163
  14.3 10.0 %collective-permute-start.5 = (bf16[4,128,128]{2,1,0:T(8,128)(2,1)S(1)}, bf16[4,128,128]{2,1,0:T(8,128)(2,1)S(1)}, u32[]{:S(2)}, u32[]{:S(2)}) collective-permute-start(bf16[4,128,128]{2,1,0:T(8,128)(2,1)S(1)} %get-tuple-element.32), channel_id=1, source_target_pairs={{0,96},{16,112},{32,64},{48,80},{64,32},{80,48},{96,0},{112,16},{1... | collective-permute-start | bytes 393224 | tf_op jit(solution)/shard_map/ppermute | solution.py:163
  14.8 14.8 %collective-permute-start = (bf16[4,128,128]{2,1,0:T(8,128)(2,1)S(1)}, bf16[4,128,128]{2,1,0:T(8,128)(2,1)S(1)}, u32[]{:S(2)}, u32[]{:S(2)}) collective-permute-start(bf16[4,128,128]{2,1,0:T(8,128)(2,1)S(1)} %get-tuple-element.22), channel_id=1, source_target_pairs={{0,32},{16,48},{32,0},{48,16},{64,96},{80,112},{96,64},{112,80},{1... | collective-permute-start | bytes 393224 | tf_op jit(solution)/shard_map/ppermute | solution.py:163
  15.2 15.2 %collective-permute-start.1 = (bf16[4,128,128]{2,1,0:T(8,128)(2,1)S(1)}, bf16[4,128,128]{2,1,0:T(8,128)(2,1)S(1)}, u32[]{:S(2)}, u32[]{:S(2)}) collective-permute-start(bf16[4,128,128]{2,1,0:T(8,128)(2,1)S(1)} %get-tuple-element.23), channel_id=1, source_target_pairs={{0,64},{16,80},{32,96},{48,112},{64,0},{80,16},{96,32},{112,48},{1... | collective-permute-start | bytes 393224 | tf_op jit(solution)/shard_map/ppermute | solution.py:163
  19.1 11.2 %collective-permute-start.2 = (bf16[4,128,128]{2,1,0:T(8,128)(2,1)S(1)}, bf16[4,128,128]{2,1,0:T(8,128)(2,1)S(1)}, u32[]{:S(2)}, u32[]{:S(2)}) collective-permute-start(bf16[4,128,128]{2,1,0:T(8,128)(2,1)S(1)} %get-tuple-element.24), channel_id=1, source_target_pairs={{0,96},{16,112},{32,64},{48,80},{64,32},{80,48},{96,0},{112,16},{1... | collective-permute-start | bytes 393224 | tf_op jit(solution)/shard_map/ppermute | solution.py:163
  24.4 1.3 %collective-permute-start.6 = (bf16[2,128,128]{2,1,0:T(8,128)(2,1)S(1)}, bf16[2,128,128]{2,1,0:T(8,128)(2,1)S(1)}, u32[]{:S(2)}, u32[]{:S(2)}) collective-permute-start(bf16[2,128,128]{2,1,0:T(8,128)(2,1)S(1)} %get-tuple-element.34), channel_id=1, source_target_pairs={{0,1},{1,0},{2,3},{3,2},{4,5},{5,4},{6,7},{7,6},{8,9},{9,8},{10,11... | collective-permute-start | bytes 196616 | tf_op jit(solution)/shard_map/ppermute | solution.py:181
  25.7 7.6 %collective-permute-start.8 = (bf16[2,128,128]{2,1,0:T(8,128)(2,1)S(1)}, bf16[2,128,128]{2,1,0:T(8,128)(2,1)S(1)}, u32[]{:S(2)}, u32[]{:S(2)}) collective-permute-start(bf16[2,128,128]{2,1,0:T(8,128)(2,1)S(1)} %get-tuple-element.35), channel_id=1, source_target_pairs={{0,8},{1,9},{2,10},{3,11},{4,12},{5,13},{6,14},{7,15},{8,0},{9,1},... | collective-permute-start | bytes 196616 | tf_op jit(solution)/shard_map/ppermute | solution.py:186
  29.3 5.5 %collective-permute-start.7 = (bf16[2,128,128]{2,1,0:T(8,128)(2,1)S(1)}, bf16[2,128,128]{2,1,0:T(8,128)(2,1)S(1)}, u32[]{:S(2)}, u32[]{:S(2)}) collective-permute-start(bf16[2,128,128]{2,1,0:T(8,128)(2,1)S(1)} %get-tuple-element.35), channel_id=1, source_target_pairs={{0,24},{1,25},{2,26},{3,27},{4,28},{5,29},{6,30},{7,31},{8,16},{9,... | collective-permute-start | bytes 196616 | tf_op jit(solution)/shard_map/ppermute | solution.py:186
  29.6 5.2 %collective-permute-start.9 = (bf16[2,128,128]{2,1,0:T(8,128)(2,1)S(1)}, bf16[2,128,128]{2,1,0:T(8,128)(2,1)S(1)}, u32[]{:S(2)}, u32[]{:S(2)}) collective-permute-start(bf16[2,128,128]{2,1,0:T(8,128)(2,1)S(1)} %get-tuple-element.36.a0_ref), channel_id=1, source_target_pairs={{0,16},{16,0},{32,48},{48,32},{64,80},{80,64},{96,112},{112,96},{1... | collective-permute-start | bytes 196616 | tf_op jit(solution)/shard_map/ppermute | solution.py:163
  31.2 5.6 %collective-permute-start.11 = (bf16[4,128,128]{2,1,0:T(8,128)(2,1)S(1)}, bf16[4,128,128]{2,1,0:T(8,128)(2,1)S(1)}, u32[]{:S(2)}, u32[]{:S(2)}) collective-permute-start(bf16[4,128,128]{2,1,0:T(8,128)(2,1)S(1)} %get-tuple-element.38.a_ref), channel_id=1, source_target_pairs={{0,16},{16,0},{32,48},{48,32},{64,80},{80,64},{96,112},{112,96},{1... | collective-permute-start | bytes 393224 | tf_op jit(solution)/shard_map/ppermute | solution.py:163
  34.8 7.2 %collective-permute-start.10 = (bf16[2,2,128,128]{3,2,1,0:T(8,128)(2,1)S(1)}, bf16[2,2,128,128]{3,2,1,0:T(8,128)(2,1)S(1)}, u32[]{:S(2)}, u32[]{:S(2)}) collective-permute-start(bf16[2,2,128,128]{3,2,1,0:T(8,128)(2,1)S(1)} %gown.1), channel_id=1, source_target_pairs={{0,0},{1,1},{2,2},{3,3},{4,4},{5,5},{6,6},{7,7},{8,8},{9,9},{10,10... | collective-permute-start | bytes 393224 | tf_op jit(solution)/shard_map/ppermute | solution.py:186
  36.8 11.6 %collective-permute-start.14 = (bf16[4,128,128]{2,1,0:T(8,128)(2,1)S(1)}, bf16[4,128,128]{2,1,0:T(8,128)(2,1)S(1)}, u32[]{:S(2)}, u32[]{:S(2)}) collective-permute-start(bf16[4,128,128]{2,1,0:T(8,128)(2,1)S(1)} %weights.1.refs_0_), channel_id=1, source_target_pairs={{0,96},{16,112},{32,64},{48,80},{64,32},{80,48},{96,0},{112,16},{1... | collective-permute-start | bytes 393224 | tf_op jit(solution)/shard_map/ppermute | solution.py:163
  41.1 7.8 %collective-permute-start.13 = (bf16[4,128,128]{2,1,0:T(8,128)(2,1)S(1)}, bf16[4,128,128]{2,1,0:T(8,128)(2,1)S(1)}, u32[]{:S(2)}, u32[]{:S(2)}) collective-permute-start(bf16[4,128,128]{2,1,0:T(8,128)(2,1)S(1)} %weights.1.refs_0_), channel_id=1, source_target_pairs={{0,64},{16,80},{32,96},{48,112},{64,0},{80,16},{96,32},{112,48},{1... | collective-permute-start | bytes 393224 | tf_op jit(solution)/shard_map/ppermute | solution.py:163
  41.2 7.6 %collective-permute-start.12 = (bf16[4,128,128]{2,1,0:T(8,128)(2,1)S(1)}, bf16[4,128,128]{2,1,0:T(8,128)(2,1)S(1)}, u32[]{:S(2)}, u32[]{:S(2)}) collective-permute-start(bf16[4,128,128]{2,1,0:T(8,128)(2,1)S(1)} %weights.1.refs_0_), channel_id=1, source_target_pairs={{0,32},{16,48},{32,0},{48,16},{64,96},{80,112},{96,64},{112,80},{1... | collective-permute-start | bytes 393224 | tf_op jit(solution)/shard_map/ppermute | solution.py:163
  43.2 11.6 %all-to-all-start.1 = ((bf16[8,4,16,128]{3,2,1,0:T(8,128)(2,1)}), bf16[8,4,16,128]{3,2,1,0:T(8,128)(2,1)S(1)}, u32[]{:S(2)}, u32[]{:S(2)}) async-start(bf16[8,4,16,128]{3,2,1,0:T(8,128)(2,1)} %diag.1), calls=%async_computation.1 | async-start | bytes 262144 | tf_op jit(solution)/shard_map/all_to_all | solution.py:215
